TPU v7x, 32 devices: a whole 2x2x4 slice. The times are simulated.
32 devices in a mesh: groups: 2 (over x), tile: 16 (over z, y, core).
Axes of the slice: x: 2, y: 2, z: 4, core: 2. Of those that a mesh axis runs over, the one named last changes fastest.
Arguments:
- source: bfloat16 [512, 2, 69, 128], P('tile', 'groups'), parts along dimension 1, may hold values from -42 to 42
- weights: bfloat16 [1536, 128, 128], P('tile'), may hold values from -0.5 to 0.5
- block_source: int32 [1536], P('tile'), may hold values from 0 to 31
- block_target: int32 [1536], P('tile'), may hold values from 0 to 511, as said below
- edge_flip: int32 [16, 2], P('tile'), may hold values 0 or 1
- norm_gain: float32 [69], replicated, may hold values from 0.1 to 1.9
- first_kernel: bfloat16 [9, 69, 69], replicated, may hold values from -0.25 to 0.25
- second_kernel: bfloat16 [9, 69, 69], replicated, may hold values from -0.25 to 0.25
Outputs:
- gridded: bfloat16 [512, 2, 69, 128], P('tile', 'groups'), parts along dimension 1
- smoothed: bfloat16 [512, 2, 69, 128], P('tile', 'groups'), parts along dimension 1
There are 2 independent parts, one for each index of `groups`. A program takes and returns all parts, laid end to end along the dimension named above; an argument that names none is the same for every part. Nothing has to cross between parts.
Inputs may be any that keep to these rules, and one draw needn't show every extreme that they name: `block_target`: band d lies at the latitude of tile position p = d mod 2, in column d // 2. Its entries name exactly 64 distinct target rows, all in tiles c * 2 + p or c * 2 + p + 1 (any column c, positions below 2). One band names at most 8 distinct rows of one tile, and every band at position 1 names exactly 8 rows of each tile at its own position.
All inputs are finite; a program needn't handle non-finite values. No bound on the sum of `edge_flip` on one device may be relied on, other than what follows from the above.
Results may differ from a plain program's by a relative error of at most 0.001.
The roundings to bfloat16 on the way count: a program that leaves them out, or rounds other values in their place, can miss the bound.
Values may be sent and summed in bfloat16 or wider, within the bound.
No kernel may reach another device: no remote copies, remote signals or barrier semaphores. Data moves between devices by JAX's collectives and lax.ppermute only.
A program may use at most 64 MiB of HBM per device.

v0:
```python
import functools

import jax
import jax.numpy as jnp
from jax import lax
from jax.experimental import pallas as pl
from jax.experimental.pallas import tpu as pltpu
from jax.sharding import PartitionSpec as P

BLOCK = 128
CHANNELS = 69
PADDED = 72
WIDE = 80
ROWS = 32
ROW_BITS = 5
TILE_COLS = 8
CAP = 8
GROUPS = 2 * TILE_COLS
SLOTS = GROUPS * CAP
CHUNK = 96
MARK = CHANNELS
EPSILON = 1e-05
VMEM_LIMIT = 40 * 1024 * 1024
REGRID_VMEM = 60 * 1024 * 1024


def vmem():
    return pl.BlockSpec(memory_space=pltpu.VMEM)


def smem():
    return pl.BlockSpec(memory_space=pltpu.SMEM)


def split(value, size):
    if size & (size - 1) == 0:
        return value >> (size.bit_length() - 1), value & (size - 1)
    return lax.div(value, size), lax.rem(value, size)


def lanes(shape):
    return lax.broadcasted_iota(jnp.int32, shape, len(shape) - 1)


def regrid_kernel(
    column_rows, target_hbm, target_row_hbm, index_hbm, source_hbm, weight_hbm, *rest
):
    same_out, next_outs = rest[0], rest[1 : 1 + TILE_COLS]
    (
        target_ref,
        target_row_ref,
        index_ref,
        source,
        weight,
        wide,
        field,
        sums,
        rounded,
        plan,
        plan_scalars,
        plan_sem,
        in_sems,
        weight_sems,
        out_sems,
    ) = rest[1 + TILE_COLS :]
    entries = weight.shape[0]
    chunks = entries // CHUNK
    tile = lax.axis_index("tile")
    column, position = split(tile, column_rows)

    small_copies = [
        pltpu.make_async_copy(target_row_hbm, target_row_ref, in_sems.at[0]),
        pltpu.make_async_copy(target_hbm, target_ref, in_sems.at[1]),
        pltpu.make_async_copy(index_hbm, index_ref, in_sems.at[2]),
    ]
    source_copy = pltpu.make_async_copy(source_hbm, source, in_sems.at[3])
    for copy in small_copies:
        copy.start()
    source_copy.start()

    def chunk_copy(chunk):
        part = pl.ds(chunk * CHUNK, CHUNK)
        return pltpu.make_async_copy(weight_hbm.at[part], weight.at[part], weight_sems.at[chunk])

    for chunk in range(chunks):
        chunk_copy(chunk).start()

    small_copies[0].wait()
    target = target_row_ref[...]
    owner, row = split(target, ROWS)
    owner_column, owner_position = split(owner, column_rows)
    group = jnp.where(
        owner_position == position, owner_column, TILE_COLS + (owner_column ^ column)
    )
    key = group * ROWS + row
    square = (entries, entries)
    down = lax.broadcasted_iota(jnp.int32, square, 0)
    along = lanes(square)
    key_along = jnp.broadcast_to(key.astype(jnp.float32), square)
    key_down = jnp.broadcast_to(
        jnp.sum(jnp.where(down == along, key_along, 0.0), axis=1, keepdims=True), square
    )
    equal = key_along == key_down
    doubles = jnp.sum(jnp.where(equal & (along < down), 1.0, 0.0), axis=1, keepdims=True)
    in_group = (key_down.astype(jnp.int32) >> ROW_BITS) == (key_along.astype(jnp.int32) >> ROW_BITS)
    below = in_group & (key_down < key_along) & (jnp.broadcast_to(doubles, square) == 0.0)
    rank = jnp.sum(jnp.where(below, 1.0, 0.0), axis=0, keepdims=True)
    mentions = jnp.sum(jnp.where(equal & (down < along), 1.0, 0.0), axis=0, keepdims=True)
    slots = group * CAP + rank.astype(jnp.int32)
    plan[...] = slots + jnp.where(mentions == 0.0, SLOTS, 0)
    plan_copy = pltpu.make_async_copy(plan, plan_scalars, plan_sem)
    plan_copy.start()

    tail = PADDED - 8
    for slot in range(SLOTS):
        rounded[slot, tail:] = jnp.full((8, BLOCK), ROWS, jnp.bfloat16)
    wide[pl.ds(CHANNELS * ROWS, (PADDED - CHANNELS) * ROWS), :] = jnp.zeros(
        ((PADDED - CHANNELS) * ROWS, BLOCK), jnp.float32
    )
    nothing = jnp.zeros((WIDE - PADDED, BLOCK), jnp.float32)
    source_copy.wait()
    wide[pl.ds(0, CHANNELS * ROWS), :] = source[...].astype(jnp.float32)
    for row in range(ROWS):
        block = wide[pl.ds(row, PADDED, stride=ROWS), :]
        field[row] = jnp.concatenate([block, nothing], axis=0).astype(jnp.bfloat16)
    is_mark = lax.broadcasted_iota(jnp.int32, (8, BLOCK), 0) == MARK - tail
    blank = jnp.zeros((WIDE, BLOCK), jnp.bfloat16)
    small_copies[1].wait()
    small_copies[2].wait()
    plan_copy.wait()

    for chunk in range(chunks):
        chunk_copy(chunk).wait()
        for entry in range(chunk * CHUNK, (chunk + 1) * CHUNK, 2):
            one = jnp.concatenate([field[index_ref[entry]], blank], axis=1)
            two = jnp.concatenate([blank, field[index_ref[entry + 1]]], axis=1)
            products = jnp.dot(
                jnp.concatenate([one, two], axis=0),
                weight[entry : entry + 2].reshape(2 * BLOCK, BLOCK),
                preferred_element_type=jnp.float32,
            )
            for at in range(2):
                code = plan_scalars[0, entry + at]
                slot = code & (SLOTS - 1)
                row = split(target_ref[entry + at], ROWS)[1]
                product = products[at * WIDE : at * WIDE + PADDED]
                total = jnp.where(code >= SLOTS, 0.0, sums[slot]) + product
                sums[slot] = total
                marked = jnp.where(is_mark, row.astype(jnp.float32), total[tail:])
                rounded[slot] = jnp.concatenate([total[:tail], marked], axis=0).astype(jnp.bfloat16)
    copies = []
    for group in range(GROUPS):
        part = rounded.at[pl.ds(group * CAP, CAP)]
        if group < TILE_COLS:
            out = same_out.at[pl.ds(group * CAP, CAP)]
        else:
            out = next_outs[group - TILE_COLS]
        copies.append(pltpu.make_async_copy(part, out, out_sems.at[group]))
    for copy in copies:
        copy.start()
    for copy in copies:
        copy.wait()


def regrid(target, source_index, field, weights, column_rows):
    piece = jax.ShapeDtypeStruct((CAP, PADDED, BLOCK), jnp.bfloat16)
    same = jax.ShapeDtypeStruct((TILE_COLS * CAP, PADDED, BLOCK), jnp.bfloat16)
    hbm = pl.BlockSpec(memory_space=pl.ANY)
    entries = weights.shape[0]
    return pl.pallas_call(
        functools.partial(regrid_kernel, column_rows),
        in_specs=[hbm] * 5,
        out_specs=[hbm] * (1 + TILE_COLS),
        out_shape=[same] + [piece] * TILE_COLS,
        scratch_shapes=[
            pltpu.SMEM(target.shape, jnp.int32),
            pltpu.VMEM((1, entries), jnp.int32),
            pltpu.SMEM(source_index.shape, jnp.int32),
            pltpu.VMEM(field.shape, jnp.bfloat16),
            pltpu.VMEM(weights.shape, jnp.bfloat16),
            pltpu.VMEM((PADDED * ROWS, BLOCK), jnp.float32),
            pltpu.VMEM((ROWS, WIDE, BLOCK), jnp.bfloat16),
            pltpu.VMEM((SLOTS, PADDED, BLOCK), jnp.float32),
            pltpu.VMEM((SLOTS, PADDED, BLOCK), jnp.bfloat16),
            pltpu.VMEM((1, entries), jnp.int32),
            pltpu.SMEM((1, entries), jnp.int32),
            pltpu.SemaphoreType.DMA,
            pltpu.SemaphoreType.DMA((4,)),
            pltpu.SemaphoreType.DMA((entries // CHUNK,)),
            pltpu.SemaphoreType.DMA((GROUPS,)),
        ],
        compiler_params=pltpu.CompilerParams(vmem_limit_bytes=REGRID_VMEM),
        name="regrid",
    )(target, target.reshape(1, -1), source_index, field, weights)


def gather_kernel(column_rows, flip_ref, gain_ref, same, *rest):
    nexts = rest[:TILE_COLS]
    (
        gridded,
        normed,
        upward,
        downward,
        strip_out,
        summed,
    ) = rest[TILE_COLS:]
    position = lax.rem(lax.axis_index("tile"), column_rows)
    summed[...] = jnp.zeros_like(summed)

    def add(piece):
        row = piece[MARK : MARK + 1].astype(jnp.float32).astype(jnp.int32)[0, 0]
        summed[row] = summed[row] + piece[...].astype(jnp.float32)

    for slot in range(SLOTS // 2):
        add(same.at[slot])

    @pl.when(position > 0)
    def _():
        for group in range(TILE_COLS):
            for place in range(CAP):
                add(nexts[group].at[place])

    gain = gain_ref[...]
    channel = lax.broadcasted_iota(jnp.int32, (PADDED, BLOCK), 0)
    nothing = jnp.zeros((WIDE - PADDED, BLOCK), jnp.float32)
    lane = lanes((WIDE, BLOCK))
    strip = jnp.zeros((WIDE, BLOCK), jnp.bfloat16)
    for row in range(ROWS):
        rounded = summed[row].astype(jnp.bfloat16)
        gridded[row] = rounded
        value = rounded.astype(jnp.float32)
        value = jnp.where(channel < CHANNELS, value, 0.0)
        square = jnp.sum(value * value, axis=0, keepdims=True) * (1.0 / CHANNELS)
        scaled = value * lax.rsqrt(square + EPSILON) * gain
        scaled = jnp.concatenate([scaled, nothing], axis=0).astype(jnp.bfloat16)
        normed[row] = scaled
        if row < 2:
            upward[row] = scaled
        if row >= ROWS - 2:
            downward[row - ROWS + 2] = scaled
        strip = jnp.where((lane >> 2) == row, pltpu.roll(scaled, 4 * row + 2, 1), strip)
    to_lane = lanes((BLOCK, BLOCK))
    from_lane = 4 * (to_lane & (ROWS - 1)) + (((to_lane >> ROW_BITS) + 2) & 3)
    order = lax.broadcasted_iota(jnp.int32, (BLOCK, BLOCK), 0) == from_lane
    strip = jnp.dot(strip, order.astype(jnp.bfloat16), preferred_element_type=jnp.float32)
    channel = lax.broadcasted_iota(jnp.int32, (WIDE, BLOCK), 0)
    for side in range(2):
        strip = jnp.where(channel == CHANNELS + side, flip_ref[0, side].astype(jnp.float32), strip)
    strip = strip.astype(jnp.bfloat16)
    upward[2] = strip
    downward[2] = strip
    strip_out[...] = strip


GRIDDED = jax.ShapeDtypeStruct((ROWS, PADDED, BLOCK), jnp.bfloat16)
FIELD = jax.ShapeDtypeStruct((ROWS, WIDE, BLOCK), jnp.bfloat16)
RIM = jax.ShapeDtypeStruct((3, WIDE, BLOCK), jnp.bfloat16)
STRIP_COLUMNS = (0, 1, BLOCK - 2, BLOCK - 1)
STRIP = jax.ShapeDtypeStruct((WIDE, BLOCK), jnp.bfloat16)


def gather_rows(column_rows, edge_flip, gain, same, nexts):
    return pl.pallas_call(
        functools.partial(gather_kernel, column_rows),
        in_specs=[smem()] + [vmem()] * (2 + TILE_COLS),
        out_specs=[vmem()] * 5,
        out_shape=[GRIDDED, FIELD, RIM, RIM, STRIP],
        scratch_shapes=[
            pltpu.VMEM((ROWS + 1, PADDED, BLOCK), jnp.float32),
        ],
        compiler_params=pltpu.CompilerParams(vmem_limit_bytes=VMEM_LIMIT),
        name="gather_rows",
    )(edge_flip, gain, same, *nexts)


def turn_kernel(field, out, turned):
    for row in range(ROWS):
        turned[pl.ds(row, PADDED, stride=ROWS), :] = field[row].astype(jnp.float32)
    out[...] = turned[pl.ds(0, CHANNELS * ROWS), :].astype(jnp.bfloat16)


def channels_first(field):
    return pl.pallas_call(
        turn_kernel,
        in_specs=[vmem()],
        out_specs=vmem(),
        out_shape=jax.ShapeDtypeStruct((CHANNELS * ROWS, BLOCK), jnp.bfloat16),
        scratch_shapes=[pltpu.VMEM((PADDED * ROWS, BLOCK), jnp.float32)],
        compiler_params=pltpu.CompilerParams(vmem_limit_bytes=VMEM_LIMIT),
        name="channels_first",
    )(field)


def shifted_columns(value, left_end, right_end):
    lane = lanes((WIDE, BLOCK))
    left = jnp.where(lane == 0, left_end, pltpu.roll(value, 1, 1))
    right = jnp.where(lane == BLOCK - 1, right_end, pltpu.roll(value, BLOCK - 1, 1))
    return jnp.concatenate([left, value, right], axis=0)


def tap_sums(taps, one, two):
    both = jnp.concatenate([one, two], axis=1)
    result = jnp.dot(taps, both, preferred_element_type=jnp.float32)
    return result[:, :BLOCK], result[:, BLOCK:]


def row_tap(sums, at):
    return sums[at * WIDE : (at + 1) * WIDE]


def activated(value):
    return jax.nn.gelu(value).astype(jnp.bfloat16)


def inner_kernel(taps_ref, field, hidden, ends, sides, partial):
    taps = taps_ref[...]
    blank = jnp.zeros((WIDE, BLOCK), jnp.bfloat16)
    for row in range(0, ROWS, 2):
        partial[row], partial[row + 1] = tap_sums(
            taps,
            shifted_columns(field[row], blank, blank),
            shifted_columns(field[row + 1], blank, blank),
        )
    lane = lanes((WIDE, BLOCK))
    west = jnp.zeros((WIDE, BLOCK), jnp.float32)
    east = jnp.zeros((WIDE, BLOCK), jnp.float32)
    for row in range(ROWS):
        value = partial[row, WIDE : 2 * WIDE]
        if row > 0:
            value = value + partial[row - 1, :WIDE]
        if row < ROWS - 1:
            value = value + partial[row + 1, 2 * WIDE :]
        if row == 0:
            ends[0] = value
        elif row == ROWS - 1:
            ends[1] = value
        else:
            hidden[row] = activated(value)
        west = jnp.where(lane == row, pltpu.roll(value, row, 1), west)
        east = jnp.where(lane == row, pltpu.roll(value, row + 1, 1), east)
    hidden[0] = blank
    hidden[ROWS - 1] = blank
    sides[0] = west
    sides[1] = east


def inner_convolution(taps, field):
    pair = jax.ShapeDtypeStruct((2, WIDE, BLOCK), jnp.float32)
    return pl.pallas_call(
        inner_kernel,
        in_specs=[vmem()] * 2,
        out_specs=[vmem()] * 3,
        out_shape=[FIELD, pair, pair],
        scratch_shapes=[pltpu.VMEM((ROWS, 3 * WIDE, BLOCK), jnp.float32)],
        compiler_params=pltpu.CompilerParams(vmem_limit_bytes=VMEM_LIMIT),
        cost_estimate=pl.CostEstimate(
            flops=2 * 9 * WIDE * WIDE * ROWS * BLOCK, bytes_accessed=2 << 20, transcendentals=0
        ),
        name="inner_convolution",
    )(taps, field)


def strip_plan(column_rows):
    if column_rows == 2:
        return [], 3, 1
    return [-2, 2], column_rows, 2


def conv_kernel(
    column_rows,
    first_taps_ref,
    second_taps_ref,
    field,
    gridded,
    inner,
    ends_ref,
    sides_ref,
    above,
    below,
    own_strip,
    *rest,
):
    near, far, reach = strip_plan(column_rows)
    near_strips, (west_pack, east_pack) = rest[: len(near)], rest[len(near) : len(near) + 2]
    smoothed, hidden, partial, turned = rest[len(near) + 2 :]
    count = lax.axis_size("tile")
    tile = lax.axis_index("tile")
    lane = lanes((WIDE, BLOCK))
    last = ROWS + 1
    R = column_rows
    blank = jnp.zeros((WIDE, BLOCK), jnp.bfloat16)

    strips = {-1: above[2], 0: own_strip[...], 1: below[2]}
    strips.update((shift, ref[...]) for shift, ref in zip(near, near_strips))
    for at in range(-reach, reach + 1):
        strips[at - far], strips[at + far] = west_pack[at + reach], east_pack[at + reach]

    def place(shift):
        return lax.rem(tile + shift + count, count)

    def ends(shift, before, after, middle):
        before = jnp.where(place(shift) > 0, before, blank)
        after = jnp.where(place(shift) < count - 1, after, blank)
        return jnp.where(lane == 0, before, jnp.where(lane == last, after, middle))

    memo = {}

    def padded_column(shift, which):
        if (shift, which) not in memo:
            base = which * ROWS
            memo[shift, which] = ends(
                shift,
                pltpu.roll(strips[shift - 1], (1 - base - ROWS) % BLOCK, 1),
                pltpu.roll(strips[shift + 1], (last - base) % BLOCK, 1),
                pltpu.roll(strips[shift], (1 - base) % BLOCK, 1),
            )
        return memo[shift, which]

    row_id = lax.broadcasted_iota(jnp.int32, (BLOCK, BLOCK), 0)
    reversal = (row_id + lanes((BLOCK, BLOCK)) == last).astype(jnp.bfloat16)

    def reversed_lanes(planes):
        stacked = jnp.concatenate(planes, axis=0)
        turned_round = jnp.dot(stacked, reversal, preferred_element_type=jnp.float32)
        return [row_tap(turned_round, at) for at in range(len(planes))]

    def choose(shift, which, turned_round, plain):
        flips = strips[shift].astype(jnp.float32)[CHANNELS + which : CHANNELS + which + 1]
        return jnp.where(flips > 0.5, turned_round, plain.astype(jnp.float32)).astype(jnp.bfloat16)

    west_of = {shift: (shift - R, 3) for shift in {-1, 0, 1, R - 1, R, R + 1}}
    east_of = {shift: (shift + R, 0) for shift in {-1, 0, 1, -R - 1, -R, -R + 1}}
    keys = sorted(set(west_of.values()) | set(east_of.values()))
    flipped = dict(zip(keys, reversed_lanes([padded_column(*key) for key in keys])))
    west = {
        shift: choose(shift, 0, flipped[west_of[shift]], padded_column(*west_of[shift]))
        for shift in sorted(west_of)
    }
    east = {
        shift: choose(shift, 1, flipped[east_of[shift]], padded_column(*east_of[shift]))
        for shift in sorted(east_of)
    }

    def columns(value, west_plane, west_row, east_plane, east_row):
        return shifted_columns(
            value,
            pltpu.roll(west_plane, (BLOCK - west_row) % BLOCK, 1),
            pltpu.roll(east_plane, BLOCK - 1 - east_row, 1),
        )

    def along(result):
        return (
            row_tap(result, 0)
            + pltpu.roll(row_tap(result, 1), BLOCK - 1, 1)
            + pltpu.roll(row_tap(result, 2), BLOCK - 2, 1)
        )

    first_taps = first_taps_ref[...]
    up = [jnp.where(tile > 0, above[at], blank) for at in range(2)]
    down = [jnp.where(tile < count - 1, below[at], blank) for at in range(2)]
    from_up, from_down = tap_sums(
        first_taps, shifted_columns(up[1], blank, blank), shifted_columns(down[0], blank, blank)
    )
    from_up, from_down = row_tap(from_up, 0), row_tap(from_down, 2)
    from_west, from_east = tap_sums(
        first_taps,
        jnp.concatenate([west[0], blank, blank], axis=0),
        jnp.concatenate([blank, blank, east[0]], axis=0),
    )
    from_west, from_east = along(from_west), along(from_east)
    first = ends_ref[0] + from_up
    first = first + jnp.where(lane == 0, from_west, 0.0)
    first = first + jnp.where(lane == BLOCK - 1, pltpu.roll(from_east, BLOCK - 1, 1), 0.0)
    final = ends_ref[1] + from_down
    final = final + jnp.where(lane == 0, pltpu.roll(from_west, BLOCK - ROWS + 1, 1), 0.0)
    final = final + jnp.where(lane == BLOCK - 1, pltpu.roll(from_east, BLOCK - ROWS, 1), 0.0)
    hidden[1] = activated(first)
    hidden[ROWS] = activated(final)
    first_column = activated(sides_ref[0] + from_west)
    last_column = activated(sides_ref[1] + from_east)
    for row in range(1, ROWS - 1):
        value = jnp.where(lane == 0, pltpu.roll(first_column, BLOCK - row, 1), inner[row])
        hidden[row + 1] = jnp.where(
            lane == BLOCK - 1, pltpu.roll(last_column, BLOCK - 1 - row, 1), value
        )

    upper = jnp.zeros((WIDE, BLOCK), jnp.float32)
    lower = jnp.zeros((WIDE, BLOCK), jnp.float32)
    for at, (high, low) in enumerate(
        [(up[0], field[ROWS - 1]), (up[1], down[0]), (field[0], down[1])]
    ):
        from_row = ROWS - 1 + at
        one, two = tap_sums(
            first_taps,
            columns(high, west[-1], from_row, east[-1], from_row),
            columns(low, west[1], at, east[1], at),
        )
        upper += row_tap(one, at)
        lower += row_tap(two, at)
    hidden[0] = jnp.where(tile > 0, activated(upper), blank)
    hidden[last] = jnp.where(tile < count - 1, activated(lower), blank)

    west_hidden, east_hidden = {}, {}
    for at in (-1, 0, 1):
        q = at - R
        one = jnp.concatenate([padded_column(q, 2), padded_column(q, 3), east[q]], axis=0)
        q = at + R
        two = jnp.concatenate([west[q], padded_column(q, 0), padded_column(q, 1)], axis=0)
        one, two = tap_sums(first_taps, one, two)
        west_hidden[at], east_hidden[at] = activated(along(one)), activated(along(two))

    def hidden_side(shift, values):
        return ends(
            shift,
            pltpu.roll(values[-1], BLOCK - ROWS + 1, 1),
            pltpu.roll(values[1], last, 1),
            pltpu.roll(values[0], 1, 1),
        )

    plain = [hidden_side(-R, west_hidden), hidden_side(R, east_hidden)]
    west_side, east_side = [
        choose(0, which, turned_side, plain[which])
        for which, turned_side in enumerate(reversed_lanes(plain))
    ]

    second_taps = second_taps_ref[...]
    for p in range(0, ROWS + 2, 2):
        partial[p], partial[p + 1] = tap_sums(
            second_taps,
            columns(hidden[p], west_side, p, east_side, p),
            columns(hidden[p + 1], west_side, p + 1, east_side, p + 1),
        )
    for row in range(ROWS):
        branch = (
            partial[row, :PADDED]
            + partial[row + 1, WIDE : WIDE + PADDED]
            + partial[row + 2, 2 * WIDE : 2 * WIDE + PADDED]
        )
        turned[pl.ds(row, PADDED, stride=ROWS), :] = gridded[row].astype(jnp.float32) + branch
    smoothed[...] = turned[pl.ds(0, CHANNELS * ROWS), :].astype(jnp.bfloat16)


def convolutions(column_rows, *operands):
    return pl.pallas_call(
        functools.partial(conv_kernel, column_rows),
        in_specs=[vmem()] * len(operands),
        out_specs=vmem(),
        out_shape=jax.ShapeDtypeStruct((CHANNELS * ROWS, BLOCK), jnp.bfloat16),
        scratch_shapes=[
            pltpu.VMEM((ROWS + 2, WIDE, BLOCK), jnp.bfloat16),
            pltpu.VMEM((ROWS + 2, 3 * WIDE, BLOCK), jnp.float32),
            pltpu.VMEM((PADDED * ROWS, BLOCK), jnp.float32),
        ],
        compiler_params=pltpu.CompilerParams(vmem_limit_bytes=VMEM_LIMIT),
        name="convolutions",
    )(*operands)


def tap_matrix(kernel):
    pad = WIDE - CHANNELS
    taps = jnp.pad(kernel, ((0, 0), (0, pad), (0, pad))).reshape(3, 3, WIDE, WIDE)
    return taps.transpose(0, 2, 1, 3).reshape(3 * WIDE, 3 * WIDE)


def from_shift(value, shift):
    count = lax.axis_size("tile")
    return lax.ppermute(value, "tile", [(i, (i - shift) % count) for i in range(count)])


def per_device(
    source, weights, block_source, block_target, edge_flip, norm_gain, first_kernel, second_kernel
):
    count = lax.axis_size("tile")
    column_rows = count // TILE_COLS
    field = source.reshape(ROWS, CHANNELS, BLOCK).transpose(1, 0, 2).reshape(-1, BLOCK)
    same, *nexts = regrid(block_target, block_source, field, weights, column_rows)

    for across in range(TILE_COLS):
        pairs = [
            (c * column_rows + p, (c ^ across) * column_rows + p + 1)
            for c in range(TILE_COLS)
            for p in range(column_rows - 1)
        ]
        nexts[across] = lax.ppermute(nexts[across], "tile", pairs)
    same = lax.all_to_all(
        same,
        "tile",
        0,
        0,
        axis_index_groups=[
            [c * column_rows + p for c in range(TILE_COLS)] for p in range(column_rows)
        ],
        tiled=True,
    )

    gain = jnp.broadcast_to(
        jnp.pad(norm_gain, (0, PADDED - CHANNELS))[:, None], (PADDED, BLOCK)
    )
    first_taps, second_taps = tap_matrix(first_kernel), tap_matrix(second_kernel)
    same, nexts, gain, first_taps, second_taps = lax.optimization_barrier(
        (same, nexts, gain, first_taps, second_taps)
    )
    gridded, normed, upward, downward, strip = gather_rows(
        column_rows, edge_flip, gain, same, nexts
    )
    rims = [from_shift(downward, -1), from_shift(upward, 1)]
    near, far, reach = strip_plan(column_rows)
    strips = [from_shift(strip, shift) for shift in near]
    inner = inner_convolution(first_taps, normed)
    held = {-1: rims[0][2], 0: strip, 1: rims[1][2], **dict(zip(near, strips))}
    pack = jnp.stack([held[at] for at in range(-reach, reach + 1)])
    pack, inner = lax.optimization_barrier((pack, inner))
    strips += [from_shift(pack, -far), from_shift(pack, far)]
    gridded_out = channels_first(gridded)
    smoothed = convolutions(
        column_rows, first_taps, second_taps, normed, gridded, *inner, *rims, strip, *strips
    )

    def placed(value):
        return value.reshape(CHANNELS, ROWS, BLOCK).transpose(1, 0, 2)[:, None]

    return placed(gridded_out), placed(smoothed)


def solution(mesh):
    in_specs = (
        P("tile", "groups", None, None),
        P("tile", None, None),
        P("tile"),
        P("tile"),
        P("tile", None),
        P(),
        P(),
        P(),
    )
    out_specs = (P("tile", "groups", None, None), P("tile", "groups", None, None))
    return jax.shard_map(
        per_device, mesh=mesh, in_specs=in_specs, out_specs=out_specs, check_vma=False
    )
```

profile of v0, /device:TPU:1, one launch (start us, length us, event | category | flops | bytes accessed | tf_op | source)
XLA Modules:
  0.0 69.5 jit_solution(8416750415413854173)
XLA Ops:
  0.6 4.9 %regrid.1 = (bf16[64,72,128]{2,1,0:T(8,128)(2,1)}, bf16[8,72,128]{2,1,0:T(8,128)(2,1)}, bf16[8,72,128]{2,1,0:T(8,128)(2,1)}, bf16[8,72,128]{2,1,0:T(8,128)(2,1)}...) custom-call(s32[96]{0:T(128)} %target_hbm.1, ...), custom_call_target="tpu_custom_call" | custom-call | tf_op jit(solution)/shard_map/regrid/pallas_call | solution.py:170
  5.5 0.0 copy-start.8
  5.6 0.0 copy-start.7
  5.6 0.0 copy-start.6
  5.6 0.0 copy-start.5
  5.6 0.0 copy-start.4
  5.6 0.0 copy-start.3
  5.6 0.0 copy-start.1
  5.6 0.0 copy-start.2
  5.6 6.5 %all-to-all-start = ((bf16[64,72,128]{2,1,0:T(8,128)(2,1)}), bf16[64,72,128]{2,1,0:T(8,128)(2,1)S(1)}, u32[]{:S(2)}, u32[]{:S(2)}) async-start(bf16[64,72,128]{2,1,0:T(8,128)(2,1)} %get-tuple-element.35), calls=%async_computation | async-start | bytes 2359296 | tf_op jit(solution)/shard_map/all_to_all | solution.py:585
  12.2 0.0 copy-start
  12.2 1.3 %collective-permute-start = (bf16[8,72,128]{2,1,0:T(8,128)(2,1)S(1)}, bf16[8,72,128]{2,1,0:T(8,128)(2,1)S(1)}, u32[]{:S(2)}, u32[]{:S(2)}) collective-permute-start(bf16[8,72,128]{2,1,0:T(8,128)(2,1)S(1)} %copy-done.8), channel_id=1, source_target_pairs={{0,1},{2,3},{4,5},{6,7},{8,9},{10,11},{12,13},{14,15},{16,17},{18,... | collective-permute-start | bytes 442376 | tf_op jit(solution)/shard_map/ppermute | solution.py:584
  13.5 0.0 copy-done.7
  13.5 1.3 %collective-permute-start.1 = (bf16[8,72,128]{2,1,0:T(8,128)(2,1)S(1)}, bf16[8,72,128]{2,1,0:T(8,128)(2,1)S(1)}, u32[]{:S(2)}, u32[]{:S(2)}) collective-permute-start(bf16[8,72,128]{2,1,0:T(8,128)(2,1)S(1)} %copy-done.7), channel_id=1, source_target_pairs={{0,3},{2,1},{4,7},{6,5},{8,11},{10,9},{12,15},{14,13},{16,19},{18,... | collective-permute-start | bytes 442376 | tf_op jit(solution)/shard_map/ppermute | solution.py:584
  14.8 0.0 copy-done.6
  14.8 1.3 %collective-permute-start.2 = (bf16[8,72,128]{2,1,0:T(8,128)(2,1)S(1)}, bf16[8,72,128]{2,1,0:T(8,128)(2,1)S(1)}, u32[]{:S(2)}, u32[]{:S(2)}) collective-permute-start(bf16[8,72,128]{2,1,0:T(8,128)(2,1)S(1)} %copy-done.6), channel_id=1, source_target_pairs={{0,5},{2,7},{4,1},{6,3},{8,13},{10,15},{12,9},{14,11},{16,21},{18,... | collective-permute-start | bytes 442376 | tf_op jit(solution)/shard_map/ppermute | solution.py:584
  16.1 1.3 %collective-permute-start.3 = (bf16[8,72,128]{2,1,0:T(8,128)(2,1)}, bf16[8,72,128]{2,1,0:T(8,128)(2,1)S(1)}, u32[]{:S(2)}, u32[]{:S(2)}) collective-permute-start(bf16[8,72,128]{2,1,0:T(8,128)(2,1)} %get-tuple-element.39), channel_id=1, source_target_pairs={{0,7},{2,5},{4,3},{6,1},{8,15},{10,13},{12,11},{14,9},{16,23},{18,... | collective-permute-start | bytes 442376 | tf_op jit(solution)/shard_map/ppermute | solution.py:584
  17.4 1.3 %collective-permute-start.4 = (bf16[8,72,128]{2,1,0:T(8,128)(2,1)}, bf16[8,72,128]{2,1,0:T(8,128)(2,1)S(1)}, u32[]{:S(2)}, u32[]{:S(2)}) collective-permute-start(bf16[8,72,128]{2,1,0:T(8,128)(2,1)} %get-tuple-element.40), channel_id=1, source_target_pairs={{0,9},{2,11},{4,13},{6,15},{8,1},{10,3},{12,5},{14,7},{16,25},{18,... | collective-permute-start | bytes 442376 | tf_op jit(solution)/shard_map/ppermute | solution.py:584
  18.7 0.0 collective-permute-done.rest_0_
  18.7 1.3 %collective-permute-start.5 = (bf16[8,72,128]{2,1,0:T(8,128)(2,1)S(1)}, bf16[8,72,128]{2,1,0:T(8,128)(2,1)S(1)}, u32[]{:S(2)}, u32[]{:S(2)}) collective-permute-start(bf16[8,72,128]{2,1,0:T(8,128)(2,1)S(1)} %copy-done.5), channel_id=1, source_target_pairs={{0,11},{2,9},{4,15},{6,13},{8,3},{10,1},{12,7},{14,5},{16,27},{18,... | collective-permute-start | bytes 442376 | tf_op jit(solution)/shard_map/ppermute | solution.py:584
  20.0 4.0 %collective-permute-done.1.rest_1_ = bf16[8,72,128]{2,1,0:T(8,128)(2,1)S(1)} collective-permute-done((bf16[8,72,128]{2,1,0:T(8,128)(2,1)S(1)}, bf16[8,72,128]{2,1,0:T(8,128)(2,1)S(1)}, u32[]{:S(2)}, u32[]{:S(2)}) %collective-permute-start.1) | collective-permute-done | bytes 147488 | tf_op jit(solution)/shard_map/ppermute | solution.py:584
  24.1 0.0 copy-done.4
  24.1 1.3 %collective-permute-start.6 = (bf16[8,72,128]{2,1,0:T(8,128)(2,1)S(1)}, bf16[8,72,128]{2,1,0:T(8,128)(2,1)S(1)}, u32[]{:S(2)}, u32[]{:S(2)}) collective-permute-start(bf16[8,72,128]{2,1,0:T(8,128)(2,1)S(1)} %copy-done.4), channel_id=1, source_target_pairs={{0,13},{2,15},{4,9},{6,11},{8,5},{10,7},{12,1},{14,3},{16,29},{18,... | collective-permute-start | bytes 442376 | tf_op jit(solution)/shard_map/ppermute | solution.py:584
  25.4 4.7 %collective-permute-done.2.rest_2_ = bf16[8,72,128]{2,1,0:T(8,128)(2,1)S(1)} collective-permute-done((bf16[8,72,128]{2,1,0:T(8,128)(2,1)S(1)}, bf16[8,72,128]{2,1,0:T(8,128)(2,1)S(1)}, u32[]{:S(2)}, u32[]{:S(2)}) %collective-permute-start.2) | collective-permute-done | bytes 147488 | tf_op jit(solution)/shard_map/ppermute | solution.py:584
  30.0 1.3 %collective-permute-start.7 = (bf16[8,72,128]{2,1,0:T(8,128)(2,1)S(1)}, bf16[8,72,128]{2,1,0:T(8,128)(2,1)S(1)}, u32[]{:S(2)}, u32[]{:S(2)}) collective-permute-start(bf16[8,72,128]{2,1,0:T(8,128)(2,1)S(1)} %copy-done.3), channel_id=1, source_target_pairs={{0,15},{2,13},{4,11},{6,9},{8,7},{10,5},{12,3},{14,1},{16,31},{18,... | collective-permute-start | bytes 442376 | tf_op jit(solution)/shard_map/ppermute | solution.py:584
  31.4 0.1 copy.17
  31.5 0.2 reshape.36.taps_ref.first_taps_ref
  31.7 0.1 copy.16
  31.8 0.2 reshape.38.second_taps_ref
  32.0 2.8 %collective-permute-done.3.rest_3_ = bf16[8,72,128]{2,1,0:T(8,128)(2,1)S(1)} collective-permute-done((bf16[8,72,128]{2,1,0:T(8,128)(2,1)}, bf16[8,72,128]{2,1,0:T(8,128)(2,1)S(1)}, u32[]{:S(2)}, u32[]{:S(2)}) %collective-permute-start.3) | collective-permute-done | bytes 147488 | tf_op jit(solution)/shard_map/ppermute | solution.py:584
  34.8 14.1 %collective-permute-done.4.rest_4_ = bf16[8,72,128]{2,1,0:T(8,128)(2,1)S(1)} collective-permute-done((bf16[8,72,128]{2,1,0:T(8,128)(2,1)}, bf16[8,72,128]{2,1,0:T(8,128)(2,1)S(1)}, u32[]{:S(2)}, u32[]{:S(2)}) %collective-permute-start.4) | collective-permute-done | bytes 147488 | tf_op jit(solution)/shard_map/ppermute | solution.py:584
  48.9 2.5 %collective-permute-done.5.rest_5_ = bf16[8,72,128]{2,1,0:T(8,128)(2,1)S(1)} collective-permute-done((bf16[8,72,128]{2,1,0:T(8,128)(2,1)S(1)}, bf16[8,72,128]{2,1,0:T(8,128)(2,1)S(1)}, u32[]{:S(2)}, u32[]{:S(2)}) %collective-permute-start.5) | collective-permute-done | bytes 147488 | tf_op jit(solution)/shard_map/ppermute | solution.py:584
  51.4 0.0 collective-permute-done.6.rest_6_
  51.4 0.0 collective-permute-done.7.rest_7_
  51.4 0.0 all-to-all-done.same
  51.4 0.1 broadcast_in_dim.12.gain_ref
  51.5 2.1 %gather_rows.1 = (bf16[32,72,128]{2,1,0:T(8,128)(2,1)S(1)}, bf16[32,80,128]{2,1,0:T(8,128)(2,1)S(1)}, bf16[3,80,128]{2,1,0:T(8,128)(2,1)S(1)}, bf16[3,80,128]{2,1,0:T(8,128)(2,1)S(1)}, bf16[80,128]{1,0:T(8,128)(2,1)S(1)}) custom-call(s32[1,2]{1,0:T(1,128)S(1)} %copy-done, f32[72,128]{1,0:T(8,128)S(1)} %broadcast_in_dim.12.gain_ref, ...), custom_call_target="tpu_custom_call" | custom-call | tf_op jit(solution)/shard_map/gather_rows/pallas_call | solution.py:263
  53.6 0.1 collective-permute-start.8
  53.7 0.5 collective-permute-start.9
  54.2 1.2 %inner_convolution.1 = (bf16[32,80,128]{2,1,0:T(8,128)(2,1)S(1)}, f32[2,80,128]{2,1,0:T(8,128)S(1)}, f32[2,80,128]{2,1,0:T(8,128)S(1)}) custom-call(bf16[240,240]{1,0:T(8,128)(2,1)S(1)} %reshape.36.taps_ref.first_taps_ref, bf16[32,80,128]{2,1,0:T(8,128)(2,1)S(1)} %get-tuple-element.57.field), custom_call_target="tpu_custom_call" | custom-call | flops 471859200 | bytes 2097152 | tf_op jit(solution)/shard_map/inner_convolution/pallas_call | solution.py:349
  55.4 0.0 collective-permute-done.8.above
  55.4 2.0 %collective-permute-done.9.below = bf16[3,80,128]{2,1,0:T(8,128)(2,1)S(1)} collective-permute-done((bf16[3,80,128]{2,1,0:T(8,128)(2,1)S(1)}, bf16[3,80,128]{2,1,0:T(8,128)(2,1)S(1)}, u32[]{:S(2)}, u32[]{:S(2)}) %collective-permute-start.9) | collective-permute-done | bytes 61472 | tf_op jit(solution)/shard_map/ppermute | solution.py:567
  57.4 0.9 %collective-permute-start.11 = (bf16[3,80,128]{2,1,0:T(8,128)(2,1)S(1)}, bf16[3,80,128]{2,1,0:T(8,128)(2,1)S(1)}, u32[]{:S(2)}, u32[]{:S(2)}) collective-permute-start(bf16[3,80,128]{2,1,0:T(8,128)(2,1)S(1)} %pad_maximum_fusion), channel_id=1, source_target_pairs={{0,13},{1,14},{2,15},{3,0},{4,1},{5,2},{6,3},{7,4},{8,5},{9,6},{10... | collective-permute-start | bytes 184328 | tf_op jit(solution)/shard_map/ppermute | solution.py:567
  58.3 1.2 %collective-permute-start.10 = (bf16[3,80,128]{2,1,0:T(8,128)(2,1)S(1)}, bf16[3,80,128]{2,1,0:T(8,128)(2,1)S(1)}, u32[]{:S(2)}, u32[]{:S(2)}) collective-permute-start(bf16[3,80,128]{2,1,0:T(8,128)(2,1)S(1)} %pad_maximum_fusion), channel_id=1, source_target_pairs={{0,3},{1,4},{2,5},{3,6},{4,7},{5,8},{6,9},{7,10},{8,11},{9,12},{10... | collective-permute-start | bytes 184328 | tf_op jit(solution)/shard_map/ppermute | solution.py:567
  59.5 2.0 %channels_first.1 = bf16[2208,128]{1,0:T(8,128)(2,1)} custom-call(bf16[32,72,128]{2,1,0:T(8,128)(2,1)S(1)} %get-tuple-element.54.field.gridded), custom_call_target="tpu_custom_call" | custom-call | tf_op jit(solution)/shard_map/channels_first/pallas_call | solution.py:283
  61.5 0.0 collective-permute-done.11.rest_1_
  61.5 4.3 %collective-permute-done.10.rest_0_ = bf16[3,80,128]{2,1,0:T(8,128)(2,1)S(1)} collective-permute-done((bf16[3,80,128]{2,1,0:T(8,128)(2,1)S(1)}, bf16[3,80,128]{2,1,0:T(8,128)(2,1)S(1)}, u32[]{:S(2)}, u32[]{:S(2)}) %collective-permute-start.10) | collective-permute-done | bytes 61472 | tf_op jit(solution)/shard_map/ppermute | solution.py:567
  65.8 3.7 %convolutions.1 = bf16[2208,128]{1,0:T(8,128)(2,1)} custom-call(bf16[240,240]{1,0:T(8,128)(2,1)S(1)} %reshape.36.taps_ref.first_taps_ref, bf16[240,240]{1,0:T(8,128)(2,1)S(1)} %reshape.38.second_taps_ref, bf16[32,80,128]{2,1,0:T(8,128)(2,1)S(1)} %get-tuple-element.57.field, bf16[32,72,128]{2,1,0:T(8,128)(2,1)S(1)} %get-tuple-element.54.field.gridded, ...), custom_call_target="tpu_custom_call" | custom-call | tf_op jit(solution)/shard_map/convolutions/pallas_call | solution.py:544
  (14 shorter events, 0.1 us)
Async XLA Ops:
  5.5 6.6 %copy-start.8 = (bf16[8,72,128]{2,1,0:T(8,128)(2,1)S(1)}, bf16[8,72,128]{2,1,0:T(8,128)(2,1)}, u32[]{:S(2)}) copy-start(bf16[8,72,128]{2,1,0:T(8,128)(2,1)} %get-tuple-element.36) | copy-start | bytes 442372
  5.6 7.9 %copy-start.7 = (bf16[8,72,128]{2,1,0:T(8,128)(2,1)S(1)}, bf16[8,72,128]{2,1,0:T(8,128)(2,1)}, u32[]{:S(2)}) copy-start(bf16[8,72,128]{2,1,0:T(8,128)(2,1)} %get-tuple-element.37) | copy-start | bytes 442372
  5.6 9.2 %copy-start.6 = (bf16[8,72,128]{2,1,0:T(8,128)(2,1)S(1)}, bf16[8,72,128]{2,1,0:T(8,128)(2,1)}, u32[]{:S(2)}) copy-start(bf16[8,72,128]{2,1,0:T(8,128)(2,1)} %get-tuple-element.38) | copy-start | bytes 442372
  5.6 13.1 %copy-start.5 = (bf16[8,72,128]{2,1,0:T(8,128)(2,1)S(1)}, bf16[8,72,128]{2,1,0:T(8,128)(2,1)}, u32[]{:S(2)}) copy-start(bf16[8,72,128]{2,1,0:T(8,128)(2,1)} %get-tuple-element.41) | copy-start | bytes 442372
  5.6 18.5 %copy-start.4 = (bf16[8,72,128]{2,1,0:T(8,128)(2,1)S(1)}, bf16[8,72,128]{2,1,0:T(8,128)(2,1)}, u32[]{:S(2)}) copy-start(bf16[8,72,128]{2,1,0:T(8,128)(2,1)} %get-tuple-element.42) | copy-start | bytes 442372
  5.6 24.4 %copy-start.3 = (bf16[8,72,128]{2,1,0:T(8,128)(2,1)S(1)}, bf16[8,72,128]{2,1,0:T(8,128)(2,1)}, u32[]{:S(2)}) copy-start(bf16[8,72,128]{2,1,0:T(8,128)(2,1)} %get-tuple-element.43) | copy-start | bytes 442372
  5.6 25.7 %copy-start.1 = (bf16[9,69,69]{2,1,0:T(8,128)(2,1)S(1)}, bf16[9,69,69]{2,1,0:T(8,128)(2,1)}, u32[]{:S(2)}) copy-start(bf16[9,69,69]{2,1,0:T(8,128)(2,1)} %param.14) | copy-start | bytes 257098
  5.6 26.0 %copy-start.2 = (bf16[9,69,69]{2,1,0:T(8,128)(2,1)S(1)}, bf16[9,69,69]{2,1,0:T(8,128)(2,1)}, u32[]{:S(2)}) copy-start(bf16[9,69,69]{2,1,0:T(8,128)(2,1)} %param.15) | copy-start | bytes 257098
  5.6 45.8 %all-to-all-start = ((bf16[64,72,128]{2,1,0:T(8,128)(2,1)}), bf16[64,72,128]{2,1,0:T(8,128)(2,1)S(1)}, u32[]{:S(2)}, u32[]{:S(2)}) async-start(bf16[64,72,128]{2,1,0:T(8,128)(2,1)} %get-tuple-element.35), calls=%async_computation | async-start | bytes 2359296 | tf_op jit(solution)/shard_map/all_to_all | solution.py:585
  12.2 19.8 %copy-start.9 = (f32[69]{0:T(128)S(1)}, f32[69]{0:T(128)}, u32[]{:S(2)}) copy-start(f32[69]{0:T(128)} %param.13) | copy-start | bytes 832
  12.2 39.3 %copy-start = (s32[1,2]{1,0:T(1,128)S(1)}, s32[1,2]{1,0:T(1,128)}, u32[]{:S(2)}) copy-start(s32[1,2]{1,0:T(1,128)} %flip_ref.1) | copy-start | bytes 28
  12.2 6.5 %collective-permute-start = (bf16[8,72,128]{2,1,0:T(8,128)(2,1)S(1)}, bf16[8,72,128]{2,1,0:T(8,128)(2,1)S(1)}, u32[]{:S(2)}, u32[]{:S(2)}) collective-permute-start(bf16[8,72,128]{2,1,0:T(8,128)(2,1)S(1)} %copy-done.8), channel_id=1, source_target_pairs={{0,1},{2,3},{4,5},{6,7},{8,9},{10,11},{12,13},{14,15},{16,17},{18,... | collective-permute-start | bytes 442376 | tf_op jit(solution)/shard_map/ppermute | solution.py:584
  13.5 10.6 %collective-permute-start.1 = (bf16[8,72,128]{2,1,0:T(8,128)(2,1)S(1)}, bf16[8,72,128]{2,1,0:T(8,128)(2,1)S(1)}, u32[]{:S(2)}, u32[]{:S(2)}) collective-permute-start(bf16[8,72,128]{2,1,0:T(8,128)(2,1)S(1)} %copy-done.7), channel_id=1, source_target_pairs={{0,3},{2,1},{4,7},{6,5},{8,11},{10,9},{12,15},{14,13},{16,19},{18,... | collective-permute-start | bytes 442376 | tf_op jit(solution)/shard_map/ppermute | solution.py:584
  14.8 15.2 %collective-permute-start.2 = (bf16[8,72,128]{2,1,0:T(8,128)(2,1)S(1)}, bf16[8,72,128]{2,1,0:T(8,128)(2,1)S(1)}, u32[]{:S(2)}, u32[]{:S(2)}) collective-permute-start(bf16[8,72,128]{2,1,0:T(8,128)(2,1)S(1)} %copy-done.6), channel_id=1, source_target_pairs={{0,5},{2,7},{4,1},{6,3},{8,13},{10,15},{12,9},{14,11},{16,21},{18,... | collective-permute-start | bytes 442376 | tf_op jit(solution)/shard_map/ppermute | solution.py:584
  16.1 18.7 %collective-permute-start.3 = (bf16[8,72,128]{2,1,0:T(8,128)(2,1)}, bf16[8,72,128]{2,1,0:T(8,128)(2,1)S(1)}, u32[]{:S(2)}, u32[]{:S(2)}) collective-permute-start(bf16[8,72,128]{2,1,0:T(8,128)(2,1)} %get-tuple-element.39), channel_id=1, source_target_pairs={{0,7},{2,5},{4,3},{6,1},{8,15},{10,13},{12,11},{14,9},{16,23},{18,... | collective-permute-start | bytes 442376 | tf_op jit(solution)/shard_map/ppermute | solution.py:584
  17.4 31.5 %collective-permute-start.4 = (bf16[8,72,128]{2,1,0:T(8,128)(2,1)}, bf16[8,72,128]{2,1,0:T(8,128)(2,1)S(1)}, u32[]{:S(2)}, u32[]{:S(2)}) collective-permute-start(bf16[8,72,128]{2,1,0:T(8,128)(2,1)} %get-tuple-element.40), channel_id=1, source_target_pairs={{0,9},{2,11},{4,13},{6,15},{8,1},{10,3},{12,5},{14,7},{16,25},{18,... | collective-permute-start | bytes 442376 | tf_op jit(solution)/shard_map/ppermute | solution.py:584
  18.7 32.7 %collective-permute-start.5 = (bf16[8,72,128]{2,1,0:T(8,128)(2,1)S(1)}, bf16[8,72,128]{2,1,0:T(8,128)(2,1)S(1)}, u32[]{:S(2)}, u32[]{:S(2)}) collective-permute-start(bf16[8,72,128]{2,1,0:T(8,128)(2,1)S(1)} %copy-done.5), channel_id=1, source_target_pairs={{0,11},{2,9},{4,15},{6,13},{8,3},{10,1},{12,7},{14,5},{16,27},{18,... | collective-permute-start | bytes 442376 | tf_op jit(solution)/shard_map/ppermute | solution.py:584
  24.1 27.4 %collective-permute-start.6 = (bf16[8,72,128]{2,1,0:T(8,128)(2,1)S(1)}, bf16[8,72,128]{2,1,0:T(8,128)(2,1)S(1)}, u32[]{:S(2)}, u32[]{:S(2)}) collective-permute-start(bf16[8,72,128]{2,1,0:T(8,128)(2,1)S(1)} %copy-done.4), channel_id=1, source_target_pairs={{0,13},{2,15},{4,9},{6,11},{8,5},{10,7},{12,1},{14,3},{16,29},{18,... | collective-permute-start | bytes 442376 | tf_op jit(solution)/shard_map/ppermute | solution.py:584
  30.0 21.4 %collective-permute-start.7 = (bf16[8,72,128]{2,1,0:T(8,128)(2,1)S(1)}, bf16[8,72,128]{2,1,0:T(8,128)(2,1)S(1)}, u32[]{:S(2)}, u32[]{:S(2)}) collective-permute-start(bf16[8,72,128]{2,1,0:T(8,128)(2,1)S(1)} %copy-done.3), channel_id=1, source_target_pairs={{0,15},{2,13},{4,11},{6,9},{8,7},{10,5},{12,3},{14,1},{16,31},{18,... | collective-permute-start | bytes 442376 | tf_op jit(solution)/shard_map/ppermute | solution.py:584
  53.6 1.7 %collective-permute-start.8 = (bf16[3,80,128]{2,1,0:T(8,128)(2,1)S(1)}, bf16[3,80,128]{2,1,0:T(8,128)(2,1)S(1)}, u32[]{:S(2)}, u32[]{:S(2)}) collective-permute-start(bf16[3,80,128]{2,1,0:T(8,128)(2,1)S(1)} %get-tuple-element.58), channel_id=1, source_target_pairs={{0,1},{1,2},{2,3},{3,4},{4,5},{5,6},{6,7},{7,8},{8,9},{9,10},{10,1... | collective-permute-start | bytes 184328 | tf_op jit(solution)/shard_map/ppermute | solution.py:567
  53.7 3.7 %collective-permute-start.9 = (bf16[3,80,128]{2,1,0:T(8,128)(2,1)S(1)}, bf16[3,80,128]{2,1,0:T(8,128)(2,1)S(1)}, u32[]{:S(2)}, u32[]{:S(2)}) collective-permute-start(bf16[3,80,128]{2,1,0:T(8,128)(2,1)S(1)} %get-tuple-element.60), channel_id=1, source_target_pairs={{0,15},{1,0},{2,1},{3,2},{4,3},{5,4},{6,5},{7,6},{8,7},{9,8},{10,9... | collective-permute-start | bytes 184328 | tf_op jit(solution)/shard_map/ppermute | solution.py:567
  57.4 4.1 %collective-permute-start.11 = (bf16[3,80,128]{2,1,0:T(8,128)(2,1)S(1)}, bf16[3,80,128]{2,1,0:T(8,128)(2,1)S(1)}, u32[]{:S(2)}, u32[]{:S(2)}) collective-permute-start(bf16[3,80,128]{2,1,0:T(8,128)(2,1)S(1)} %pad_maximum_fusion), channel_id=1, source_target_pairs={{0,13},{1,14},{2,15},{3,0},{4,1},{5,2},{6,3},{7,4},{8,5},{9,6},{10... | collective-permute-start | bytes 184328 | tf_op jit(solution)/shard_map/ppermute | solution.py:567
  58.3 7.5 %collective-permute-start.10 = (bf16[3,80,128]{2,1,0:T(8,128)(2,1)S(1)}, bf16[3,80,128]{2,1,0:T(8,128)(2,1)S(1)}, u32[]{:S(2)}, u32[]{:S(2)}) collective-permute-start(bf16[3,80,128]{2,1,0:T(8,128)(2,1)S(1)} %pad_maximum_fusion), channel_id=1, source_target_pairs={{0,3},{1,4},{2,5},{3,6},{4,7},{5,8},{6,9},{7,10},{8,11},{9,12},{10... | collective-permute-start | bytes 184328 | tf_op jit(solution)/shard_map/ppermute | solution.py:567
where the time goes:
time: 69.8 us; the launch traced here: 69.5 us
  waiting for transfers between devices  34.4 us (49%)
  starting transfers between devices  19.5 us (28%)
  Pallas kernels  13.9 us (20%)
  between operations  0.95 us (1%)
  local copies, waits for them, and re-layouts  0.71 us (1%)
    ppermute x8, waiting for transfers between devices, per_device(): nexts[across] = lax.ppermute(nexts[across], 'tile', pairs)  28.2 us
    ppermute x8, starting transfers between devices, per_device(): nexts[across] = lax.ppermute(nexts[across], 'tile', pairs)  10.3 us
    all_to_all x1, starting transfers between devices, per_device(): lax.all_to_all(same, 'tile', 0, 0, axis_index_groups=[[c * column_rows +...  6.53 us
    ppermute x4, waiting for transfers between devices, from_shift(): lax.ppermute(value, 'tile', [(i, (i - shift) % count) for i in range(coun...  6.29 us
    pallas_call x1, Pallas kernels, regrid(): pl.pallas_call(functools.partial(regrid_kernel, column_rows), in_specs=[h...  4.9 us
    pallas_call x1, Pallas kernels, convolutions(): pl.pallas_call(functools.partial(conv_kernel, column_rows), in_specs=[vme...  3.72 us
    ppermute x4, starting transfers between devices, from_shift(): lax.ppermute(value, 'tile', [(i, (i - shift) % count) for i in range(coun...  2.66 us
    pallas_call x1, Pallas kernels, gather_rows(): pl.pallas_call(functools.partial(gather_kernel, column_rows), in_specs=[s...  2.12 us
  transfers between devices with their start and end apart: 13, of which 7 were waited for; matrix products, arithmetic and copies ran while one was open for 1% of the time, Pallas kernels for 5%

commit v1 on v0

--- a/solution.py
+++ b/solution.py
@@ -335,7 +335,7 @@
         elif row == ROWS - 1:
             ends[1] = value
         else:
-            hidden[row] = activated(value)
+            hidden[row] = jnp.where((lane == 0) | (lane == BLOCK - 1), blank, activated(value))
         west = jnp.where(lane == row, pltpu.roll(value, row, 1), west)
         east = jnp.where(lane == row, pltpu.roll(value, row + 1, 1), east)
     hidden[0] = blank
@@ -360,6 +360,39 @@
     )(taps, field)
 
 
+def second_kernel_inner(taps_ref, hidden, gridded, base, partial):
+    taps = taps_ref[...]
+    blank = jnp.zeros((WIDE, BLOCK), jnp.bfloat16)
+    for row in range(0, ROWS, 2):
+        partial[row], partial[row + 1] = tap_sums(
+            taps,
+            shifted_columns(hidden[row], blank, blank),
+            shifted_columns(hidden[row + 1], blank, blank),
+        )
+    for row in range(ROWS):
+        value = gridded[row].astype(jnp.float32) + partial[row, WIDE : WIDE + PADDED]
+        if row > 0:
+            value = value + partial[row - 1, :PADDED]
+        if row < ROWS - 1:
+            value = value + partial[row + 1, 2 * WIDE : 2 * WIDE + PADDED]
+        base[row] = value
+
+
+def inner_second_convolution(taps, hidden, gridded):
+    return pl.pallas_call(
+        second_kernel_inner,
+        in_specs=[vmem()] * 3,
+        out_specs=vmem(),
+        out_shape=jax.ShapeDtypeStruct((ROWS, PADDED, BLOCK), jnp.float32),
+        scratch_shapes=[pltpu.VMEM((ROWS, 3 * WIDE, BLOCK), jnp.float32)],
+        compiler_params=pltpu.CompilerParams(vmem_limit_bytes=VMEM_LIMIT),
+        cost_estimate=pl.CostEstimate(
+            flops=2 * 9 * WIDE * WIDE * ROWS * BLOCK, bytes_accessed=2 << 20, transcendentals=0
+        ),
+        name="inner_second_convolution",
+    )(taps, hidden, gridded)
+
+
 def strip_plan(column_rows):
     if column_rows == 2:
         return [], 3, 1
@@ -371,8 +404,7 @@
     first_taps_ref,
     second_taps_ref,
     field,
-    gridded,
-    inner,
+    base,
     ends_ref,
     sides_ref,
     above,
@@ -382,7 +414,7 @@
 ):
     near, far, reach = strip_plan(column_rows)
     near_strips, (west_pack, east_pack) = rest[: len(near)], rest[len(near) : len(near) + 2]
-    smoothed, hidden, partial, turned = rest[len(near) + 2 :]
+    smoothed, turned = rest[len(near) + 2 :]
     count = lax.axis_size("tile")
     tile = lax.axis_index("tile")
     lane = lanes((WIDE, BLOCK))
@@ -474,15 +506,9 @@
     final = ends_ref[1] + from_down
     final = final + jnp.where(lane == 0, pltpu.roll(from_west, BLOCK - ROWS + 1, 1), 0.0)
     final = final + jnp.where(lane == BLOCK - 1, pltpu.roll(from_east, BLOCK - ROWS, 1), 0.0)
-    hidden[1] = activated(first)
-    hidden[ROWS] = activated(final)
+    first, final = activated(first), activated(final)
     first_column = activated(sides_ref[0] + from_west)
     last_column = activated(sides_ref[1] + from_east)
-    for row in range(1, ROWS - 1):
-        value = jnp.where(lane == 0, pltpu.roll(first_column, BLOCK - row, 1), inner[row])
-        hidden[row + 1] = jnp.where(
-            lane == BLOCK - 1, pltpu.roll(last_column, BLOCK - 1 - row, 1), value
-        )
 
     upper = jnp.zeros((WIDE, BLOCK), jnp.float32)
     lower = jnp.zeros((WIDE, BLOCK), jnp.float32)
@@ -497,8 +523,8 @@
         )
         upper += row_tap(one, at)
         lower += row_tap(two, at)
-    hidden[0] = jnp.where(tile > 0, activated(upper), blank)
-    hidden[last] = jnp.where(tile < count - 1, activated(lower), blank)
+    top = jnp.where(tile > 0, activated(upper), blank)
+    bottom = jnp.where(tile < count - 1, activated(lower), blank)
 
     west_hidden, east_hidden = {}, {}
     for at in (-1, 0, 1):
@@ -524,19 +550,66 @@
     ]
 
     second_taps = second_taps_ref[...]
-    for p in range(0, ROWS + 2, 2):
-        partial[p], partial[p + 1] = tap_sums(
-            second_taps,
-            columns(hidden[p], west_side, p, east_side, p),
-            columns(hidden[p + 1], west_side, p + 1, east_side, p + 1),
+    from_top, from_first = tap_sums(
+        second_taps,
+        columns(top, west_side, 0, east_side, 0),
+        columns(first, west_side, 1, east_side, 1),
+    )
+    from_final, from_bottom = tap_sums(
+        second_taps,
+        columns(final, west_side, ROWS, east_side, ROWS),
+        columns(bottom, west_side, last, east_side, last),
+    )
+    rim_rows = {
+        0: row_tap(from_top, 0) + row_tap(from_first, 1),
+        1: row_tap(from_first, 0),
+        ROWS - 2: row_tap(from_final, 2),
+        ROWS - 1: row_tap(from_final, 1) + row_tap(from_bottom, 2),
+    }
+
+    other = (lane >= 2) & (lane < ROWS)
+
+    def other_rows(plane):
+        return jnp.where(other, plane, blank)
+
+    near_west, near_east = other_rows(west_side), other_rows(east_side)
+    first_column = other_rows(pltpu.roll(first_column, 1, 1))
+    last_column = other_rows(pltpu.roll(last_column, 1, 1))
+    to_0, to_1 = tap_sums(
+        second_taps,
+        jnp.concatenate([near_west, first_column, blank], axis=0),
+        jnp.concatenate([first_column, blank, blank], axis=0),
+    )
+    to_127, to_126 = tap_sums(
+        second_taps,
+        jnp.concatenate([blank, last_column, near_east], axis=0),
+        jnp.concatenate([blank, blank, last_column], axis=0),
+    )
+    spread = jnp.zeros((WIDE, BLOCK), jnp.float32)
+    for at, sums in enumerate((to_126, to_127, to_0, to_1)):
+        sums = along(sums)
+        high = sums.astype(jnp.bfloat16)
+        sums = sums - high.astype(jnp.float32)
+        middle = sums.astype(jnp.bfloat16)
+        low = (sums - middle.astype(jnp.float32)).astype(jnp.bfloat16)
+        to_lane = (lanes((BLOCK, BLOCK)) == 4 * row_id + at).astype(jnp.bfloat16)
+        parts = jnp.dot(
+            jnp.concatenate([high, middle, low], axis=0),
+            to_lane,
+            preferred_element_type=jnp.float32,
         )
+        spread = spread + (row_tap(parts, 0) + (row_tap(parts, 1) + row_tap(parts, 2)))
+
+    rim_lanes = lanes((PADDED, BLOCK))
+    rim_lanes = (rim_lanes < 2) | (rim_lanes >= BLOCK - 2)
+    spread = spread[:PADDED]
     for row in range(ROWS):
-        branch = (
-            partial[row, :PADDED]
-            + partial[row + 1, WIDE : WIDE + PADDED]
-            + partial[row + 2, 2 * WIDE : 2 * WIDE + PADDED]
+        value = base[row] + jnp.where(
+            rim_lanes, pltpu.roll(spread, (BLOCK - 4 * row - 2) % BLOCK, 1), 0.0
         )
-        turned[pl.ds(row, PADDED, stride=ROWS), :] = gridded[row].astype(jnp.float32) + branch
+        if row in rim_rows:
+            value = value + rim_rows[row][:PADDED]
+        turned[pl.ds(row, PADDED, stride=ROWS), :] = value
     smoothed[...] = turned[pl.ds(0, CHANNELS * ROWS), :].astype(jnp.bfloat16)
 
 
@@ -547,8 +620,6 @@
         out_specs=vmem(),
         out_shape=jax.ShapeDtypeStruct((CHANNELS * ROWS, BLOCK), jnp.bfloat16),
         scratch_shapes=[
-            pltpu.VMEM((ROWS + 2, WIDE, BLOCK), jnp.bfloat16),
-            pltpu.VMEM((ROWS + 2, 3 * WIDE, BLOCK), jnp.float32),
             pltpu.VMEM((PADDED * ROWS, BLOCK), jnp.float32),
         ],
         compiler_params=pltpu.CompilerParams(vmem_limit_bytes=VMEM_LIMIT),
@@ -582,6 +653,7 @@
             for p in range(column_rows - 1)
         ]
         nexts[across] = lax.ppermute(nexts[across], "tile", pairs)
+    nexts = [nexts[across] for across in (0, 1, 2, 4, 5, 6, 7, 3)]
     same = lax.all_to_all(
         same,
         "tile",
@@ -612,8 +684,10 @@
     pack, inner = lax.optimization_barrier((pack, inner))
     strips += [from_shift(pack, -far), from_shift(pack, far)]
     gridded_out = channels_first(gridded)
+    hidden, *unfinished = inner
+    base = inner_second_convolution(second_taps, hidden, gridded)
     smoothed = convolutions(
-        column_rows, first_taps, second_taps, normed, gridded, *inner, *rims, strip, *strips
+        column_rows, first_taps, second_taps, normed, base, *unfinished, *rims, strip, *strips
     )
 
     def placed(value):

time: 69.8 us -> 69.1 us (0.990)
  waiting for transfers between devices: 34.4 us -> 30.7 us
  starting transfers between devices: 19.5 us -> 21.9 us
    ppermute x4, waiting for transfers between devices: 6.29 us -> 2.62 us  [from_shift(): lax.ppermute(value, 'tile', [(i, (i - shift) % count) for i in range(coun...]
    ppermute x4, starting transfers between devices: 2.66 us -> 5.05 us  [from_shift(): lax.ppermute(value, 'tile', [(i, (i - shift) % count) for i in range(coun...]
    pallas_call x0 -> x1, Pallas kernels: none -> 0.79 us  [inner_second_convolution(): pl.pallas_call(second_kernel_inner, in_specs=[vmem()] * 3, out_specs=vmem...]
  transfers between devices with their start and end apart: 13 -> 13, of which waited for: 7 -> 5; matrix products, arithmetic and copies ran while one was open for 1% -> 1% of each run, Pallas kernels for 5% -> 6%
where the time goes in v1:
time: 69.1 us; the launch traced here: 68.7 us
  waiting for transfers between devices  30.7 us (44%)
  starting transfers between devices  21.9 us (32%)
  Pallas kernels  14.5 us (21%)
  between operations  0.98 us (1%)
  local copies, waits for them, and re-layouts  0.71 us (1%)
    ppermute x8, waiting for transfers between devices, per_device(): nexts[across] = lax.ppermute(nexts[across], 'tile', pairs)  28.1 us
    ppermute x8, starting transfers between devices, per_device(): nexts[across] = lax.ppermute(nexts[across], 'tile', pairs)  10.3 us
    all_to_all x1, starting transfers between devices, per_device(): lax.all_to_all(same, 'tile', 0, 0, axis_index_groups=[[c * column_rows +...  6.53 us
    ppermute x4, starting transfers between devices, from_shift(): lax.ppermute(value, 'tile', [(i, (i - shift) % count) for i in range(coun...  5.05 us
    pallas_call x1, Pallas kernels, regrid(): pl.pallas_call(functools.partial(regrid_kernel, column_rows), in_specs=[h...  4.9 us
    pallas_call x1, Pallas kernels, convolutions(): pl.pallas_call(functools.partial(conv_kernel, column_rows), in_specs=[vme...  3.45 us
    ppermute x4, waiting for transfers between devices, from_shift(): lax.ppermute(value, 'tile', [(i, (i - shift) % count) for i in range(coun...  2.62 us
    pallas_call x1, Pallas kernels, gather_rows(): pl.pallas_call(functools.partial(gather_kernel, column_rows), in_specs=[s...  2.12 us
  transfers between devices with their start and end apart: 13, of which 5 were waited for; matrix products, arithmetic and copies ran while one was open for 1% of the time, Pallas kernels for 6%

profile of v1, /device:TPU:1, one launch (start us, length us, event | category | flops | bytes accessed | tf_op | source)
XLA Modules:
  0.0 68.7 jit_solution(12203889388039676494)
XLA Ops:
  0.6 4.9 %regrid.1 = (bf16[64,72,128]{2,1,0:T(8,128)(2,1)}, bf16[8,72,128]{2,1,0:T(8,128)(2,1)}, bf16[8,72,128]{2,1,0:T(8,128)(2,1)}, bf16[8,72,128]{2,1,0:T(8,128)(2,1)}...) custom-call(s32[96]{0:T(128)} %target_hbm.1, ...), custom_call_target="tpu_custom_call" | custom-call | tf_op jit(solution)/shard_map/regrid/pallas_call | solution.py:170
  5.5 0.0 copy-start.8
  5.5 0.0 copy-start.7
  5.6 0.0 copy-start.6
  5.6 0.0 copy-start.5
  5.6 0.0 copy-start.4
  5.6 0.0 copy-start.3
  5.6 0.0 copy-start.1
  5.6 0.0 copy-start.2
  5.6 6.5 %all-to-all-start = ((bf16[64,72,128]{2,1,0:T(8,128)(2,1)}), bf16[64,72,128]{2,1,0:T(8,128)(2,1)S(1)}, u32[]{:S(2)}, u32[]{:S(2)}) async-start(bf16[64,72,128]{2,1,0:T(8,128)(2,1)} %get-tuple-element.35), calls=%async_computation | async-start | bytes 2359296 | tf_op jit(solution)/shard_map/all_to_all | solution.py:657
  12.2 0.0 copy-start
  12.2 1.3 %collective-permute-start = (bf16[8,72,128]{2,1,0:T(8,128)(2,1)S(1)}, bf16[8,72,128]{2,1,0:T(8,128)(2,1)S(1)}, u32[]{:S(2)}, u32[]{:S(2)}) collective-permute-start(bf16[8,72,128]{2,1,0:T(8,128)(2,1)S(1)} %copy-done.8), channel_id=1, source_target_pairs={{0,1},{2,3},{4,5},{6,7},{8,9},{10,11},{12,13},{14,15},{16,17},{18,... | collective-permute-start | bytes 442376 | tf_op jit(solution)/shard_map/ppermute | solution.py:655
  13.5 1.3 %collective-permute-start.1 = (bf16[8,72,128]{2,1,0:T(8,128)(2,1)S(1)}, bf16[8,72,128]{2,1,0:T(8,128)(2,1)S(1)}, u32[]{:S(2)}, u32[]{:S(2)}) collective-permute-start(bf16[8,72,128]{2,1,0:T(8,128)(2,1)S(1)} %copy-done.7), channel_id=1, source_target_pairs={{0,3},{2,1},{4,7},{6,5},{8,11},{10,9},{12,15},{14,13},{16,19},{18,... | collective-permute-start | bytes 442376 | tf_op jit(solution)/shard_map/ppermute | solution.py:655
  14.8 1.3 %collective-permute-start.2 = (bf16[8,72,128]{2,1,0:T(8,128)(2,1)S(1)}, bf16[8,72,128]{2,1,0:T(8,128)(2,1)S(1)}, u32[]{:S(2)}, u32[]{:S(2)}) collective-permute-start(bf16[8,72,128]{2,1,0:T(8,128)(2,1)S(1)} %copy-done.6), channel_id=1, source_target_pairs={{0,5},{2,7},{4,1},{6,3},{8,13},{10,15},{12,9},{14,11},{16,21},{18,... | collective-permute-start | bytes 442376 | tf_op jit(solution)/shard_map/ppermute | solution.py:655
  16.1 1.3 %collective-permute-start.3 = (bf16[8,72,128]{2,1,0:T(8,128)(2,1)}, bf16[8,72,128]{2,1,0:T(8,128)(2,1)S(1)}, u32[]{:S(2)}, u32[]{:S(2)}) collective-permute-start(bf16[8,72,128]{2,1,0:T(8,128)(2,1)} %get-tuple-element.39), channel_id=1, source_target_pairs={{0,9},{2,11},{4,13},{6,15},{8,1},{10,3},{12,5},{14,7},{16,25},{18,... | collective-permute-start | bytes 442376 | tf_op jit(solution)/shard_map/ppermute | solution.py:655
  17.4 1.3 %collective-permute-start.4 = (bf16[8,72,128]{2,1,0:T(8,128)(2,1)}, bf16[8,72,128]{2,1,0:T(8,128)(2,1)S(1)}, u32[]{:S(2)}, u32[]{:S(2)}) collective-permute-start(bf16[8,72,128]{2,1,0:T(8,128)(2,1)} %get-tuple-element.40), channel_id=1, source_target_pairs={{0,11},{2,9},{4,15},{6,13},{8,3},{10,1},{12,7},{14,5},{16,27},{18,... | collective-permute-start | bytes 442376 | tf_op jit(solution)/shard_map/ppermute | solution.py:655
  18.7 0.0 collective-permute-done.rest_0_
  18.7 1.3 %collective-permute-start.5 = (bf16[8,72,128]{2,1,0:T(8,128)(2,1)S(1)}, bf16[8,72,128]{2,1,0:T(8,128)(2,1)S(1)}, u32[]{:S(2)}, u32[]{:S(2)}) collective-permute-start(bf16[8,72,128]{2,1,0:T(8,128)(2,1)S(1)} %copy-done.5), channel_id=1, source_target_pairs={{0,13},{2,15},{4,9},{6,11},{8,5},{10,7},{12,1},{14,3},{16,29},{18,... | collective-permute-start | bytes 442376 | tf_op jit(solution)/shard_map/ppermute | solution.py:655
  20.0 4.0 %collective-permute-done.1.rest_1_ = bf16[8,72,128]{2,1,0:T(8,128)(2,1)S(1)} collective-permute-done((bf16[8,72,128]{2,1,0:T(8,128)(2,1)S(1)}, bf16[8,72,128]{2,1,0:T(8,128)(2,1)S(1)}, u32[]{:S(2)}, u32[]{:S(2)}) %collective-permute-start.1) | collective-permute-done | bytes 147488 | tf_op jit(solution)/shard_map/ppermute | solution.py:655
  24.1 1.3 %collective-permute-start.6 = (bf16[8,72,128]{2,1,0:T(8,128)(2,1)S(1)}, bf16[8,72,128]{2,1,0:T(8,128)(2,1)S(1)}, u32[]{:S(2)}, u32[]{:S(2)}) collective-permute-start(bf16[8,72,128]{2,1,0:T(8,128)(2,1)S(1)} %copy-done.4), channel_id=1, source_target_pairs={{0,15},{2,13},{4,11},{6,9},{8,7},{10,5},{12,3},{14,1},{16,31},{18,... | collective-permute-start | bytes 442376 | tf_op jit(solution)/shard_map/ppermute | solution.py:655
  25.4 4.7 %collective-permute-done.2.rest_2_ = bf16[8,72,128]{2,1,0:T(8,128)(2,1)S(1)} collective-permute-done((bf16[8,72,128]{2,1,0:T(8,128)(2,1)S(1)}, bf16[8,72,128]{2,1,0:T(8,128)(2,1)S(1)}, u32[]{:S(2)}, u32[]{:S(2)}) %collective-permute-start.2) | collective-permute-done | bytes 147488 | tf_op jit(solution)/shard_map/ppermute | solution.py:655
  30.0 1.3 %collective-permute-start.7 = (bf16[8,72,128]{2,1,0:T(8,128)(2,1)S(1)}, bf16[8,72,128]{2,1,0:T(8,128)(2,1)S(1)}, u32[]{:S(2)}, u32[]{:S(2)}) collective-permute-start(bf16[8,72,128]{2,1,0:T(8,128)(2,1)S(1)} %copy-done.3), channel_id=1, source_target_pairs={{0,7},{2,5},{4,3},{6,1},{8,15},{10,13},{12,11},{14,9},{16,23},{18,... | collective-permute-start | bytes 442376 | tf_op jit(solution)/shard_map/ppermute | solution.py:655
  31.4 0.1 copy.17
  31.5 0.2 reshape.36.taps_ref.first_taps_ref
  31.6 0.0 copy-done.2
  31.7 0.1 copy.16
  31.8 0.2 reshape.38.taps_ref.second_taps_ref
  32.0 17.0 %collective-permute-done.3.rest_3_ = bf16[8,72,128]{2,1,0:T(8,128)(2,1)S(1)} collective-permute-done((bf16[8,72,128]{2,1,0:T(8,128)(2,1)}, bf16[8,72,128]{2,1,0:T(8,128)(2,1)S(1)}, u32[]{:S(2)}, u32[]{:S(2)}) %collective-permute-start.3) | collective-permute-done | bytes 147488 | tf_op jit(solution)/shard_map/ppermute | solution.py:655
  48.9 2.4 %collective-permute-done.4.rest_4_ = bf16[8,72,128]{2,1,0:T(8,128)(2,1)S(1)} collective-permute-done((bf16[8,72,128]{2,1,0:T(8,128)(2,1)}, bf16[8,72,128]{2,1,0:T(8,128)(2,1)S(1)}, u32[]{:S(2)}, u32[]{:S(2)}) %collective-permute-start.4) | collective-permute-done | bytes 147488 | tf_op jit(solution)/shard_map/ppermute | solution.py:655
  51.3 0.0 collective-permute-done.5.rest_5_
  51.3 0.0 collective-permute-done.6.rest_6_
  51.3 0.0 collective-permute-done.7.rest_7_
  51.3 0.0 all-to-all-done.same
  51.4 0.1 broadcast_in_dim.12.gain_ref
  51.4 0.0 copy-done
  51.4 2.1 %gather_rows.1 = (bf16[32,72,128]{2,1,0:T(8,128)(2,1)S(1)}, bf16[32,80,128]{2,1,0:T(8,128)(2,1)S(1)}, bf16[3,80,128]{2,1,0:T(8,128)(2,1)S(1)}, bf16[3,80,128]{2,1,0:T(8,128)(2,1)S(1)}, bf16[80,128]{1,0:T(8,128)(2,1)S(1)}) custom-call(s32[1,2]{1,0:T(1,128)S(1)} %copy-done, f32[72,128]{1,0:T(8,128)S(1)} %broadcast_in_dim.12.gain_ref, ...), custom_call_target="tpu_custom_call" | custom-call | tf_op jit(solution)/shard_map/gather_rows/pallas_call | solution.py:263
  53.6 0.1 collective-permute-start.8
  53.6 0.5 collective-permute-start.9
  54.1 1.2 %inner_convolution.1 = (bf16[32,80,128]{2,1,0:T(8,128)(2,1)S(1)}, f32[2,80,128]{2,1,0:T(8,128)S(1)}, f32[2,80,128]{2,1,0:T(8,128)S(1)}) custom-call(bf16[240,240]{1,0:T(8,128)(2,1)S(1)} %reshape.36.taps_ref.first_taps_ref, bf16[32,80,128]{2,1,0:T(8,128)(2,1)S(1)} %get-tuple-element.57.field), custom_call_target="tpu_custom_call" | custom-call | flops 471859200 | bytes 2097152 | tf_op jit(solution)/shard_map/inner_convolution/pallas_call | solution.py:349
  55.3 0.0 collective-permute-done.8.above
  55.4 2.6 %collective-permute-done.9.below = bf16[3,80,128]{2,1,0:T(8,128)(2,1)S(1)} collective-permute-done((bf16[3,80,128]{2,1,0:T(8,128)(2,1)S(1)}, bf16[3,80,128]{2,1,0:T(8,128)(2,1)S(1)}, u32[]{:S(2)}, u32[]{:S(2)}) %collective-permute-start.9) | collective-permute-done | bytes 61472 | tf_op jit(solution)/shard_map/ppermute | solution.py:638
  58.0 1.4 %collective-permute-start.10 = (bf16[3,80,128]{2,1,0:T(8,128)(2,1)S(1)}, bf16[3,80,128]{2,1,0:T(8,128)(2,1)S(1)}, u32[]{:S(2)}, u32[]{:S(2)}) collective-permute-start(bf16[3,80,128]{2,1,0:T(8,128)(2,1)S(1)} %pad_maximum_fusion), channel_id=1, source_target_pairs={{0,3},{1,4},{2,5},{3,6},{4,7},{5,8},{6,9},{7,10},{8,11},{9,12},{10... | collective-permute-start | bytes 184328 | tf_op jit(solution)/shard_map/ppermute | solution.py:638
  59.4 3.1 %collective-permute-start.11 = (bf16[3,80,128]{2,1,0:T(8,128)(2,1)S(1)}, bf16[3,80,128]{2,1,0:T(8,128)(2,1)S(1)}, u32[]{:S(2)}, u32[]{:S(2)}) collective-permute-start(bf16[3,80,128]{2,1,0:T(8,128)(2,1)S(1)} %pad_maximum_fusion), channel_id=1, source_target_pairs={{0,13},{1,14},{2,15},{3,0},{4,1},{5,2},{6,3},{7,4},{8,5},{9,6},{10... | collective-permute-start | bytes 184328 | tf_op jit(solution)/shard_map/ppermute | solution.py:638
  62.5 2.0 %channels_first.1 = bf16[2208,128]{1,0:T(8,128)(2,1)} custom-call(bf16[32,72,128]{2,1,0:T(8,128)(2,1)S(1)} %get-tuple-element.54.field.gridded), custom_call_target="tpu_custom_call" | custom-call | tf_op jit(solution)/shard_map/channels_first/pallas_call | solution.py:283
  64.5 0.8 %inner_second_convolution.1.base = f32[32,72,128]{2,1,0:T(8,128)S(1)} custom-call(bf16[240,240]{1,0:T(8,128)(2,1)S(1)} %reshape.38.taps_ref.second_taps_ref, bf16[32,80,128]{2,1,0:T(8,128)(2,1)S(1)} %get-tuple-element.64.hidden, bf16[32,72,128]{2,1,0:T(8,128)(2,1)S(1)} %get-tuple-element.54.field.gridded), custom_call_target="tpu_custom_call" | custom-call | flops 471859200 | bytes 2097152 | tf_op jit(solution)/shard_map/inner_second_convolution/pallas_call | solution.py:382
  65.3 0.0 collective-permute-done.10.rest_0_
  65.3 0.0 collective-permute-done.11.rest_1_
  65.3 3.5 %convolutions.1 = bf16[2208,128]{1,0:T(8,128)(2,1)} custom-call(bf16[240,240]{1,0:T(8,128)(2,1)S(1)} %reshape.36.taps_ref.first_taps_ref, bf16[240,240]{1,0:T(8,128)(2,1)S(1)} %reshape.38.taps_ref.second_taps_ref, bf16[32,80,128]{2,1,0:T(8,128)(2,1)S(1)} %get-tuple-element.57.field, f32[32,72,128]{2,1,0:T(8,128)S(1)} %inner_second_convolution.1.base, ...), custom_call_target="tpu_custom_call" | custom-call | tf_op jit(solution)/shard_map/convolutions/pallas_call | solution.py:617
  (15 shorter events, 0.1 us)
Async XLA Ops:
  5.5 6.6 %copy-start.8 = (bf16[8,72,128]{2,1,0:T(8,128)(2,1)S(1)}, bf16[8,72,128]{2,1,0:T(8,128)(2,1)}, u32[]{:S(2)}) copy-start(bf16[8,72,128]{2,1,0:T(8,128)(2,1)} %get-tuple-element.36) | copy-start | bytes 442372
  5.5 7.9 %copy-start.7 = (bf16[8,72,128]{2,1,0:T(8,128)(2,1)S(1)}, bf16[8,72,128]{2,1,0:T(8,128)(2,1)}, u32[]{:S(2)}) copy-start(bf16[8,72,128]{2,1,0:T(8,128)(2,1)} %get-tuple-element.37) | copy-start | bytes 442372
  5.6 9.2 %copy-start.6 = (bf16[8,72,128]{2,1,0:T(8,128)(2,1)S(1)}, bf16[8,72,128]{2,1,0:T(8,128)(2,1)}, u32[]{:S(2)}) copy-start(bf16[8,72,128]{2,1,0:T(8,128)(2,1)} %get-tuple-element.38) | copy-start | bytes 442372
  5.6 13.1 %copy-start.5 = (bf16[8,72,128]{2,1,0:T(8,128)(2,1)S(1)}, bf16[8,72,128]{2,1,0:T(8,128)(2,1)}, u32[]{:S(2)}) copy-start(bf16[8,72,128]{2,1,0:T(8,128)(2,1)} %get-tuple-element.41) | copy-start | bytes 442372
  5.6 18.5 %copy-start.4 = (bf16[8,72,128]{2,1,0:T(8,128)(2,1)S(1)}, bf16[8,72,128]{2,1,0:T(8,128)(2,1)}, u32[]{:S(2)}) copy-start(bf16[8,72,128]{2,1,0:T(8,128)(2,1)} %get-tuple-element.42) | copy-start | bytes 442372
  5.6 24.4 %copy-start.3 = (bf16[8,72,128]{2,1,0:T(8,128)(2,1)S(1)}, bf16[8,72,128]{2,1,0:T(8,128)(2,1)}, u32[]{:S(2)}) copy-start(bf16[8,72,128]{2,1,0:T(8,128)(2,1)} %get-tuple-element.43) | copy-start | bytes 442372
  5.6 25.7 %copy-start.1 = (bf16[9,69,69]{2,1,0:T(8,128)(2,1)S(1)}, bf16[9,69,69]{2,1,0:T(8,128)(2,1)}, u32[]{:S(2)}) copy-start(bf16[9,69,69]{2,1,0:T(8,128)(2,1)} %param.14) | copy-start | bytes 257098
  5.6 26.0 %copy-start.2 = (bf16[9,69,69]{2,1,0:T(8,128)(2,1)S(1)}, bf16[9,69,69]{2,1,0:T(8,128)(2,1)}, u32[]{:S(2)}) copy-start(bf16[9,69,69]{2,1,0:T(8,128)(2,1)} %param.15) | copy-start | bytes 257098
  5.6 45.7 %all-to-all-start = ((bf16[64,72,128]{2,1,0:T(8,128)(2,1)}), bf16[64,72,128]{2,1,0:T(8,128)(2,1)S(1)}, u32[]{:S(2)}, u32[]{:S(2)}) async-start(bf16[64,72,128]{2,1,0:T(8,128)(2,1)} %get-tuple-element.35), calls=%async_computation | async-start | bytes 2359296 | tf_op jit(solution)/shard_map/all_to_all | solution.py:657
  12.2 19.8 %copy-start.9 = (f32[69]{0:T(128)S(1)}, f32[69]{0:T(128)}, u32[]{:S(2)}) copy-start(f32[69]{0:T(128)} %param.13) | copy-start | bytes 832
  12.2 39.3 %copy-start = (s32[1,2]{1,0:T(1,128)S(1)}, s32[1,2]{1,0:T(1,128)}, u32[]{:S(2)}) copy-start(s32[1,2]{1,0:T(1,128)} %flip_ref.1) | copy-start | bytes 28
  12.2 6.5 %collective-permute-start = (bf16[8,72,128]{2,1,0:T(8,128)(2,1)S(1)}, bf16[8,72,128]{2,1,0:T(8,128)(2,1)S(1)}, u32[]{:S(2)}, u32[]{:S(2)}) collective-permute-start(bf16[8,72,128]{2,1,0:T(8,128)(2,1)S(1)} %copy-done.8), channel_id=1, source_target_pairs={{0,1},{2,3},{4,5},{6,7},{8,9},{10,11},{12,13},{14,15},{16,17},{18,... | collective-permute-start | bytes 442376 | tf_op jit(solution)/shard_map/ppermute | solution.py:655
  13.5 10.6 %collective-permute-start.1 = (bf16[8,72,128]{2,1,0:T(8,128)(2,1)S(1)}, bf16[8,72,128]{2,1,0:T(8,128)(2,1)S(1)}, u32[]{:S(2)}, u32[]{:S(2)}) collective-permute-start(bf16[8,72,128]{2,1,0:T(8,128)(2,1)S(1)} %copy-done.7), channel_id=1, source_target_pairs={{0,3},{2,1},{4,7},{6,5},{8,11},{10,9},{12,15},{14,13},{16,19},{18,... | collective-permute-start | bytes 442376 | tf_op jit(solution)/shard_map/ppermute | solution.py:655
  14.8 15.2 %collective-permute-start.2 = (bf16[8,72,128]{2,1,0:T(8,128)(2,1)S(1)}, bf16[8,72,128]{2,1,0:T(8,128)(2,1)S(1)}, u32[]{:S(2)}, u32[]{:S(2)}) collective-permute-start(bf16[8,72,128]{2,1,0:T(8,128)(2,1)S(1)} %copy-done.6), channel_id=1, source_target_pairs={{0,5},{2,7},{4,1},{6,3},{8,13},{10,15},{12,9},{14,11},{16,21},{18,... | collective-permute-start | bytes 442376 | tf_op jit(solution)/shard_map/ppermute | solution.py:655
  16.1 32.8 %collective-permute-start.3 = (bf16[8,72,128]{2,1,0:T(8,128)(2,1)}, bf16[8,72,128]{2,1,0:T(8,128)(2,1)S(1)}, u32[]{:S(2)}, u32[]{:S(2)}) collective-permute-start(bf16[8,72,128]{2,1,0:T(8,128)(2,1)} %get-tuple-element.39), channel_id=1, source_target_pairs={{0,9},{2,11},{4,13},{6,15},{8,1},{10,3},{12,5},{14,7},{16,25},{18,... | collective-permute-start | bytes 442376 | tf_op jit(solution)/shard_map/ppermute | solution.py:655
  17.4 33.9 %collective-permute-start.4 = (bf16[8,72,128]{2,1,0:T(8,128)(2,1)}, bf16[8,72,128]{2,1,0:T(8,128)(2,1)S(1)}, u32[]{:S(2)}, u32[]{:S(2)}) collective-permute-start(bf16[8,72,128]{2,1,0:T(8,128)(2,1)} %get-tuple-element.40), channel_id=1, source_target_pairs={{0,11},{2,9},{4,15},{6,13},{8,3},{10,1},{12,7},{14,5},{16,27},{18,... | collective-permute-start | bytes 442376 | tf_op jit(solution)/shard_map/ppermute | solution.py:655
  18.7 32.6 %collective-permute-start.5 = (bf16[8,72,128]{2,1,0:T(8,128)(2,1)S(1)}, bf16[8,72,128]{2,1,0:T(8,128)(2,1)S(1)}, u32[]{:S(2)}, u32[]{:S(2)}) collective-permute-start(bf16[8,72,128]{2,1,0:T(8,128)(2,1)S(1)} %copy-done.5), channel_id=1, source_target_pairs={{0,13},{2,15},{4,9},{6,11},{8,5},{10,7},{12,1},{14,3},{16,29},{18,... | collective-permute-start | bytes 442376 | tf_op jit(solution)/shard_map/ppermute | solution.py:655
  24.1 27.3 %collective-permute-start.6 = (bf16[8,72,128]{2,1,0:T(8,128)(2,1)S(1)}, bf16[8,72,128]{2,1,0:T(8,128)(2,1)S(1)}, u32[]{:S(2)}, u32[]{:S(2)}) collective-permute-start(bf16[8,72,128]{2,1,0:T(8,128)(2,1)S(1)} %copy-done.4), channel_id=1, source_target_pairs={{0,15},{2,13},{4,11},{6,9},{8,7},{10,5},{12,3},{14,1},{16,31},{18,... | collective-permute-start | bytes 442376 | tf_op jit(solution)/shard_map/ppermute | solution.py:655
  30.0 21.3 %collective-permute-start.7 = (bf16[8,72,128]{2,1,0:T(8,128)(2,1)S(1)}, bf16[8,72,128]{2,1,0:T(8,128)(2,1)S(1)}, u32[]{:S(2)}, u32[]{:S(2)}) collective-permute-start(bf16[8,72,128]{2,1,0:T(8,128)(2,1)S(1)} %copy-done.3), channel_id=1, source_target_pairs={{0,7},{2,5},{4,3},{6,1},{8,15},{10,13},{12,11},{14,9},{16,23},{18,... | collective-permute-start | bytes 442376 | tf_op jit(solution)/shard_map/ppermute | solution.py:655
  53.6 1.8 %collective-permute-start.8 = (bf16[3,80,128]{2,1,0:T(8,128)(2,1)S(1)}, bf16[3,80,128]{2,1,0:T(8,128)(2,1)S(1)}, u32[]{:S(2)}, u32[]{:S(2)}) collective-permute-start(bf16[3,80,128]{2,1,0:T(8,128)(2,1)S(1)} %get-tuple-element.58), channel_id=1, source_target_pairs={{0,1},{1,2},{2,3},{3,4},{4,5},{5,6},{6,7},{7,8},{8,9},{9,10},{10,1... | collective-permute-start | bytes 184328 | tf_op jit(solution)/shard_map/ppermute | solution.py:638
  53.6 4.4 %collective-permute-start.9 = (bf16[3,80,128]{2,1,0:T(8,128)(2,1)S(1)}, bf16[3,80,128]{2,1,0:T(8,128)(2,1)S(1)}, u32[]{:S(2)}, u32[]{:S(2)}) collective-permute-start(bf16[3,80,128]{2,1,0:T(8,128)(2,1)S(1)} %get-tuple-element.60), channel_id=1, source_target_pairs={{0,15},{1,0},{2,1},{3,2},{4,3},{5,4},{6,5},{7,6},{8,7},{9,8},{10,9... | collective-permute-start | bytes 184328 | tf_op jit(solution)/shard_map/ppermute | solution.py:638
  58.0 7.3 %collective-permute-start.10 = (bf16[3,80,128]{2,1,0:T(8,128)(2,1)S(1)}, bf16[3,80,128]{2,1,0:T(8,128)(2,1)S(1)}, u32[]{:S(2)}, u32[]{:S(2)}) collective-permute-start(bf16[3,80,128]{2,1,0:T(8,128)(2,1)S(1)} %pad_maximum_fusion), channel_id=1, source_target_pairs={{0,3},{1,4},{2,5},{3,6},{4,7},{5,8},{6,9},{7,10},{8,11},{9,12},{10... | collective-permute-start | bytes 184328 | tf_op jit(solution)/shard_map/ppermute | solution.py:638
  59.4 5.9 %collective-permute-start.11 = (bf16[3,80,128]{2,1,0:T(8,128)(2,1)S(1)}, bf16[3,80,128]{2,1,0:T(8,128)(2,1)S(1)}, u32[]{:S(2)}, u32[]{:S(2)}) collective-permute-start(bf16[3,80,128]{2,1,0:T(8,128)(2,1)S(1)} %pad_maximum_fusion), channel_id=1, source_target_pairs={{0,13},{1,14},{2,15},{3,0},{4,1},{5,2},{6,3},{7,4},{8,5},{9,6},{10... | collective-permute-start | bytes 184328 | tf_op jit(solution)/shard_map/ppermute | solution.py:638

commit v2 on v1

--- a/solution.py
+++ b/solution.py
@@ -15,7 +15,9 @@
 ROW_BITS = 5
 TILE_COLS = 8
 CAP = 8
+HALF = TILE_COLS // 2
 GROUPS = 2 * TILE_COLS
+COLUMN_ORDER = [half * HALF + at for at in range(HALF) for half in range(2)]
 SLOTS = GROUPS * CAP
 CHUNK = 96
 MARK = CHANNELS
@@ -89,9 +91,8 @@
     target = target_row_ref[...]
     owner, row = split(target, ROWS)
     owner_column, owner_position = split(owner, column_rows)
-    group = jnp.where(
-        owner_position == position, owner_column, TILE_COLS + (owner_column ^ column)
-    )
+    place = ((owner_column & (HALF - 1)) << 1) + (owner_column >= HALF).astype(jnp.int32)
+    group = jnp.where(owner_position == position, place, TILE_COLS + (owner_column ^ column))
     key = group * ROWS + row
     square = (entries, entries)
     down = lax.broadcasted_iota(jnp.int32, square, 0)
@@ -517,12 +518,12 @@
     ):
         from_row = ROWS - 1 + at
         one, two = tap_sums(
-            first_taps,
+            row_tap(first_taps, at),
             columns(high, west[-1], from_row, east[-1], from_row),
             columns(low, west[1], at, east[1], at),
         )
-        upper += row_tap(one, at)
-        lower += row_tap(two, at)
+        upper += one
+        lower += two
     top = jnp.where(tile > 0, activated(upper), blank)
     bottom = jnp.where(tile < count - 1, activated(lower), blank)
 
@@ -660,7 +661,7 @@
         0,
         0,
         axis_index_groups=[
-            [c * column_rows + p for c in range(TILE_COLS)] for p in range(column_rows)
+            [c * column_rows + p for c in COLUMN_ORDER] for p in range(column_rows)
         ],
         tiled=True,
     )
@@ -681,9 +682,9 @@
     inner = inner_convolution(first_taps, normed)
     held = {-1: rims[0][2], 0: strip, 1: rims[1][2], **dict(zip(near, strips))}
     pack = jnp.stack([held[at] for at in range(-reach, reach + 1)])
-    pack, inner = lax.optimization_barrier((pack, inner))
+    gridded_out = channels_first(gridded)
+    pack, inner, gridded_out = lax.optimization_barrier((pack, inner, gridded_out))
     strips += [from_shift(pack, -far), from_shift(pack, far)]
-    gridded_out = channels_first(gridded)
     hidden, *unfinished = inner
     base = inner_second_convolution(second_taps, hidden, gridded)
     smoothed = convolutions(

time: 69.1 us -> 69 us (level)
  transfers between devices with their start and end apart: 13 -> 13, of which waited for: 5 -> 6; matrix products, arithmetic and copies ran while one was open for 1% -> 1% of each run, Pallas kernels for 6% -> 6%
where the time goes in v2:
time: 69 us; the launch traced here: 68.2 us
  waiting for transfers between devices  30.1 us (44%)
  starting transfers between devices  21.9 us (32%)
  Pallas kernels  14.5 us (21%)
  between operations  0.98 us (1%)
  local copies, waits for them, and re-layouts  0.71 us (1%)
    ppermute x8, waiting for transfers between devices, per_device(): nexts[across] = lax.ppermute(nexts[across], 'tile', pairs)  28.1 us
    ppermute x8, starting transfers between devices, per_device(): nexts[across] = lax.ppermute(nexts[across], 'tile', pairs)  10.3 us
    all_to_all x1, starting transfers between devices, per_device(): lax.all_to_all(same, 'tile', 0, 0, axis_index_groups=[[c * column_rows +...  6.52 us
    ppermute x4, starting transfers between devices, from_shift(): lax.ppermute(value, 'tile', [(i, (i - shift) % count) for i in range(coun...  5.05 us
    pallas_call x1, Pallas kernels, regrid(): pl.pallas_call(functools.partial(regrid_kernel, column_rows), in_specs=[h...  4.91 us
    pallas_call x1, Pallas kernels, convolutions(): pl.pallas_call(functools.partial(conv_kernel, column_rows), in_specs=[vme...  3.5 us
    pallas_call x1, Pallas kernels, gather_rows(): pl.pallas_call(functools.partial(gather_kernel, column_rows), in_specs=[s...  2.12 us
    ppermute x4, waiting for transfers between devices, from_shift(): lax.ppermute(value, 'tile', [(i, (i - shift) % count) for i in range(coun...  2.04 us
  transfers between devices with their start and end apart: 13, of which 6 were waited for; matrix products, arithmetic and copies ran while one was open for 1% of the time, Pallas kernels for 6%

profile of v2, /device:TPU:1, one launch (start us, length us, event | category | flops | bytes accessed | tf_op | source)
XLA Modules:
  0.0 68.2 jit_solution(13534546384827841370)
XLA Ops:
  0.6 4.9 %regrid.1 = (bf16[64,72,128]{2,1,0:T(8,128)(2,1)}, bf16[8,72,128]{2,1,0:T(8,128)(2,1)}, bf16[8,72,128]{2,1,0:T(8,128)(2,1)}, bf16[8,72,128]{2,1,0:T(8,128)(2,1)}...) custom-call(s32[96]{0:T(128)} %target_hbm.1, ...), custom_call_target="tpu_custom_call" | custom-call | tf_op jit(solution)/shard_map/regrid/pallas_call | solution.py:171
  5.5 0.0 copy-start.8
  5.6 0.0 copy-start.7
  5.6 0.0 copy-start.6
  5.6 0.0 copy-start.5
  5.6 0.0 copy-start.4
  5.6 0.0 copy-start.3
  5.6 0.0 copy-start.1
  5.6 0.0 copy-start.2
  5.6 6.5 %all-to-all-start = ((bf16[64,72,128]{2,1,0:T(8,128)(2,1)}), bf16[64,72,128]{2,1,0:T(8,128)(2,1)S(1)}, u32[]{:S(2)}, u32[]{:S(2)}) async-start(bf16[64,72,128]{2,1,0:T(8,128)(2,1)} %get-tuple-element.36), calls=%async_computation | async-start | bytes 2359296 | tf_op jit(solution)/shard_map/all_to_all | solution.py:658
  12.2 0.0 copy-done.8
  12.2 0.0 copy-start
  12.2 1.3 %collective-permute-start = (bf16[8,72,128]{2,1,0:T(8,128)(2,1)S(1)}, bf16[8,72,128]{2,1,0:T(8,128)(2,1)S(1)}, u32[]{:S(2)}, u32[]{:S(2)}) collective-permute-start(bf16[8,72,128]{2,1,0:T(8,128)(2,1)S(1)} %copy-done.8), channel_id=1, source_target_pairs={{0,1},{2,3},{4,5},{6,7},{8,9},{10,11},{12,13},{14,15},{16,17},{18,... | collective-permute-start | bytes 442376 | tf_op jit(solution)/shard_map/ppermute | solution.py:656
  13.5 1.3 %collective-permute-start.1 = (bf16[8,72,128]{2,1,0:T(8,128)(2,1)S(1)}, bf16[8,72,128]{2,1,0:T(8,128)(2,1)S(1)}, u32[]{:S(2)}, u32[]{:S(2)}) collective-permute-start(bf16[8,72,128]{2,1,0:T(8,128)(2,1)S(1)} %copy-done.7), channel_id=1, source_target_pairs={{0,3},{2,1},{4,7},{6,5},{8,11},{10,9},{12,15},{14,13},{16,19},{18,... | collective-permute-start | bytes 442376 | tf_op jit(solution)/shard_map/ppermute | solution.py:656
  14.8 1.3 %collective-permute-start.2 = (bf16[8,72,128]{2,1,0:T(8,128)(2,1)S(1)}, bf16[8,72,128]{2,1,0:T(8,128)(2,1)S(1)}, u32[]{:S(2)}, u32[]{:S(2)}) collective-permute-start(bf16[8,72,128]{2,1,0:T(8,128)(2,1)S(1)} %copy-done.6), channel_id=1, source_target_pairs={{0,5},{2,7},{4,1},{6,3},{8,13},{10,15},{12,9},{14,11},{16,21},{18,... | collective-permute-start | bytes 442376 | tf_op jit(solution)/shard_map/ppermute | solution.py:656
  16.1 1.3 %collective-permute-start.3 = (bf16[8,72,128]{2,1,0:T(8,128)(2,1)}, bf16[8,72,128]{2,1,0:T(8,128)(2,1)S(1)}, u32[]{:S(2)}, u32[]{:S(2)}) collective-permute-start(bf16[8,72,128]{2,1,0:T(8,128)(2,1)} %get-tuple-element.40), channel_id=1, source_target_pairs={{0,9},{2,11},{4,13},{6,15},{8,1},{10,3},{12,5},{14,7},{16,25},{18,... | collective-permute-start | bytes 442376 | tf_op jit(solution)/shard_map/ppermute | solution.py:656
  17.4 1.3 %collective-permute-start.4 = (bf16[8,72,128]{2,1,0:T(8,128)(2,1)}, bf16[8,72,128]{2,1,0:T(8,128)(2,1)S(1)}, u32[]{:S(2)}, u32[]{:S(2)}) collective-permute-start(bf16[8,72,128]{2,1,0:T(8,128)(2,1)} %get-tuple-element.41), channel_id=1, source_target_pairs={{0,11},{2,9},{4,15},{6,13},{8,3},{10,1},{12,7},{14,5},{16,27},{18,... | collective-permute-start | bytes 442376 | tf_op jit(solution)/shard_map/ppermute | solution.py:656
  18.7 0.0 collective-permute-done.rest_0_
  18.7 0.0 copy-done.5
  18.7 1.3 %collective-permute-start.5 = (bf16[8,72,128]{2,1,0:T(8,128)(2,1)S(1)}, bf16[8,72,128]{2,1,0:T(8,128)(2,1)S(1)}, u32[]{:S(2)}, u32[]{:S(2)}) collective-permute-start(bf16[8,72,128]{2,1,0:T(8,128)(2,1)S(1)} %copy-done.5), channel_id=1, source_target_pairs={{0,13},{2,15},{4,9},{6,11},{8,5},{10,7},{12,1},{14,3},{16,29},{18,... | collective-permute-start | bytes 442376 | tf_op jit(solution)/shard_map/ppermute | solution.py:656
  20.0 2.9 %collective-permute-done.1.rest_1_ = bf16[8,72,128]{2,1,0:T(8,128)(2,1)S(1)} collective-permute-done((bf16[8,72,128]{2,1,0:T(8,128)(2,1)S(1)}, bf16[8,72,128]{2,1,0:T(8,128)(2,1)S(1)}, u32[]{:S(2)}, u32[]{:S(2)}) %collective-permute-start.1) | collective-permute-done | bytes 147488 | tf_op jit(solution)/shard_map/ppermute | solution.py:656
  22.9 1.3 %collective-permute-start.6 = (bf16[8,72,128]{2,1,0:T(8,128)(2,1)S(1)}, bf16[8,72,128]{2,1,0:T(8,128)(2,1)S(1)}, u32[]{:S(2)}, u32[]{:S(2)}) collective-permute-start(bf16[8,72,128]{2,1,0:T(8,128)(2,1)S(1)} %copy-done.4), channel_id=1, source_target_pairs={{0,15},{2,13},{4,11},{6,9},{8,7},{10,5},{12,3},{14,1},{16,31},{18,... | collective-permute-start | bytes 442376 | tf_op jit(solution)/shard_map/ppermute | solution.py:656
  24.2 8.3 %collective-permute-done.2.rest_2_ = bf16[8,72,128]{2,1,0:T(8,128)(2,1)S(1)} collective-permute-done((bf16[8,72,128]{2,1,0:T(8,128)(2,1)S(1)}, bf16[8,72,128]{2,1,0:T(8,128)(2,1)S(1)}, u32[]{:S(2)}, u32[]{:S(2)}) %collective-permute-start.2) | collective-permute-done | bytes 147488 | tf_op jit(solution)/shard_map/ppermute | solution.py:656
  32.5 1.3 %collective-permute-start.7 = (bf16[8,72,128]{2,1,0:T(8,128)(2,1)S(1)}, bf16[8,72,128]{2,1,0:T(8,128)(2,1)S(1)}, u32[]{:S(2)}, u32[]{:S(2)}) collective-permute-start(bf16[8,72,128]{2,1,0:T(8,128)(2,1)S(1)} %copy-done.3), channel_id=1, source_target_pairs={{0,7},{2,5},{4,3},{6,1},{8,15},{10,13},{12,11},{14,9},{16,23},{18,... | collective-permute-start | bytes 442376 | tf_op jit(solution)/shard_map/ppermute | solution.py:656
  33.8 0.1 copy.17
  33.9 0.2 reshape.36.taps_ref.first_taps_ref
  34.2 0.1 copy.16
  34.3 0.2 reshape.38.taps_ref.second_taps_ref
  34.4 14.4 %collective-permute-done.3.rest_3_ = bf16[8,72,128]{2,1,0:T(8,128)(2,1)S(1)} collective-permute-done((bf16[8,72,128]{2,1,0:T(8,128)(2,1)}, bf16[8,72,128]{2,1,0:T(8,128)(2,1)S(1)}, u32[]{:S(2)}, u32[]{:S(2)}) %collective-permute-start.3) | collective-permute-done | bytes 147488 | tf_op jit(solution)/shard_map/ppermute | solution.py:656
  48.9 2.5 %collective-permute-done.4.rest_4_ = bf16[8,72,128]{2,1,0:T(8,128)(2,1)S(1)} collective-permute-done((bf16[8,72,128]{2,1,0:T(8,128)(2,1)}, bf16[8,72,128]{2,1,0:T(8,128)(2,1)S(1)}, u32[]{:S(2)}, u32[]{:S(2)}) %collective-permute-start.4) | collective-permute-done | bytes 147488 | tf_op jit(solution)/shard_map/ppermute | solution.py:656
  51.4 0.0 collective-permute-done.5.rest_5_
  51.4 0.0 collective-permute-done.6.rest_6_
  51.4 0.0 collective-permute-done.7.rest_7_
  51.4 0.0 all-to-all-done.same
  51.4 0.1 broadcast_in_dim.12.gain_ref
  51.5 2.1 %gather_rows.1 = (bf16[32,72,128]{2,1,0:T(8,128)(2,1)S(1)}, bf16[32,80,128]{2,1,0:T(8,128)(2,1)S(1)}, bf16[3,80,128]{2,1,0:T(8,128)(2,1)S(1)}, bf16[3,80,128]{2,1,0:T(8,128)(2,1)S(1)}, bf16[80,128]{1,0:T(8,128)(2,1)S(1)}) custom-call(s32[1,2]{1,0:T(1,128)S(1)} %copy-done, f32[72,128]{1,0:T(8,128)S(1)} %broadcast_in_dim.12.gain_ref, ...), custom_call_target="tpu_custom_call" | custom-call | tf_op jit(solution)/shard_map/gather_rows/pallas_call | solution.py:264
  53.6 0.1 collective-permute-start.8
  53.7 0.5 collective-permute-start.9
  54.2 2.0 %channels_first.1 = bf16[2208,128]{1,0:T(8,128)(2,1)} custom-call(bf16[32,72,128]{2,1,0:T(8,128)(2,1)S(1)} %get-tuple-element.63.field.gridded), custom_call_target="tpu_custom_call" | custom-call | tf_op jit(solution)/shard_map/channels_first/pallas_call | solution.py:284
  56.1 1.2 %inner_convolution.1 = (bf16[32,80,128]{2,1,0:T(8,128)(2,1)S(1)}, f32[2,80,128]{2,1,0:T(8,128)S(1)}, f32[2,80,128]{2,1,0:T(8,128)S(1)}) custom-call(bf16[240,240]{1,0:T(8,128)(2,1)S(1)} %reshape.36.taps_ref.first_taps_ref, bf16[32,80,128]{2,1,0:T(8,128)(2,1)S(1)} %get-tuple-element.59.field), custom_call_target="tpu_custom_call" | custom-call | flops 471859200 | bytes 2097152 | tf_op jit(solution)/shard_map/inner_convolution/pallas_call | solution.py:350
  57.4 0.0 collective-permute-done.8.above
  57.4 0.0 collective-permute-done.9.below
  57.4 3.4 %collective-permute-start.10 = (bf16[3,80,128]{2,1,0:T(8,128)(2,1)S(1)}, bf16[3,80,128]{2,1,0:T(8,128)(2,1)S(1)}, u32[]{:S(2)}, u32[]{:S(2)}) collective-permute-start(bf16[3,80,128]{2,1,0:T(8,128)(2,1)S(1)} %pad_maximum_fusion), channel_id=1, source_target_pairs={{0,3},{1,4},{2,5},{3,6},{4,7},{5,8},{6,9},{7,10},{8,11},{9,12},{10... | collective-permute-start | bytes 184328 | tf_op jit(solution)/shard_map/ppermute | solution.py:639
  60.8 1.1 %collective-permute-start.11 = (bf16[3,80,128]{2,1,0:T(8,128)(2,1)S(1)}, bf16[3,80,128]{2,1,0:T(8,128)(2,1)S(1)}, u32[]{:S(2)}, u32[]{:S(2)}) collective-permute-start(bf16[3,80,128]{2,1,0:T(8,128)(2,1)S(1)} %pad_maximum_fusion), channel_id=1, source_target_pairs={{0,13},{1,14},{2,15},{3,0},{4,1},{5,2},{6,3},{7,4},{8,5},{9,6},{10... | collective-permute-start | bytes 184328 | tf_op jit(solution)/shard_map/ppermute | solution.py:639
  61.9 0.8 %inner_second_convolution.1.base = f32[32,72,128]{2,1,0:T(8,128)S(1)} custom-call(bf16[240,240]{1,0:T(8,128)(2,1)S(1)} %reshape.38.taps_ref.second_taps_ref, bf16[32,80,128]{2,1,0:T(8,128)(2,1)S(1)} %get-tuple-element.66.hidden, bf16[32,72,128]{2,1,0:T(8,128)(2,1)S(1)} %get-tuple-element.63.field.gridded), custom_call_target="tpu_custom_call" | custom-call | flops 471859200 | bytes 2097152 | tf_op jit(solution)/shard_map/inner_second_convolution/pallas_call | solution.py:383
  62.7 1.4 %collective-permute-done.10.rest_0_ = bf16[3,80,128]{2,1,0:T(8,128)(2,1)S(1)} collective-permute-done((bf16[3,80,128]{2,1,0:T(8,128)(2,1)S(1)}, bf16[3,80,128]{2,1,0:T(8,128)(2,1)S(1)}, u32[]{:S(2)}, u32[]{:S(2)}) %collective-permute-start.10) | collective-permute-done | bytes 61472 | tf_op jit(solution)/shard_map/ppermute | solution.py:639
  64.1 0.6 collective-permute-done.11.rest_1_
  64.7 3.5 %convolutions.1 = bf16[2208,128]{1,0:T(8,128)(2,1)} custom-call(bf16[240,240]{1,0:T(8,128)(2,1)S(1)} %reshape.36.taps_ref.first_taps_ref, bf16[240,240]{1,0:T(8,128)(2,1)S(1)} %reshape.38.taps_ref.second_taps_ref, bf16[32,80,128]{2,1,0:T(8,128)(2,1)S(1)} %get-tuple-element.59.field, f32[32,72,128]{2,1,0:T(8,128)S(1)} %inner_second_convolution.1.base, ...), custom_call_target="tpu_custom_call" | custom-call | tf_op jit(solution)/shard_map/convolutions/pallas_call | solution.py:618
  (15 shorter events, 0.1 us)
Async XLA Ops:
  5.5 6.6 %copy-start.8 = (bf16[8,72,128]{2,1,0:T(8,128)(2,1)S(1)}, bf16[8,72,128]{2,1,0:T(8,128)(2,1)}, u32[]{:S(2)}) copy-start(bf16[8,72,128]{2,1,0:T(8,128)(2,1)} %get-tuple-element.37) | copy-start | bytes 442372
  5.6 7.9 %copy-start.7 = (bf16[8,72,128]{2,1,0:T(8,128)(2,1)S(1)}, bf16[8,72,128]{2,1,0:T(8,128)(2,1)}, u32[]{:S(2)}) copy-start(bf16[8,72,128]{2,1,0:T(8,128)(2,1)} %get-tuple-element.38) | copy-start | bytes 442372
  5.6 9.2 %copy-start.6 = (bf16[8,72,128]{2,1,0:T(8,128)(2,1)S(1)}, bf16[8,72,128]{2,1,0:T(8,128)(2,1)}, u32[]{:S(2)}) copy-start(bf16[8,72,128]{2,1,0:T(8,128)(2,1)} %get-tuple-element.39) | copy-start | bytes 442372
  5.6 13.1 %copy-start.5 = (bf16[8,72,128]{2,1,0:T(8,128)(2,1)S(1)}, bf16[8,72,128]{2,1,0:T(8,128)(2,1)}, u32[]{:S(2)}) copy-start(bf16[8,72,128]{2,1,0:T(8,128)(2,1)} %get-tuple-element.42) | copy-start | bytes 442372
  5.6 17.3 %copy-start.4 = (bf16[8,72,128]{2,1,0:T(8,128)(2,1)S(1)}, bf16[8,72,128]{2,1,0:T(8,128)(2,1)}, u32[]{:S(2)}) copy-start(bf16[8,72,128]{2,1,0:T(8,128)(2,1)} %get-tuple-element.43) | copy-start | bytes 442372
  5.6 26.9 %copy-start.3 = (bf16[8,72,128]{2,1,0:T(8,128)(2,1)S(1)}, bf16[8,72,128]{2,1,0:T(8,128)(2,1)}, u32[]{:S(2)}) copy-start(bf16[8,72,128]{2,1,0:T(8,128)(2,1)} %get-tuple-element.44) | copy-start | bytes 442372
  5.6 28.2 %copy-start.1 = (bf16[9,69,69]{2,1,0:T(8,128)(2,1)S(1)}, bf16[9,69,69]{2,1,0:T(8,128)(2,1)}, u32[]{:S(2)}) copy-start(bf16[9,69,69]{2,1,0:T(8,128)(2,1)} %param.14) | copy-start | bytes 257098
  5.6 28.5 %copy-start.2 = (bf16[9,69,69]{2,1,0:T(8,128)(2,1)S(1)}, bf16[9,69,69]{2,1,0:T(8,128)(2,1)}, u32[]{:S(2)}) copy-start(bf16[9,69,69]{2,1,0:T(8,128)(2,1)} %param.15) | copy-start | bytes 257098
  5.6 45.8 %all-to-all-start = ((bf16[64,72,128]{2,1,0:T(8,128)(2,1)}), bf16[64,72,128]{2,1,0:T(8,128)(2,1)S(1)}, u32[]{:S(2)}, u32[]{:S(2)}) async-start(bf16[64,72,128]{2,1,0:T(8,128)(2,1)} %get-tuple-element.36), calls=%async_computation | async-start | bytes 2359296 | tf_op jit(solution)/shard_map/all_to_all | solution.py:658
  12.1 22.3 %copy-start.9 = (f32[69]{0:T(128)S(1)}, f32[69]{0:T(128)}, u32[]{:S(2)}) copy-start(f32[69]{0:T(128)} %param.13) | copy-start | bytes 832
  12.2 39.3 %copy-start = (s32[1,2]{1,0:T(1,128)S(1)}, s32[1,2]{1,0:T(1,128)}, u32[]{:S(2)}) copy-start(s32[1,2]{1,0:T(1,128)} %flip_ref.1) | copy-start | bytes 28
  12.2 6.5 %collective-permute-start = (bf16[8,72,128]{2,1,0:T(8,128)(2,1)S(1)}, bf16[8,72,128]{2,1,0:T(8,128)(2,1)S(1)}, u32[]{:S(2)}, u32[]{:S(2)}) collective-permute-start(bf16[8,72,128]{2,1,0:T(8,128)(2,1)S(1)} %copy-done.8), channel_id=1, source_target_pairs={{0,1},{2,3},{4,5},{6,7},{8,9},{10,11},{12,13},{14,15},{16,17},{18,... | collective-permute-start | bytes 442376 | tf_op jit(solution)/shard_map/ppermute | solution.py:656
  13.5 9.4 %collective-permute-start.1 = (bf16[8,72,128]{2,1,0:T(8,128)(2,1)S(1)}, bf16[8,72,128]{2,1,0:T(8,128)(2,1)S(1)}, u32[]{:S(2)}, u32[]{:S(2)}) collective-permute-start(bf16[8,72,128]{2,1,0:T(8,128)(2,1)S(1)} %copy-done.7), channel_id=1, source_target_pairs={{0,3},{2,1},{4,7},{6,5},{8,11},{10,9},{12,15},{14,13},{16,19},{18,... | collective-permute-start | bytes 442376 | tf_op jit(solution)/shard_map/ppermute | solution.py:656
  14.8 17.7 %collective-permute-start.2 = (bf16[8,72,128]{2,1,0:T(8,128)(2,1)S(1)}, bf16[8,72,128]{2,1,0:T(8,128)(2,1)S(1)}, u32[]{:S(2)}, u32[]{:S(2)}) collective-permute-start(bf16[8,72,128]{2,1,0:T(8,128)(2,1)S(1)} %copy-done.6), channel_id=1, source_target_pairs={{0,5},{2,7},{4,1},{6,3},{8,13},{10,15},{12,9},{14,11},{16,21},{18,... | collective-permute-start | bytes 442376 | tf_op jit(solution)/shard_map/ppermute | solution.py:656
  16.1 32.8 %collective-permute-start.3 = (bf16[8,72,128]{2,1,0:T(8,128)(2,1)}, bf16[8,72,128]{2,1,0:T(8,128)(2,1)S(1)}, u32[]{:S(2)}, u32[]{:S(2)}) collective-permute-start(bf16[8,72,128]{2,1,0:T(8,128)(2,1)} %get-tuple-element.40), channel_id=1, source_target_pairs={{0,9},{2,11},{4,13},{6,15},{8,1},{10,3},{12,5},{14,7},{16,25},{18,... | collective-permute-start | bytes 442376 | tf_op jit(solution)/shard_map/ppermute | solution.py:656
  17.4 34.0 %collective-permute-start.4 = (bf16[8,72,128]{2,1,0:T(8,128)(2,1)}, bf16[8,72,128]{2,1,0:T(8,128)(2,1)S(1)}, u32[]{:S(2)}, u32[]{:S(2)}) collective-permute-start(bf16[8,72,128]{2,1,0:T(8,128)(2,1)} %get-tuple-element.41), channel_id=1, source_target_pairs={{0,11},{2,9},{4,15},{6,13},{8,3},{10,1},{12,7},{14,5},{16,27},{18,... | collective-permute-start | bytes 442376 | tf_op jit(solution)/shard_map/ppermute | solution.py:656
  18.7 32.7 %collective-permute-start.5 = (bf16[8,72,128]{2,1,0:T(8,128)(2,1)S(1)}, bf16[8,72,128]{2,1,0:T(8,128)(2,1)S(1)}, u32[]{:S(2)}, u32[]{:S(2)}) collective-permute-start(bf16[8,72,128]{2,1,0:T(8,128)(2,1)S(1)} %copy-done.5), channel_id=1, source_target_pairs={{0,13},{2,15},{4,9},{6,11},{8,5},{10,7},{12,1},{14,3},{16,29},{18,... | collective-permute-start | bytes 442376 | tf_op jit(solution)/shard_map/ppermute | solution.py:656
  22.9 28.5 %collective-permute-start.6 = (bf16[8,72,128]{2,1,0:T(8,128)(2,1)S(1)}, bf16[8,72,128]{2,1,0:T(8,128)(2,1)S(1)}, u32[]{:S(2)}, u32[]{:S(2)}) collective-permute-start(bf16[8,72,128]{2,1,0:T(8,128)(2,1)S(1)} %copy-done.4), channel_id=1, source_target_pairs={{0,15},{2,13},{4,11},{6,9},{8,7},{10,5},{12,3},{14,1},{16,31},{18,... | collective-permute-start | bytes 442376 | tf_op jit(solution)/shard_map/ppermute | solution.py:656
  32.5 18.9 %collective-permute-start.7 = (bf16[8,72,128]{2,1,0:T(8,128)(2,1)S(1)}, bf16[8,72,128]{2,1,0:T(8,128)(2,1)S(1)}, u32[]{:S(2)}, u32[]{:S(2)}) collective-permute-start(bf16[8,72,128]{2,1,0:T(8,128)(2,1)S(1)} %copy-done.3), channel_id=1, source_target_pairs={{0,7},{2,5},{4,3},{6,1},{8,15},{10,13},{12,11},{14,9},{16,23},{18,... | collective-permute-start | bytes 442376 | tf_op jit(solution)/shard_map/ppermute | solution.py:656
  53.6 3.8 %collective-permute-start.8 = (bf16[3,80,128]{2,1,0:T(8,128)(2,1)S(1)}, bf16[3,80,128]{2,1,0:T(8,128)(2,1)S(1)}, u32[]{:S(2)}, u32[]{:S(2)}) collective-permute-start(bf16[3,80,128]{2,1,0:T(8,128)(2,1)S(1)} %get-tuple-element.55), channel_id=1, source_target_pairs={{0,1},{1,2},{2,3},{3,4},{4,5},{5,6},{6,7},{7,8},{8,9},{9,10},{10,1... | collective-permute-start | bytes 184328 | tf_op jit(solution)/shard_map/ppermute | solution.py:639
  53.7 3.7 %collective-permute-start.9 = (bf16[3,80,128]{2,1,0:T(8,128)(2,1)S(1)}, bf16[3,80,128]{2,1,0:T(8,128)(2,1)S(1)}, u32[]{:S(2)}, u32[]{:S(2)}) collective-permute-start(bf16[3,80,128]{2,1,0:T(8,128)(2,1)S(1)} %get-tuple-element.57), channel_id=1, source_target_pairs={{0,15},{1,0},{2,1},{3,2},{4,3},{5,4},{6,5},{7,6},{8,7},{9,8},{10,9... | collective-permute-start | bytes 184328 | tf_op jit(solution)/shard_map/ppermute | solution.py:639
  57.4 6.7 %collective-permute-start.10 = (bf16[3,80,128]{2,1,0:T(8,128)(2,1)S(1)}, bf16[3,80,128]{2,1,0:T(8,128)(2,1)S(1)}, u32[]{:S(2)}, u32[]{:S(2)}) collective-permute-start(bf16[3,80,128]{2,1,0:T(8,128)(2,1)S(1)} %pad_maximum_fusion), channel_id=1, source_target_pairs={{0,3},{1,4},{2,5},{3,6},{4,7},{5,8},{6,9},{7,10},{8,11},{9,12},{10... | collective-permute-start | bytes 184328 | tf_op jit(solution)/shard_map/ppermute | solution.py:639
  60.8 3.9 %collective-permute-start.11 = (bf16[3,80,128]{2,1,0:T(8,128)(2,1)S(1)}, bf16[3,80,128]{2,1,0:T(8,128)(2,1)S(1)}, u32[]{:S(2)}, u32[]{:S(2)}) collective-permute-start(bf16[3,80,128]{2,1,0:T(8,128)(2,1)S(1)} %pad_maximum_fusion), channel_id=1, source_target_pairs={{0,13},{1,14},{2,15},{3,0},{4,1},{5,2},{6,3},{7,4},{8,5},{9,6},{10... | collective-permute-start | bytes 184328 | tf_op jit(solution)/shard_map/ppermute | solution.py:639

commit v3 on v2

--- a/solution.py
+++ b/solution.py
@@ -21,6 +21,9 @@
 SLOTS = GROUPS * CAP
 CHUNK = 96
 MARK = CHANNELS
+BODY = 64
+TAILS = (MARK + 1 - BODY) * CAP
+MESSAGE = CAP * BODY + TAILS
 EPSILON = 1e-05
 VMEM_LIMIT = 40 * 1024 * 1024
 REGRID_VMEM = 60 * 1024 * 1024
@@ -57,7 +60,8 @@
         wide,
         field,
         sums,
-        rounded,
+        message,
+        tails,
         plan,
         plan_scalars,
         plan_sem,
@@ -112,9 +116,8 @@
     plan_copy = pltpu.make_async_copy(plan, plan_scalars, plan_sem)
     plan_copy.start()
 
-    tail = PADDED - 8
     for slot in range(SLOTS):
-        rounded[slot, tail:] = jnp.full((8, BLOCK), ROWS, jnp.bfloat16)
+        tails[pl.ds(slot * 8, 8), :] = jnp.full((8, BLOCK), ROWS, jnp.float32)
     wide[pl.ds(CHANNELS * ROWS, (PADDED - CHANNELS) * ROWS), :] = jnp.zeros(
         ((PADDED - CHANNELS) * ROWS, BLOCK), jnp.float32
     )
@@ -124,7 +127,7 @@
     for row in range(ROWS):
         block = wide[pl.ds(row, PADDED, stride=ROWS), :]
         field[row] = jnp.concatenate([block, nothing], axis=0).astype(jnp.bfloat16)
-    is_mark = lax.broadcasted_iota(jnp.int32, (8, BLOCK), 0) == MARK - tail
+    is_mark = lax.broadcasted_iota(jnp.int32, (8, BLOCK), 0) == MARK - BODY
     blank = jnp.zeros((WIDE, BLOCK), jnp.bfloat16)
     small_copies[1].wait()
     small_copies[2].wait()
@@ -147,25 +150,31 @@
                 product = products[at * WIDE : at * WIDE + PADDED]
                 total = jnp.where(code >= SLOTS, 0.0, sums[slot]) + product
                 sums[slot] = total
-                marked = jnp.where(is_mark, row.astype(jnp.float32), total[tail:])
-                rounded[slot] = jnp.concatenate([total[:tail], marked], axis=0).astype(jnp.bfloat16)
+                group, place = split(slot, CAP)
+                message[group, pl.ds(pl.multiple_of(place * BODY, BODY), BODY), :] = total[
+                    :BODY
+                ].astype(jnp.bfloat16)
+                tails[pl.ds(pl.multiple_of(slot * 8, 8), 8), :] = jnp.where(
+                    is_mark, row.astype(jnp.float32), total[BODY:]
+                )
     copies = []
     for group in range(GROUPS):
-        part = rounded.at[pl.ds(group * CAP, CAP)]
+        start = group * CAP * 8
+        ends = [tails[pl.ds(start + at, CAP, stride=8), :] for at in range(MARK + 1 - BODY)]
+        message[group, CAP * BODY :] = jnp.concatenate(ends, axis=0).astype(jnp.bfloat16)
         if group < TILE_COLS:
-            out = same_out.at[pl.ds(group * CAP, CAP)]
+            out = same_out.at[pl.ds(group * MESSAGE, MESSAGE)]
         else:
             out = next_outs[group - TILE_COLS]
-        copies.append(pltpu.make_async_copy(part, out, out_sems.at[group]))
-    for copy in copies:
-        copy.start()
+        copies.append(pltpu.make_async_copy(message.at[group], out, out_sems.at[group]))
+        copies[-1].start()
     for copy in copies:
         copy.wait()
 
 
 def regrid(target, source_index, field, weights, column_rows):
-    piece = jax.ShapeDtypeStruct((CAP, PADDED, BLOCK), jnp.bfloat16)
-    same = jax.ShapeDtypeStruct((TILE_COLS * CAP, PADDED, BLOCK), jnp.bfloat16)
+    piece = jax.ShapeDtypeStruct((MESSAGE, BLOCK), jnp.bfloat16)
+    same = jax.ShapeDtypeStruct((TILE_COLS * MESSAGE, BLOCK), jnp.bfloat16)
     hbm = pl.BlockSpec(memory_space=pl.ANY)
     entries = weights.shape[0]
     return pl.pallas_call(
@@ -182,7 +191,8 @@
             pltpu.VMEM((PADDED * ROWS, BLOCK), jnp.float32),
             pltpu.VMEM((ROWS, WIDE, BLOCK), jnp.bfloat16),
             pltpu.VMEM((SLOTS, PADDED, BLOCK), jnp.float32),
-            pltpu.VMEM((SLOTS, PADDED, BLOCK), jnp.bfloat16),
+            pltpu.VMEM((GROUPS, MESSAGE, BLOCK), jnp.bfloat16),
+            pltpu.VMEM((SLOTS * 8, BLOCK), jnp.float32),
             pltpu.VMEM((1, entries), jnp.int32),
             pltpu.SMEM((1, entries), jnp.int32),
             pltpu.SemaphoreType.DMA,
@@ -204,22 +214,30 @@
         downward,
         strip_out,
         summed,
+        tails,
     ) = rest[TILE_COLS:]
     position = lax.rem(lax.axis_index("tile"), column_rows)
     summed[...] = jnp.zeros_like(summed)
 
-    def add(piece):
-        row = piece[MARK : MARK + 1].astype(jnp.float32).astype(jnp.int32)[0, 0]
-        summed[row] = summed[row] + piece[...].astype(jnp.float32)
-
-    for slot in range(SLOTS // 2):
-        add(same.at[slot])
+    def add(group, piece):
+        ends = piece[CAP * BODY :].astype(jnp.float32)
+        tails[group, :TAILS] = ends
+        rows = ends[TAILS - CAP :].astype(jnp.int32)
+        for place in range(CAP):
+            row = rows[place, 0]
+            body = piece[place * BODY : (place + 1) * BODY].astype(jnp.float32)
+            summed[row, :BODY] = summed[row, :BODY] + body
+            tail = tails[group, pl.ds(place, 8, stride=CAP), :]
+            summed[row, BODY:] = summed[row, BODY:] + tail
+
+    tails[:, TAILS:] = jnp.zeros((GROUPS, 8 * CAP - TAILS, BLOCK), jnp.float32)
+    for group in range(TILE_COLS):
+        add(group, same.at[pl.ds(group * MESSAGE, MESSAGE)])
 
     @pl.when(position > 0)
     def _():
         for group in range(TILE_COLS):
-            for place in range(CAP):
-                add(nexts[group].at[place])
+            add(TILE_COLS + group, nexts[group])
 
     gain = gain_ref[...]
     channel = lax.broadcasted_iota(jnp.int32, (PADDED, BLOCK), 0)
@@ -268,6 +286,7 @@
         out_shape=[GRIDDED, FIELD, RIM, RIM, STRIP],
         scratch_shapes=[
             pltpu.VMEM((ROWS + 1, PADDED, BLOCK), jnp.float32),
+            pltpu.VMEM((GROUPS, 8 * CAP, BLOCK), jnp.float32),
         ],
         compiler_params=pltpu.CompilerParams(vmem_limit_bytes=VMEM_LIMIT),
         name="gather_rows",

time: 69 us -> 67.9 us (0.984)
  waiting for transfers between devices: 30.1 us -> 29.1 us
    ppermute x8, waiting for transfers between devices: 28.1 us -> 27.1 us  [per_device(): nexts[across] = lax.ppermute(nexts[across], 'tile', pairs)]
where the time goes in v3:
time: 67.9 us; the launch traced here: 67.1 us
  waiting for transfers between devices  29.1 us (43%)
  starting transfers between devices  21.9 us (32%)
  Pallas kernels  14.4 us (21%)
  between operations  1 us (1%)
  local copies, waits for them, and re-layouts  0.72 us (1%)
    ppermute x8, waiting for transfers between devices, per_device(): nexts[across] = lax.ppermute(nexts[across], 'tile', pairs)  27.1 us
    ppermute x8, starting transfers between devices, per_device(): nexts[across] = lax.ppermute(nexts[across], 'tile', pairs)  10.3 us
    all_to_all x1, starting transfers between devices, per_device(): lax.all_to_all(same, 'tile', 0, 0, axis_index_groups=[[c * column_rows +...  6.52 us
    ppermute x4, starting transfers between devices, from_shift(): lax.ppermute(value, 'tile', [(i, (i - shift) % count) for i in range(coun...  5.05 us
    pallas_call x1, Pallas kernels, regrid(): pl.pallas_call(functools.partial(regrid_kernel, column_rows), in_specs=[h...  4.99 us
    pallas_call x1, Pallas kernels, convolutions(): pl.pallas_call(functools.partial(conv_kernel, column_rows), in_specs=[vme...  3.5 us
    pallas_call x1, Pallas kernels, channels_first(): pl.pallas_call(turn_kernel, in_specs=[vmem()], out_specs=vmem(), out_shap...  1.98 us
    pallas_call x1, Pallas kernels, gather_rows(): pl.pallas_call(functools.partial(gather_kernel, column_rows), in_specs=[s...  1.98 us
  transfers between devices with their start and end apart: 13, of which 6 were waited for; matrix products, arithmetic and copies ran while one was open for 1% of the time, Pallas kernels for 6%

profile of v3, /device:TPU:1, one launch (start us, length us, event | category | flops | bytes accessed | tf_op | source)
XLA Modules:
  0.0 67.1 jit_solution(84854493557509566)
XLA Ops:
  0.6 5.0 %regrid.1 = (bf16[4480,128]{1,0:T(8,128)(2,1)}, bf16[560,128]{1,0:T(8,128)(2,1)}, bf16[560,128]{1,0:T(8,128)(2,1)}, bf16[560,128]{1,0:T(8,128)(2,1)}, bf16[560,1...) custom-call(s32[96]{0:T(128)} %target_hbm.1, ...), custom_call_target="tpu_custom_call" | custom-call | tf_op jit(solution)/shard_map/regrid/pallas_call | solution.py:180
  5.6 0.0 copy-start.9
  5.6 0.0 copy-start.8
  5.6 0.0 copy-start.7
  5.7 0.0 copy-start.6
  5.7 0.0 copy-start.5
  5.7 0.0 copy-start.1
  5.7 0.0 copy-start.2
  5.7 6.5 %all-to-all-start = ((bf16[8,560,128]{2,1,0:T(8,128)(2,1)}), bf16[8,560,128]{2,1,0:T(8,128)(2,1)S(1)}, u32[]{:S(2)}, u32[]{:S(2)}) async-start(bf16[8,560,128]{2,1,0:T(8,128)(2,1)} %bitcast.29), calls=%async_computation | async-start | bytes 2293760 | tf_op jit(solution)/shard_map/all_to_all | solution.py:677
  12.3 0.0 copy-done.9
  12.3 1.3 %collective-permute-start = (bf16[560,128]{1,0:T(8,128)(2,1)S(1)}, bf16[560,128]{1,0:T(8,128)(2,1)S(1)}, u32[]{:S(2)}, u32[]{:S(2)}) collective-permute-start(bf16[560,128]{1,0:T(8,128)(2,1)S(1)} %copy-done.9), channel_id=1, source_target_pairs={{0,1},{2,3},{4,5},{6,7},{8,9},{10,11},{12,13},{14,15},{16,17},{18,... | collective-permute-start | bytes 430088 | tf_op jit(solution)/shard_map/ppermute | solution.py:675
  13.6 0.0 copy-done.8
  13.6 0.0 copy-start
  13.6 1.3 %collective-permute-start.1 = (bf16[560,128]{1,0:T(8,128)(2,1)S(1)}, bf16[560,128]{1,0:T(8,128)(2,1)S(1)}, u32[]{:S(2)}, u32[]{:S(2)}) collective-permute-start(bf16[560,128]{1,0:T(8,128)(2,1)S(1)} %copy-done.8), channel_id=1, source_target_pairs={{0,3},{2,1},{4,7},{6,5},{8,11},{10,9},{12,15},{14,13},{16,19},{18,... | collective-permute-start | bytes 430088 | tf_op jit(solution)/shard_map/ppermute | solution.py:675
  14.9 1.3 %collective-permute-start.2 = (bf16[560,128]{1,0:T(8,128)(2,1)S(1)}, bf16[560,128]{1,0:T(8,128)(2,1)S(1)}, u32[]{:S(2)}, u32[]{:S(2)}) collective-permute-start(bf16[560,128]{1,0:T(8,128)(2,1)S(1)} %copy-done.7), channel_id=1, source_target_pairs={{0,5},{2,7},{4,1},{6,3},{8,13},{10,15},{12,9},{14,11},{16,21},{18,... | collective-permute-start | bytes 430088 | tf_op jit(solution)/shard_map/ppermute | solution.py:675
  16.2 1.3 %collective-permute-start.3 = (bf16[560,128]{1,0:T(8,128)(2,1)}, bf16[560,128]{1,0:T(8,128)(2,1)S(1)}, u32[]{:S(2)}, u32[]{:S(2)}) collective-permute-start(bf16[560,128]{1,0:T(8,128)(2,1)} %get-tuple-element.40), channel_id=1, source_target_pairs={{0,9},{2,11},{4,13},{6,15},{8,1},{10,3},{12,5},{14,7},{16,25},{18,... | collective-permute-start | bytes 430088 | tf_op jit(solution)/shard_map/ppermute | solution.py:675
  17.5 1.3 %collective-permute-start.4 = (bf16[560,128]{1,0:T(8,128)(2,1)S(1)}, bf16[560,128]{1,0:T(8,128)(2,1)S(1)}, u32[]{:S(2)}, u32[]{:S(2)}) collective-permute-start(bf16[560,128]{1,0:T(8,128)(2,1)S(1)} %copy-done.6), channel_id=1, source_target_pairs={{0,11},{2,9},{4,15},{6,13},{8,3},{10,1},{12,7},{14,5},{16,27},{18,... | collective-permute-start | bytes 430088 | tf_op jit(solution)/shard_map/ppermute | solution.py:675
  18.8 0.0 collective-permute-done.rest_0_
  18.8 1.3 %collective-permute-start.5 = (bf16[560,128]{1,0:T(8,128)(2,1)S(1)}, bf16[560,128]{1,0:T(8,128)(2,1)S(1)}, u32[]{:S(2)}, u32[]{:S(2)}) collective-permute-start(bf16[560,128]{1,0:T(8,128)(2,1)S(1)} %copy-done.5), channel_id=1, source_target_pairs={{0,13},{2,15},{4,9},{6,11},{8,5},{10,7},{12,1},{14,3},{16,29},{18,... | collective-permute-start | bytes 430088 | tf_op jit(solution)/shard_map/ppermute | solution.py:675
  20.1 2.7 %collective-permute-done.1.rest_1_ = bf16[560,128]{1,0:T(8,128)(2,1)S(1)} collective-permute-done((bf16[560,128]{1,0:T(8,128)(2,1)S(1)}, bf16[560,128]{1,0:T(8,128)(2,1)S(1)}, u32[]{:S(2)}, u32[]{:S(2)}) %collective-permute-start.1) | collective-permute-done | bytes 143392 | tf_op jit(solution)/shard_map/ppermute | solution.py:675
  22.8 1.3 %collective-permute-start.6 = (bf16[560,128]{1,0:T(8,128)(2,1)S(1)}, bf16[560,128]{1,0:T(8,128)(2,1)S(1)}, u32[]{:S(2)}, u32[]{:S(2)}) collective-permute-start(bf16[560,128]{1,0:T(8,128)(2,1)S(1)} %copy-done.4), channel_id=1, source_target_pairs={{0,15},{2,13},{4,11},{6,9},{8,7},{10,5},{12,3},{14,1},{16,31},{18,... | collective-permute-start | bytes 430088 | tf_op jit(solution)/shard_map/ppermute | solution.py:675
  24.1 8.0 %collective-permute-done.2.rest_2_ = bf16[560,128]{1,0:T(8,128)(2,1)S(1)} collective-permute-done((bf16[560,128]{1,0:T(8,128)(2,1)S(1)}, bf16[560,128]{1,0:T(8,128)(2,1)S(1)}, u32[]{:S(2)}, u32[]{:S(2)}) %collective-permute-start.2) | collective-permute-done | bytes 143392 | tf_op jit(solution)/shard_map/ppermute | solution.py:675
  32.1 1.3 %collective-permute-start.7 = (bf16[560,128]{1,0:T(8,128)(2,1)S(1)}, bf16[560,128]{1,0:T(8,128)(2,1)S(1)}, u32[]{:S(2)}, u32[]{:S(2)}) collective-permute-start(bf16[560,128]{1,0:T(8,128)(2,1)S(1)} %copy-done.3), channel_id=1, source_target_pairs={{0,7},{2,5},{4,3},{6,1},{8,15},{10,13},{12,11},{14,9},{16,23},{18,... | collective-permute-start | bytes 430088 | tf_op jit(solution)/shard_map/ppermute | solution.py:675
  33.5 0.1 copy.17
  33.6 0.2 reshape.38.taps_ref.first_taps_ref
  33.7 0.0 copy-done.2
  33.8 0.1 copy.16
  33.9 0.2 reshape.40.taps_ref.second_taps_ref
  34.1 14.0 %collective-permute-done.3.rest_3_ = bf16[560,128]{1,0:T(8,128)(2,1)S(1)} collective-permute-done((bf16[560,128]{1,0:T(8,128)(2,1)}, bf16[560,128]{1,0:T(8,128)(2,1)S(1)}, u32[]{:S(2)}, u32[]{:S(2)}) %collective-permute-start.3) | collective-permute-done | bytes 143392 | tf_op jit(solution)/shard_map/ppermute | solution.py:675
  48.1 2.4 %collective-permute-done.4.rest_4_ = bf16[560,128]{1,0:T(8,128)(2,1)S(1)} collective-permute-done((bf16[560,128]{1,0:T(8,128)(2,1)S(1)}, bf16[560,128]{1,0:T(8,128)(2,1)S(1)}, u32[]{:S(2)}, u32[]{:S(2)}) %collective-permute-start.4) | collective-permute-done | bytes 143392 | tf_op jit(solution)/shard_map/ppermute | solution.py:675
  50.5 0.0 collective-permute-done.5.rest_5_
  50.5 0.0 collective-permute-done.6.rest_6_
  50.5 0.0 collective-permute-done.7.rest_7_
  50.5 0.0 all-to-all-done
  50.5 0.1 broadcast_in_dim.12.gain_ref
  50.6 2.0 %gather_rows.1 = (bf16[32,72,128]{2,1,0:T(8,128)(2,1)S(1)}, bf16[32,80,128]{2,1,0:T(8,128)(2,1)S(1)}, bf16[3,80,128]{2,1,0:T(8,128)(2,1)S(1)}, bf16[3,80,128]{2,1,0:T(8,128)(2,1)S(1)}, bf16[80,128]{1,0:T(8,128)(2,1)S(1)}) custom-call(s32[1,2]{1,0:T(1,128)S(1)} %copy-done, f32[72,128]{1,0:T(8,128)S(1)} %broadcast_in_dim.12.gain_ref, ...), custom_call_target="tpu_custom_call" | custom-call | tf_op jit(solution)/shard_map/gather_rows/pallas_call | solution.py:282
  52.6 0.1 collective-permute-start.8
  52.6 0.5 collective-permute-start.9
  53.1 2.0 %channels_first.1 = bf16[2208,128]{1,0:T(8,128)(2,1)} custom-call(bf16[32,72,128]{2,1,0:T(8,128)(2,1)S(1)} %get-tuple-element.63.field.gridded), custom_call_target="tpu_custom_call" | custom-call | tf_op jit(solution)/shard_map/channels_first/pallas_call | solution.py:303
  55.1 1.2 %inner_convolution.1 = (bf16[32,80,128]{2,1,0:T(8,128)(2,1)S(1)}, f32[2,80,128]{2,1,0:T(8,128)S(1)}, f32[2,80,128]{2,1,0:T(8,128)S(1)}) custom-call(bf16[240,240]{1,0:T(8,128)(2,1)S(1)} %reshape.38.taps_ref.first_taps_ref, bf16[32,80,128]{2,1,0:T(8,128)(2,1)S(1)} %get-tuple-element.59.field), custom_call_target="tpu_custom_call" | custom-call | flops 471859200 | bytes 2097152 | tf_op jit(solution)/shard_map/inner_convolution/pallas_call | solution.py:369
  56.4 0.0 collective-permute-done.8.above
  56.4 0.0 collective-permute-done.9.below
  56.4 3.3 %collective-permute-start.10 = (bf16[3,80,128]{2,1,0:T(8,128)(2,1)S(1)}, bf16[3,80,128]{2,1,0:T(8,128)(2,1)S(1)}, u32[]{:S(2)}, u32[]{:S(2)}) collective-permute-start(bf16[3,80,128]{2,1,0:T(8,128)(2,1)S(1)} %pad_maximum_fusion), channel_id=1, source_target_pairs={{0,3},{1,4},{2,5},{3,6},{4,7},{5,8},{6,9},{7,10},{8,11},{9,12},{10... | collective-permute-start | bytes 184328 | tf_op jit(solution)/shard_map/ppermute | solution.py:658
  59.7 1.2 %collective-permute-start.11 = (bf16[3,80,128]{2,1,0:T(8,128)(2,1)S(1)}, bf16[3,80,128]{2,1,0:T(8,128)(2,1)S(1)}, u32[]{:S(2)}, u32[]{:S(2)}) collective-permute-start(bf16[3,80,128]{2,1,0:T(8,128)(2,1)S(1)} %pad_maximum_fusion), channel_id=1, source_target_pairs={{0,13},{1,14},{2,15},{3,0},{4,1},{5,2},{6,3},{7,4},{8,5},{9,6},{10... | collective-permute-start | bytes 184328 | tf_op jit(solution)/shard_map/ppermute | solution.py:658
  60.9 0.8 %inner_second_convolution.1.base = f32[32,72,128]{2,1,0:T(8,128)S(1)} custom-call(bf16[240,240]{1,0:T(8,128)(2,1)S(1)} %reshape.40.taps_ref.second_taps_ref, bf16[32,80,128]{2,1,0:T(8,128)(2,1)S(1)} %get-tuple-element.66.hidden, bf16[32,72,128]{2,1,0:T(8,128)(2,1)S(1)} %get-tuple-element.63.field.gridded), custom_call_target="tpu_custom_call" | custom-call | flops 471859200 | bytes 2097152 | tf_op jit(solution)/shard_map/inner_second_convolution/pallas_call | solution.py:402
  61.7 1.4 %collective-permute-done.10.rest_0_ = bf16[3,80,128]{2,1,0:T(8,128)(2,1)S(1)} collective-permute-done((bf16[3,80,128]{2,1,0:T(8,128)(2,1)S(1)}, bf16[3,80,128]{2,1,0:T(8,128)(2,1)S(1)}, u32[]{:S(2)}, u32[]{:S(2)}) %collective-permute-start.10) | collective-permute-done | bytes 61472 | tf_op jit(solution)/shard_map/ppermute | solution.py:658
  63.1 0.6 collective-permute-done.11.rest_1_
  63.6 3.5 %convolutions.1 = bf16[2208,128]{1,0:T(8,128)(2,1)} custom-call(bf16[240,240]{1,0:T(8,128)(2,1)S(1)} %reshape.38.taps_ref.first_taps_ref, bf16[240,240]{1,0:T(8,128)(2,1)S(1)} %reshape.40.taps_ref.second_taps_ref, bf16[32,80,128]{2,1,0:T(8,128)(2,1)S(1)} %get-tuple-element.59.field, f32[32,72,128]{2,1,0:T(8,128)S(1)} %inner_second_convolution.1.base, ...), custom_call_target="tpu_custom_call" | custom-call | tf_op jit(solution)/shard_map/convolutions/pallas_call | solution.py:637
  (17 shorter events, 0.1 us)
Async XLA Ops:
  5.6 6.6 %copy-start.9 = (bf16[560,128]{1,0:T(8,128)(2,1)S(1)}, bf16[560,128]{1,0:T(8,128)(2,1)}, u32[]{:S(2)}) copy-start(bf16[560,128]{1,0:T(8,128)(2,1)} %get-tuple-element.37) | copy-start | bytes 430084
  5.6 7.9 %copy-start.8 = (bf16[560,128]{1,0:T(8,128)(2,1)S(1)}, bf16[560,128]{1,0:T(8,128)(2,1)}, u32[]{:S(2)}) copy-start(bf16[560,128]{1,0:T(8,128)(2,1)} %get-tuple-element.38) | copy-start | bytes 430084
  5.6 9.2 %copy-start.7 = (bf16[560,128]{1,0:T(8,128)(2,1)S(1)}, bf16[560,128]{1,0:T(8,128)(2,1)}, u32[]{:S(2)}) copy-start(bf16[560,128]{1,0:T(8,128)(2,1)} %get-tuple-element.39) | copy-start | bytes 430084
  5.7 11.8 %copy-start.6 = (bf16[560,128]{1,0:T(8,128)(2,1)S(1)}, bf16[560,128]{1,0:T(8,128)(2,1)}, u32[]{:S(2)}) copy-start(bf16[560,128]{1,0:T(8,128)(2,1)} %get-tuple-element.41) | copy-start | bytes 430084
  5.7 13.1 %copy-start.5 = (bf16[560,128]{1,0:T(8,128)(2,1)S(1)}, bf16[560,128]{1,0:T(8,128)(2,1)}, u32[]{:S(2)}) copy-start(bf16[560,128]{1,0:T(8,128)(2,1)} %get-tuple-element.42) | copy-start | bytes 430084
  5.7 17.1 %copy-start.4 = (bf16[560,128]{1,0:T(8,128)(2,1)S(1)}, bf16[560,128]{1,0:T(8,128)(2,1)}, u32[]{:S(2)}) copy-start(bf16[560,128]{1,0:T(8,128)(2,1)} %get-tuple-element.43) | copy-start | bytes 430084
  5.7 26.4 %copy-start.3 = (bf16[560,128]{1,0:T(8,128)(2,1)S(1)}, bf16[560,128]{1,0:T(8,128)(2,1)}, u32[]{:S(2)}) copy-start(bf16[560,128]{1,0:T(8,128)(2,1)} %get-tuple-element.44) | copy-start | bytes 430084
  5.7 27.7 %copy-start.1 = (bf16[9,69,69]{2,1,0:T(8,128)(2,1)S(1)}, bf16[9,69,69]{2,1,0:T(8,128)(2,1)}, u32[]{:S(2)}) copy-start(bf16[9,69,69]{2,1,0:T(8,128)(2,1)} %param.14) | copy-start | bytes 257098
  5.7 28.0 %copy-start.2 = (bf16[9,69,69]{2,1,0:T(8,128)(2,1)S(1)}, bf16[9,69,69]{2,1,0:T(8,128)(2,1)}, u32[]{:S(2)}) copy-start(bf16[9,69,69]{2,1,0:T(8,128)(2,1)} %param.15) | copy-start | bytes 257098
  5.7 44.8 %all-to-all-start = ((bf16[8,560,128]{2,1,0:T(8,128)(2,1)}), bf16[8,560,128]{2,1,0:T(8,128)(2,1)S(1)}, u32[]{:S(2)}, u32[]{:S(2)}) async-start(bf16[8,560,128]{2,1,0:T(8,128)(2,1)} %bitcast.29), calls=%async_computation | async-start | bytes 2293760 | tf_op jit(solution)/shard_map/all_to_all | solution.py:677
  12.2 21.8 %copy-start.10 = (f32[69]{0:T(128)S(1)}, f32[69]{0:T(128)}, u32[]{:S(2)}) copy-start(f32[69]{0:T(128)} %param.13) | copy-start | bytes 832
  12.3 6.5 %collective-permute-start = (bf16[560,128]{1,0:T(8,128)(2,1)S(1)}, bf16[560,128]{1,0:T(8,128)(2,1)S(1)}, u32[]{:S(2)}, u32[]{:S(2)}) collective-permute-start(bf16[560,128]{1,0:T(8,128)(2,1)S(1)} %copy-done.9), channel_id=1, source_target_pairs={{0,1},{2,3},{4,5},{6,7},{8,9},{10,11},{12,13},{14,15},{16,17},{18,... | collective-permute-start | bytes 430088 | tf_op jit(solution)/shard_map/ppermute | solution.py:675
  13.6 37.0 %copy-start = (s32[1,2]{1,0:T(1,128)S(1)}, s32[1,2]{1,0:T(1,128)}, u32[]{:S(2)}) copy-start(s32[1,2]{1,0:T(1,128)} %flip_ref.1) | copy-start | bytes 28
  13.6 9.2 %collective-permute-start.1 = (bf16[560,128]{1,0:T(8,128)(2,1)S(1)}, bf16[560,128]{1,0:T(8,128)(2,1)S(1)}, u32[]{:S(2)}, u32[]{:S(2)}) collective-permute-start(bf16[560,128]{1,0:T(8,128)(2,1)S(1)} %copy-done.8), channel_id=1, source_target_pairs={{0,3},{2,1},{4,7},{6,5},{8,11},{10,9},{12,15},{14,13},{16,19},{18,... | collective-permute-start | bytes 430088 | tf_op jit(solution)/shard_map/ppermute | solution.py:675
  14.9 17.2 %collective-permute-start.2 = (bf16[560,128]{1,0:T(8,128)(2,1)S(1)}, bf16[560,128]{1,0:T(8,128)(2,1)S(1)}, u32[]{:S(2)}, u32[]{:S(2)}) collective-permute-start(bf16[560,128]{1,0:T(8,128)(2,1)S(1)} %copy-done.7), channel_id=1, source_target_pairs={{0,5},{2,7},{4,1},{6,3},{8,13},{10,15},{12,9},{14,11},{16,21},{18,... | collective-permute-start | bytes 430088 | tf_op jit(solution)/shard_map/ppermute | solution.py:675
  16.2 31.9 %collective-permute-start.3 = (bf16[560,128]{1,0:T(8,128)(2,1)}, bf16[560,128]{1,0:T(8,128)(2,1)S(1)}, u32[]{:S(2)}, u32[]{:S(2)}) collective-permute-start(bf16[560,128]{1,0:T(8,128)(2,1)} %get-tuple-element.40), channel_id=1, source_target_pairs={{0,9},{2,11},{4,13},{6,15},{8,1},{10,3},{12,5},{14,7},{16,25},{18,... | collective-permute-start | bytes 430088 | tf_op jit(solution)/shard_map/ppermute | solution.py:675
  17.5 33.0 %collective-permute-start.4 = (bf16[560,128]{1,0:T(8,128)(2,1)S(1)}, bf16[560,128]{1,0:T(8,128)(2,1)S(1)}, u32[]{:S(2)}, u32[]{:S(2)}) collective-permute-start(bf16[560,128]{1,0:T(8,128)(2,1)S(1)} %copy-done.6), channel_id=1, source_target_pairs={{0,11},{2,9},{4,15},{6,13},{8,3},{10,1},{12,7},{14,5},{16,27},{18,... | collective-permute-start | bytes 430088 | tf_op jit(solution)/shard_map/ppermute | solution.py:675
  18.8 31.7 %collective-permute-start.5 = (bf16[560,128]{1,0:T(8,128)(2,1)S(1)}, bf16[560,128]{1,0:T(8,128)(2,1)S(1)}, u32[]{:S(2)}, u32[]{:S(2)}) collective-permute-start(bf16[560,128]{1,0:T(8,128)(2,1)S(1)} %copy-done.5), channel_id=1, source_target_pairs={{0,13},{2,15},{4,9},{6,11},{8,5},{10,7},{12,1},{14,3},{16,29},{18,... | collective-permute-start | bytes 430088 | tf_op jit(solution)/shard_map/ppermute | solution.py:675
  22.8 27.7 %collective-permute-start.6 = (bf16[560,128]{1,0:T(8,128)(2,1)S(1)}, bf16[560,128]{1,0:T(8,128)(2,1)S(1)}, u32[]{:S(2)}, u32[]{:S(2)}) collective-permute-start(bf16[560,128]{1,0:T(8,128)(2,1)S(1)} %copy-done.4), channel_id=1, source_target_pairs={{0,15},{2,13},{4,11},{6,9},{8,7},{10,5},{12,3},{14,1},{16,31},{18,... | collective-permute-start | bytes 430088 | tf_op jit(solution)/shard_map/ppermute | solution.py:675
  32.1 18.4 %collective-permute-start.7 = (bf16[560,128]{1,0:T(8,128)(2,1)S(1)}, bf16[560,128]{1,0:T(8,128)(2,1)S(1)}, u32[]{:S(2)}, u32[]{:S(2)}) collective-permute-start(bf16[560,128]{1,0:T(8,128)(2,1)S(1)} %copy-done.3), channel_id=1, source_target_pairs={{0,7},{2,5},{4,3},{6,1},{8,15},{10,13},{12,11},{14,9},{16,23},{18,... | collective-permute-start | bytes 430088 | tf_op jit(solution)/shard_map/ppermute | solution.py:675
  52.6 3.8 %collective-permute-start.8 = (bf16[3,80,128]{2,1,0:T(8,128)(2,1)S(1)}, bf16[3,80,128]{2,1,0:T(8,128)(2,1)S(1)}, u32[]{:S(2)}, u32[]{:S(2)}) collective-permute-start(bf16[3,80,128]{2,1,0:T(8,128)(2,1)S(1)} %get-tuple-element.55), channel_id=1, source_target_pairs={{0,1},{1,2},{2,3},{3,4},{4,5},{5,6},{6,7},{7,8},{8,9},{9,10},{10,1... | collective-permute-start | bytes 184328 | tf_op jit(solution)/shard_map/ppermute | solution.py:658
  52.6 3.7 %collective-permute-start.9 = (bf16[3,80,128]{2,1,0:T(8,128)(2,1)S(1)}, bf16[3,80,128]{2,1,0:T(8,128)(2,1)S(1)}, u32[]{:S(2)}, u32[]{:S(2)}) collective-permute-start(bf16[3,80,128]{2,1,0:T(8,128)(2,1)S(1)} %get-tuple-element.57), channel_id=1, source_target_pairs={{0,15},{1,0},{2,1},{3,2},{4,3},{5,4},{6,5},{7,6},{8,7},{9,8},{10,9... | collective-permute-start | bytes 184328 | tf_op jit(solution)/shard_map/ppermute | solution.py:658
  56.4 6.6 %collective-permute-start.10 = (bf16[3,80,128]{2,1,0:T(8,128)(2,1)S(1)}, bf16[3,80,128]{2,1,0:T(8,128)(2,1)S(1)}, u32[]{:S(2)}, u32[]{:S(2)}) collective-permute-start(bf16[3,80,128]{2,1,0:T(8,128)(2,1)S(1)} %pad_maximum_fusion), channel_id=1, source_target_pairs={{0,3},{1,4},{2,5},{3,6},{4,7},{5,8},{6,9},{7,10},{8,11},{9,12},{10... | collective-permute-start | bytes 184328 | tf_op jit(solution)/shard_map/ppermute | solution.py:658
  59.7 3.9 %collective-permute-start.11 = (bf16[3,80,128]{2,1,0:T(8,128)(2,1)S(1)}, bf16[3,80,128]{2,1,0:T(8,128)(2,1)S(1)}, u32[]{:S(2)}, u32[]{:S(2)}) collective-permute-start(bf16[3,80,128]{2,1,0:T(8,128)(2,1)S(1)} %pad_maximum_fusion), channel_id=1, source_target_pairs={{0,13},{1,14},{2,15},{3,0},{4,1},{5,2},{6,3},{7,4},{8,5},{9,6},{10... | collective-permute-start | bytes 184328 | tf_op jit(solution)/shard_map/ppermute | solution.py:658

commit v4 on v3

--- a/solution.py
+++ b/solution.py
@@ -13,13 +13,14 @@
 WIDE = 80
 ROWS = 32
 ROW_BITS = 5
+HALF_ROWS = ROWS // 2
 TILE_COLS = 8
 CAP = 8
 HALF = TILE_COLS // 2
 GROUPS = 2 * TILE_COLS
 COLUMN_ORDER = [half * HALF + at for at in range(HALF) for half in range(2)]
 SLOTS = GROUPS * CAP
-CHUNK = 96
+CHUNK = 16
 MARK = CHANNELS
 BODY = 64
 TAILS = (MARK + 1 - BODY) * CAP
@@ -135,28 +136,28 @@
 
     for chunk in range(chunks):
         chunk_copy(chunk).wait()
-        for entry in range(chunk * CHUNK, (chunk + 1) * CHUNK, 2):
-            one = jnp.concatenate([field[index_ref[entry]], blank], axis=1)
-            two = jnp.concatenate([blank, field[index_ref[entry + 1]]], axis=1)
-            products = jnp.dot(
-                jnp.concatenate([one, two], axis=0),
-                weight[entry : entry + 2].reshape(2 * BLOCK, BLOCK),
-                preferred_element_type=jnp.float32,
+    for entry in range(0, entries, 2):
+        one = jnp.concatenate([field[index_ref[entry]], blank], axis=1)
+        two = jnp.concatenate([blank, field[index_ref[entry + 1]]], axis=1)
+        products = jnp.dot(
+            jnp.concatenate([one, two], axis=0),
+            weight[entry : entry + 2].reshape(2 * BLOCK, BLOCK),
+            preferred_element_type=jnp.float32,
+        )
+        for at in range(2):
+            code = plan_scalars[0, entry + at]
+            slot = code & (SLOTS - 1)
+            row = split(target_ref[entry + at], ROWS)[1]
+            product = products[at * WIDE : at * WIDE + PADDED]
+            total = jnp.where(code >= SLOTS, 0.0, sums[slot]) + product
+            sums[slot] = total
+            group, place = split(slot, CAP)
+            message[group, pl.ds(pl.multiple_of(place * BODY, BODY), BODY), :] = total[
+                :BODY
+            ].astype(jnp.bfloat16)
+            tails[pl.ds(pl.multiple_of(slot * 8, 8), 8), :] = jnp.where(
+                is_mark, row.astype(jnp.float32), total[BODY:]
             )
-            for at in range(2):
-                code = plan_scalars[0, entry + at]
-                slot = code & (SLOTS - 1)
-                row = split(target_ref[entry + at], ROWS)[1]
-                product = products[at * WIDE : at * WIDE + PADDED]
-                total = jnp.where(code >= SLOTS, 0.0, sums[slot]) + product
-                sums[slot] = total
-                group, place = split(slot, CAP)
-                message[group, pl.ds(pl.multiple_of(place * BODY, BODY), BODY), :] = total[
-                    :BODY
-                ].astype(jnp.bfloat16)
-                tails[pl.ds(pl.multiple_of(slot * 8, 8), 8), :] = jnp.where(
-                    is_mark, row.astype(jnp.float32), total[BODY:]
-                )
     copies = []
     for group in range(GROUPS):
         start = group * CAP * 8
@@ -240,7 +241,7 @@
             add(TILE_COLS + group, nexts[group])
 
     gain = gain_ref[...]
-    channel = lax.broadcasted_iota(jnp.int32, (PADDED, BLOCK), 0)
+    real = lax.broadcasted_iota(jnp.int32, (PADDED - BODY, BLOCK), 0) < CHANNELS - BODY
     nothing = jnp.zeros((WIDE - PADDED, BLOCK), jnp.float32)
     lane = lanes((WIDE, BLOCK))
     strip = jnp.zeros((WIDE, BLOCK), jnp.bfloat16)
@@ -248,7 +249,7 @@
         rounded = summed[row].astype(jnp.bfloat16)
         gridded[row] = rounded
         value = rounded.astype(jnp.float32)
-        value = jnp.where(channel < CHANNELS, value, 0.0)
+        value = jnp.concatenate([value[:BODY], jnp.where(real, value[BODY:], 0.0)], axis=0)
         square = jnp.sum(value * value, axis=0, keepdims=True) * (1.0 / CHANNELS)
         scaled = value * lax.rsqrt(square + EPSILON) * gain
         scaled = jnp.concatenate([scaled, nothing], axis=0).astype(jnp.bfloat16)
@@ -434,7 +435,7 @@
 ):
     near, far, reach = strip_plan(column_rows)
     near_strips, (west_pack, east_pack) = rest[: len(near)], rest[len(near) : len(near) + 2]
-    smoothed, turned = rest[len(near) + 2 :]
+    smoothed, turned, halves, sems = rest[len(near) + 2 :]
     count = lax.axis_size("tile")
     tile = lax.axis_index("tile")
     lane = lanes((WIDE, BLOCK))
@@ -623,24 +624,34 @@
     rim_lanes = lanes((PADDED, BLOCK))
     rim_lanes = (rim_lanes < 2) | (rim_lanes >= BLOCK - 2)
     spread = spread[:PADDED]
-    for row in range(ROWS):
-        value = base[row] + jnp.where(
-            rim_lanes, pltpu.roll(spread, (BLOCK - 4 * row - 2) % BLOCK, 1), 0.0
-        )
-        if row in rim_rows:
-            value = value + rim_rows[row][:PADDED]
-        turned[pl.ds(row, PADDED, stride=ROWS), :] = value
-    smoothed[...] = turned[pl.ds(0, CHANNELS * ROWS), :].astype(jnp.bfloat16)
+    copies = []
+    for half in range(2):
+        for row in range(half * HALF_ROWS, (half + 1) * HALF_ROWS):
+            value = base[row] + jnp.where(
+                rim_lanes, pltpu.roll(spread, (BLOCK - 4 * row - 2) % BLOCK, 1), 0.0
+            )
+            if row in rim_rows:
+                value = value + rim_rows[row][:PADDED]
+            turned[half, pl.ds(row - half * HALF_ROWS, PADDED, stride=HALF_ROWS), :] = value
+        rounded = turned[half, pl.ds(0, CHANNELS * HALF_ROWS), :].astype(jnp.bfloat16)
+        halves[half] = rounded.reshape(CHANNELS, HALF_ROWS, BLOCK)
+        rows = pl.ds(half * HALF_ROWS, HALF_ROWS)
+        copies.append(pltpu.make_async_copy(halves.at[half], smoothed.at[:, rows], sems.at[half]))
+        copies[-1].start()
+    for copy in copies:
+        copy.wait()
 
 
 def convolutions(column_rows, *operands):
     return pl.pallas_call(
         functools.partial(conv_kernel, column_rows),
         in_specs=[vmem()] * len(operands),
-        out_specs=vmem(),
-        out_shape=jax.ShapeDtypeStruct((CHANNELS * ROWS, BLOCK), jnp.bfloat16),
+        out_specs=pl.BlockSpec(memory_space=pl.ANY),
+        out_shape=jax.ShapeDtypeStruct((CHANNELS, ROWS, BLOCK), jnp.bfloat16),
         scratch_shapes=[
-            pltpu.VMEM((PADDED * ROWS, BLOCK), jnp.float32),
+            pltpu.VMEM((2, PADDED * HALF_ROWS, BLOCK), jnp.float32),
+            pltpu.VMEM((2, CHANNELS, HALF_ROWS, BLOCK), jnp.bfloat16),
+            pltpu.SemaphoreType.DMA((2,)),
         ],
         compiler_params=pltpu.CompilerParams(vmem_limit_bytes=VMEM_LIMIT),
         name="convolutions",

time: 67.9 us -> 68.2 us (level)
  no operation moved by 1% of the time
where the time goes in v4:
time: 68.2 us; the launch traced here: 67.4 us
  waiting for transfers between devices  29.1 us (43%)
  starting transfers between devices  21.9 us (32%)
  Pallas kernels  14.7 us (22%)
  between operations  1 us (1%)
  local copies, waits for them, and re-layouts  0.72 us (1%)
    ppermute x8, waiting for transfers between devices, per_device(): nexts[across] = lax.ppermute(nexts[across], 'tile', pairs)  27.1 us
    ppermute x8, starting transfers between devices, per_device(): nexts[across] = lax.ppermute(nexts[across], 'tile', pairs)  10.3 us
    all_to_all x1, starting transfers between devices, per_device(): lax.all_to_all(same, 'tile', 0, 0, axis_index_groups=[[c * column_rows +...  6.52 us
    pallas_call x1, Pallas kernels, regrid(): pl.pallas_call(functools.partial(regrid_kernel, column_rows), in_specs=[h...  5.6 us
    ppermute x4, starting transfers between devices, from_shift(): lax.ppermute(value, 'tile', [(i, (i - shift) % count) for i in range(coun...  5.05 us
    pallas_call x1, Pallas kernels, convolutions(): pl.pallas_call(functools.partial(conv_kernel, column_rows), in_specs=[vme...  3.14 us
    pallas_call x1, Pallas kernels, channels_first(): pl.pallas_call(turn_kernel, in_specs=[vmem()], out_specs=vmem(), out_shap...  1.98 us
    pallas_call x1, Pallas kernels, gather_rows(): pl.pallas_call(functools.partial(gather_kernel, column_rows), in_specs=[s...  1.98 us
  transfers between devices with their start and end apart: 13, of which 6 were waited for; matrix products, arithmetic and copies ran while one was open for 1% of the time, Pallas kernels for 6%

profile of v4, /device:TPU:1, one launch (start us, length us, event | category | flops | bytes accessed | tf_op | source)
XLA Modules:
  0.0 67.4 jit_solution(17817406376188594766)
XLA Ops:
  0.6 5.6 %regrid.1 = (bf16[4480,128]{1,0:T(8,128)(2,1)}, bf16[560,128]{1,0:T(8,128)(2,1)}, bf16[560,128]{1,0:T(8,128)(2,1)}, bf16[560,128]{1,0:T(8,128)(2,1)}, bf16[560,1...) custom-call(s32[96]{0:T(128)} %target_hbm.1, ...), custom_call_target="tpu_custom_call" | custom-call | tf_op jit(solution)/shard_map/regrid/pallas_call | solution.py:181
  6.2 0.0 copy-start.9
  6.2 0.0 copy-start.8
  6.3 0.0 copy-start.7
  6.3 0.0 copy-start.6
  6.3 0.0 copy-start.5
  6.3 0.0 copy-start.4
  6.3 0.0 copy-start.3
  6.3 0.0 copy-start.1
  6.3 0.0 copy-start.2
  6.3 6.5 %all-to-all-start = ((bf16[8,560,128]{2,1,0:T(8,128)(2,1)}), bf16[8,560,128]{2,1,0:T(8,128)(2,1)S(1)}, u32[]{:S(2)}, u32[]{:S(2)}) async-start(bf16[8,560,128]{2,1,0:T(8,128)(2,1)} %bitcast.27), calls=%async_computation | async-start | bytes 2293760 | tf_op jit(solution)/shard_map/all_to_all | solution.py:688
  12.9 0.0 copy-done.9
  12.9 1.3 %collective-permute-start = (bf16[560,128]{1,0:T(8,128)(2,1)S(1)}, bf16[560,128]{1,0:T(8,128)(2,1)S(1)}, u32[]{:S(2)}, u32[]{:S(2)}) collective-permute-start(bf16[560,128]{1,0:T(8,128)(2,1)S(1)} %copy-done.9), channel_id=1, source_target_pairs={{0,1},{2,3},{4,5},{6,7},{8,9},{10,11},{12,13},{14,15},{16,17},{18,... | collective-permute-start | bytes 430088 | tf_op jit(solution)/shard_map/ppermute | solution.py:686
  14.2 0.0 copy-start
  14.2 1.3 %collective-permute-start.1 = (bf16[560,128]{1,0:T(8,128)(2,1)S(1)}, bf16[560,128]{1,0:T(8,128)(2,1)S(1)}, u32[]{:S(2)}, u32[]{:S(2)}) collective-permute-start(bf16[560,128]{1,0:T(8,128)(2,1)S(1)} %copy-done.8), channel_id=1, source_target_pairs={{0,3},{2,1},{4,7},{6,5},{8,11},{10,9},{12,15},{14,13},{16,19},{18,... | collective-permute-start | bytes 430088 | tf_op jit(solution)/shard_map/ppermute | solution.py:686
  15.5 1.3 %collective-permute-start.2 = (bf16[560,128]{1,0:T(8,128)(2,1)S(1)}, bf16[560,128]{1,0:T(8,128)(2,1)S(1)}, u32[]{:S(2)}, u32[]{:S(2)}) collective-permute-start(bf16[560,128]{1,0:T(8,128)(2,1)S(1)} %copy-done.7), channel_id=1, source_target_pairs={{0,5},{2,7},{4,1},{6,3},{8,13},{10,15},{12,9},{14,11},{16,21},{18,... | collective-permute-start | bytes 430088 | tf_op jit(solution)/shard_map/ppermute | solution.py:686
  16.8 1.3 %collective-permute-start.3 = (bf16[560,128]{1,0:T(8,128)(2,1)}, bf16[560,128]{1,0:T(8,128)(2,1)S(1)}, u32[]{:S(2)}, u32[]{:S(2)}) collective-permute-start(bf16[560,128]{1,0:T(8,128)(2,1)} %get-tuple-element.40), channel_id=1, source_target_pairs={{0,9},{2,11},{4,13},{6,15},{8,1},{10,3},{12,5},{14,7},{16,25},{18,... | collective-permute-start | bytes 430088 | tf_op jit(solution)/shard_map/ppermute | solution.py:686
  18.1 1.3 %collective-permute-start.4 = (bf16[560,128]{1,0:T(8,128)(2,1)S(1)}, bf16[560,128]{1,0:T(8,128)(2,1)S(1)}, u32[]{:S(2)}, u32[]{:S(2)}) collective-permute-start(bf16[560,128]{1,0:T(8,128)(2,1)S(1)} %copy-done.6), channel_id=1, source_target_pairs={{0,11},{2,9},{4,15},{6,13},{8,3},{10,1},{12,7},{14,5},{16,27},{18,... | collective-permute-start | bytes 430088 | tf_op jit(solution)/shard_map/ppermute | solution.py:686
  19.4 0.0 collective-permute-done.rest_0_
  19.4 1.3 %collective-permute-start.5 = (bf16[560,128]{1,0:T(8,128)(2,1)S(1)}, bf16[560,128]{1,0:T(8,128)(2,1)S(1)}, u32[]{:S(2)}, u32[]{:S(2)}) collective-permute-start(bf16[560,128]{1,0:T(8,128)(2,1)S(1)} %copy-done.5), channel_id=1, source_target_pairs={{0,13},{2,15},{4,9},{6,11},{8,5},{10,7},{12,1},{14,3},{16,29},{18,... | collective-permute-start | bytes 430088 | tf_op jit(solution)/shard_map/ppermute | solution.py:686
  20.7 2.7 %collective-permute-done.1.rest_1_ = bf16[560,128]{1,0:T(8,128)(2,1)S(1)} collective-permute-done((bf16[560,128]{1,0:T(8,128)(2,1)S(1)}, bf16[560,128]{1,0:T(8,128)(2,1)S(1)}, u32[]{:S(2)}, u32[]{:S(2)}) %collective-permute-start.1) | collective-permute-done | bytes 143392 | tf_op jit(solution)/shard_map/ppermute | solution.py:686
  23.4 1.3 %collective-permute-start.6 = (bf16[560,128]{1,0:T(8,128)(2,1)S(1)}, bf16[560,128]{1,0:T(8,128)(2,1)S(1)}, u32[]{:S(2)}, u32[]{:S(2)}) collective-permute-start(bf16[560,128]{1,0:T(8,128)(2,1)S(1)} %copy-done.4), channel_id=1, source_target_pairs={{0,15},{2,13},{4,11},{6,9},{8,7},{10,5},{12,3},{14,1},{16,31},{18,... | collective-permute-start | bytes 430088 | tf_op jit(solution)/shard_map/ppermute | solution.py:686
  24.7 8.0 %collective-permute-done.2.rest_2_ = bf16[560,128]{1,0:T(8,128)(2,1)S(1)} collective-permute-done((bf16[560,128]{1,0:T(8,128)(2,1)S(1)}, bf16[560,128]{1,0:T(8,128)(2,1)S(1)}, u32[]{:S(2)}, u32[]{:S(2)}) %collective-permute-start.2) | collective-permute-done | bytes 143392 | tf_op jit(solution)/shard_map/ppermute | solution.py:686
  32.7 1.3 %collective-permute-start.7 = (bf16[560,128]{1,0:T(8,128)(2,1)S(1)}, bf16[560,128]{1,0:T(8,128)(2,1)S(1)}, u32[]{:S(2)}, u32[]{:S(2)}) collective-permute-start(bf16[560,128]{1,0:T(8,128)(2,1)S(1)} %copy-done.3), channel_id=1, source_target_pairs={{0,7},{2,5},{4,3},{6,1},{8,15},{10,13},{12,11},{14,9},{16,23},{18,... | collective-permute-start | bytes 430088 | tf_op jit(solution)/shard_map/ppermute | solution.py:686
  34.1 0.1 copy.17
  34.2 0.2 reshape.35.taps_ref.first_taps_ref
  34.4 0.1 copy.16
  34.5 0.2 reshape.37.taps_ref.second_taps_ref
  34.7 14.0 %collective-permute-done.3.rest_3_ = bf16[560,128]{1,0:T(8,128)(2,1)S(1)} collective-permute-done((bf16[560,128]{1,0:T(8,128)(2,1)}, bf16[560,128]{1,0:T(8,128)(2,1)S(1)}, u32[]{:S(2)}, u32[]{:S(2)}) %collective-permute-start.3) | collective-permute-done | bytes 143392 | tf_op jit(solution)/shard_map/ppermute | solution.py:686
  48.7 2.4 %collective-permute-done.4.rest_4_ = bf16[560,128]{1,0:T(8,128)(2,1)S(1)} collective-permute-done((bf16[560,128]{1,0:T(8,128)(2,1)S(1)}, bf16[560,128]{1,0:T(8,128)(2,1)S(1)}, u32[]{:S(2)}, u32[]{:S(2)}) %collective-permute-start.4) | collective-permute-done | bytes 143392 | tf_op jit(solution)/shard_map/ppermute | solution.py:686
  51.1 0.0 collective-permute-done.5.rest_5_
  51.1 0.0 collective-permute-done.6.rest_6_
  51.1 0.0 collective-permute-done.7.rest_7_
  51.1 0.0 all-to-all-done
  51.1 0.1 broadcast_in_dim.12.gain_ref
  51.2 2.0 %gather_rows.1 = (bf16[32,72,128]{2,1,0:T(8,128)(2,1)S(1)}, bf16[32,80,128]{2,1,0:T(8,128)(2,1)S(1)}, bf16[3,80,128]{2,1,0:T(8,128)(2,1)S(1)}, bf16[3,80,128]{2,1,0:T(8,128)(2,1)S(1)}, bf16[80,128]{1,0:T(8,128)(2,1)S(1)}) custom-call(s32[1,2]{1,0:T(1,128)S(1)} %copy-done, f32[72,128]{1,0:T(8,128)S(1)} %broadcast_in_dim.12.gain_ref, ...), custom_call_target="tpu_custom_call" | custom-call | tf_op jit(solution)/shard_map/gather_rows/pallas_call | solution.py:283
  53.2 0.1 collective-permute-start.8
  53.3 0.5 collective-permute-start.9
  53.8 2.0 %channels_first.1 = bf16[2208,128]{1,0:T(8,128)(2,1)} custom-call(bf16[32,72,128]{2,1,0:T(8,128)(2,1)S(1)} %get-tuple-element.63.field.gridded), custom_call_target="tpu_custom_call" | custom-call | tf_op jit(solution)/shard_map/channels_first/pallas_call | solution.py:304
  55.7 1.2 %inner_convolution.1 = (bf16[32,80,128]{2,1,0:T(8,128)(2,1)S(1)}, f32[2,80,128]{2,1,0:T(8,128)S(1)}, f32[2,80,128]{2,1,0:T(8,128)S(1)}) custom-call(bf16[240,240]{1,0:T(8,128)(2,1)S(1)} %reshape.35.taps_ref.first_taps_ref, bf16[32,80,128]{2,1,0:T(8,128)(2,1)S(1)} %get-tuple-element.59.field), custom_call_target="tpu_custom_call" | custom-call | flops 471859200 | bytes 2097152 | tf_op jit(solution)/shard_map/inner_convolution/pallas_call | solution.py:370
  57.0 0.0 collective-permute-done.8.above
  57.0 0.0 collective-permute-done.9.below
  57.0 3.3 %collective-permute-start.10 = (bf16[3,80,128]{2,1,0:T(8,128)(2,1)S(1)}, bf16[3,80,128]{2,1,0:T(8,128)(2,1)S(1)}, u32[]{:S(2)}, u32[]{:S(2)}) collective-permute-start(bf16[3,80,128]{2,1,0:T(8,128)(2,1)S(1)} %pad_maximum_fusion), channel_id=1, source_target_pairs={{0,3},{1,4},{2,5},{3,6},{4,7},{5,8},{6,9},{7,10},{8,11},{9,12},{10... | collective-permute-start | bytes 184328 | tf_op jit(solution)/shard_map/ppermute | solution.py:669
  60.3 1.2 %collective-permute-start.11 = (bf16[3,80,128]{2,1,0:T(8,128)(2,1)S(1)}, bf16[3,80,128]{2,1,0:T(8,128)(2,1)S(1)}, u32[]{:S(2)}, u32[]{:S(2)}) collective-permute-start(bf16[3,80,128]{2,1,0:T(8,128)(2,1)S(1)} %pad_maximum_fusion), channel_id=1, source_target_pairs={{0,13},{1,14},{2,15},{3,0},{4,1},{5,2},{6,3},{7,4},{8,5},{9,6},{10... | collective-permute-start | bytes 184328 | tf_op jit(solution)/shard_map/ppermute | solution.py:669
  61.5 0.8 %inner_second_convolution.1.base = f32[32,72,128]{2,1,0:T(8,128)S(1)} custom-call(bf16[240,240]{1,0:T(8,128)(2,1)S(1)} %reshape.37.taps_ref.second_taps_ref, bf16[32,80,128]{2,1,0:T(8,128)(2,1)S(1)} %get-tuple-element.66.hidden, bf16[32,72,128]{2,1,0:T(8,128)(2,1)S(1)} %get-tuple-element.63.field.gridded), custom_call_target="tpu_custom_call" | custom-call | flops 471859200 | bytes 2097152 | tf_op jit(solution)/shard_map/inner_second_convolution/pallas_call | solution.py:403
  62.3 1.4 %collective-permute-done.10.rest_0_ = bf16[3,80,128]{2,1,0:T(8,128)(2,1)S(1)} collective-permute-done((bf16[3,80,128]{2,1,0:T(8,128)(2,1)S(1)}, bf16[3,80,128]{2,1,0:T(8,128)(2,1)S(1)}, u32[]{:S(2)}, u32[]{:S(2)}) %collective-permute-start.10) | collective-permute-done | bytes 61472 | tf_op jit(solution)/shard_map/ppermute | solution.py:669
  63.7 0.6 collective-permute-done.11.rest_1_
  64.2 3.1 %convolutions.1 = bf16[69,32,128]{2,1,0:T(8,128)(2,1)} custom-call(bf16[240,240]{1,0:T(8,128)(2,1)S(1)} %reshape.35.taps_ref.first_taps_ref, bf16[240,240]{1,0:T(8,128)(2,1)S(1)} %reshape.37.taps_ref.second_taps_ref, bf16[32,80,128]{2,1,0:T(8,128)(2,1)S(1)} %get-tuple-element.59.field, f32[32,72,128]{2,1,0:T(8,128)S(1)} %inner_second_convolution.1.base, ...), custom_call_target="tpu_custom_call" | custom-call | tf_op jit(solution)/shard_map/convolutions/pallas_call | solution.py:646
  (17 shorter events, 0.1 us)
Async XLA Ops:
  6.2 6.6 %copy-start.9 = (bf16[560,128]{1,0:T(8,128)(2,1)S(1)}, bf16[560,128]{1,0:T(8,128)(2,1)}, u32[]{:S(2)}) copy-start(bf16[560,128]{1,0:T(8,128)(2,1)} %get-tuple-element.37) | copy-start | bytes 430084
  6.2 7.9 %copy-start.8 = (bf16[560,128]{1,0:T(8,128)(2,1)S(1)}, bf16[560,128]{1,0:T(8,128)(2,1)}, u32[]{:S(2)}) copy-start(bf16[560,128]{1,0:T(8,128)(2,1)} %get-tuple-element.38) | copy-start | bytes 430084
  6.3 9.2 %copy-start.7 = (bf16[560,128]{1,0:T(8,128)(2,1)S(1)}, bf16[560,128]{1,0:T(8,128)(2,1)}, u32[]{:S(2)}) copy-start(bf16[560,128]{1,0:T(8,128)(2,1)} %get-tuple-element.39) | copy-start | bytes 430084
  6.3 11.8 %copy-start.6 = (bf16[560,128]{1,0:T(8,128)(2,1)S(1)}, bf16[560,128]{1,0:T(8,128)(2,1)}, u32[]{:S(2)}) copy-start(bf16[560,128]{1,0:T(8,128)(2,1)} %get-tuple-element.41) | copy-start | bytes 430084
  6.3 13.1 %copy-start.5 = (bf16[560,128]{1,0:T(8,128)(2,1)S(1)}, bf16[560,128]{1,0:T(8,128)(2,1)}, u32[]{:S(2)}) copy-start(bf16[560,128]{1,0:T(8,128)(2,1)} %get-tuple-element.42) | copy-start | bytes 430084
  6.3 17.1 %copy-start.4 = (bf16[560,128]{1,0:T(8,128)(2,1)S(1)}, bf16[560,128]{1,0:T(8,128)(2,1)}, u32[]{:S(2)}) copy-start(bf16[560,128]{1,0:T(8,128)(2,1)} %get-tuple-element.43) | copy-start | bytes 430084
  6.3 26.4 %copy-start.3 = (bf16[560,128]{1,0:T(8,128)(2,1)S(1)}, bf16[560,128]{1,0:T(8,128)(2,1)}, u32[]{:S(2)}) copy-start(bf16[560,128]{1,0:T(8,128)(2,1)} %get-tuple-element.44) | copy-start | bytes 430084
  6.3 27.7 %copy-start.1 = (bf16[9,69,69]{2,1,0:T(8,128)(2,1)S(1)}, bf16[9,69,69]{2,1,0:T(8,128)(2,1)}, u32[]{:S(2)}) copy-start(bf16[9,69,69]{2,1,0:T(8,128)(2,1)} %param.14) | copy-start | bytes 257098
  6.3 28.0 %copy-start.2 = (bf16[9,69,69]{2,1,0:T(8,128)(2,1)S(1)}, bf16[9,69,69]{2,1,0:T(8,128)(2,1)}, u32[]{:S(2)}) copy-start(bf16[9,69,69]{2,1,0:T(8,128)(2,1)} %param.15) | copy-start | bytes 257098
  6.3 44.8 %all-to-all-start = ((bf16[8,560,128]{2,1,0:T(8,128)(2,1)}), bf16[8,560,128]{2,1,0:T(8,128)(2,1)S(1)}, u32[]{:S(2)}, u32[]{:S(2)}) async-start(bf16[8,560,128]{2,1,0:T(8,128)(2,1)} %bitcast.27), calls=%async_computation | async-start | bytes 2293760 | tf_op jit(solution)/shard_map/all_to_all | solution.py:688
  12.9 21.8 %copy-start.10 = (f32[69]{0:T(128)S(1)}, f32[69]{0:T(128)}, u32[]{:S(2)}) copy-start(f32[69]{0:T(128)} %param.13) | copy-start | bytes 832
  12.9 6.5 %collective-permute-start = (bf16[560,128]{1,0:T(8,128)(2,1)S(1)}, bf16[560,128]{1,0:T(8,128)(2,1)S(1)}, u32[]{:S(2)}, u32[]{:S(2)}) collective-permute-start(bf16[560,128]{1,0:T(8,128)(2,1)S(1)} %copy-done.9), channel_id=1, source_target_pairs={{0,1},{2,3},{4,5},{6,7},{8,9},{10,11},{12,13},{14,15},{16,17},{18,... | collective-permute-start | bytes 430088 | tf_op jit(solution)/shard_map/ppermute | solution.py:686
  14.2 37.0 %copy-start = (s32[1,2]{1,0:T(1,128)S(1)}, s32[1,2]{1,0:T(1,128)}, u32[]{:S(2)}) copy-start(s32[1,2]{1,0:T(1,128)} %flip_ref.1) | copy-start | bytes 28
  14.2 9.2 %collective-permute-start.1 = (bf16[560,128]{1,0:T(8,128)(2,1)S(1)}, bf16[560,128]{1,0:T(8,128)(2,1)S(1)}, u32[]{:S(2)}, u32[]{:S(2)}) collective-permute-start(bf16[560,128]{1,0:T(8,128)(2,1)S(1)} %copy-done.8), channel_id=1, source_target_pairs={{0,3},{2,1},{4,7},{6,5},{8,11},{10,9},{12,15},{14,13},{16,19},{18,... | collective-permute-start | bytes 430088 | tf_op jit(solution)/shard_map/ppermute | solution.py:686
  15.5 17.2 %collective-permute-start.2 = (bf16[560,128]{1,0:T(8,128)(2,1)S(1)}, bf16[560,128]{1,0:T(8,128)(2,1)S(1)}, u32[]{:S(2)}, u32[]{:S(2)}) collective-permute-start(bf16[560,128]{1,0:T(8,128)(2,1)S(1)} %copy-done.7), channel_id=1, source_target_pairs={{0,5},{2,7},{4,1},{6,3},{8,13},{10,15},{12,9},{14,11},{16,21},{18,... | collective-permute-start | bytes 430088 | tf_op jit(solution)/shard_map/ppermute | solution.py:686
  16.8 31.9 %collective-permute-start.3 = (bf16[560,128]{1,0:T(8,128)(2,1)}, bf16[560,128]{1,0:T(8,128)(2,1)S(1)}, u32[]{:S(2)}, u32[]{:S(2)}) collective-permute-start(bf16[560,128]{1,0:T(8,128)(2,1)} %get-tuple-element.40), channel_id=1, source_target_pairs={{0,9},{2,11},{4,13},{6,15},{8,1},{10,3},{12,5},{14,7},{16,25},{18,... | collective-permute-start | bytes 430088 | tf_op jit(solution)/shard_map/ppermute | solution.py:686
  18.1 33.0 %collective-permute-start.4 = (bf16[560,128]{1,0:T(8,128)(2,1)S(1)}, bf16[560,128]{1,0:T(8,128)(2,1)S(1)}, u32[]{:S(2)}, u32[]{:S(2)}) collective-permute-start(bf16[560,128]{1,0:T(8,128)(2,1)S(1)} %copy-done.6), channel_id=1, source_target_pairs={{0,11},{2,9},{4,15},{6,13},{8,3},{10,1},{12,7},{14,5},{16,27},{18,... | collective-permute-start | bytes 430088 | tf_op jit(solution)/shard_map/ppermute | solution.py:686
  19.4 31.7 %collective-permute-start.5 = (bf16[560,128]{1,0:T(8,128)(2,1)S(1)}, bf16[560,128]{1,0:T(8,128)(2,1)S(1)}, u32[]{:S(2)}, u32[]{:S(2)}) collective-permute-start(bf16[560,128]{1,0:T(8,128)(2,1)S(1)} %copy-done.5), channel_id=1, source_target_pairs={{0,13},{2,15},{4,9},{6,11},{8,5},{10,7},{12,1},{14,3},{16,29},{18,... | collective-permute-start | bytes 430088 | tf_op jit(solution)/shard_map/ppermute | solution.py:686
  23.4 27.7 %collective-permute-start.6 = (bf16[560,128]{1,0:T(8,128)(2,1)S(1)}, bf16[560,128]{1,0:T(8,128)(2,1)S(1)}, u32[]{:S(2)}, u32[]{:S(2)}) collective-permute-start(bf16[560,128]{1,0:T(8,128)(2,1)S(1)} %copy-done.4), channel_id=1, source_target_pairs={{0,15},{2,13},{4,11},{6,9},{8,7},{10,5},{12,3},{14,1},{16,31},{18,... | collective-permute-start | bytes 430088 | tf_op jit(solution)/shard_map/ppermute | solution.py:686
  32.7 18.4 %collective-permute-start.7 = (bf16[560,128]{1,0:T(8,128)(2,1)S(1)}, bf16[560,128]{1,0:T(8,128)(2,1)S(1)}, u32[]{:S(2)}, u32[]{:S(2)}) collective-permute-start(bf16[560,128]{1,0:T(8,128)(2,1)S(1)} %copy-done.3), channel_id=1, source_target_pairs={{0,7},{2,5},{4,3},{6,1},{8,15},{10,13},{12,11},{14,9},{16,23},{18,... | collective-permute-start | bytes 430088 | tf_op jit(solution)/shard_map/ppermute | solution.py:686
  53.2 3.8 %collective-permute-start.8 = (bf16[3,80,128]{2,1,0:T(8,128)(2,1)S(1)}, bf16[3,80,128]{2,1,0:T(8,128)(2,1)S(1)}, u32[]{:S(2)}, u32[]{:S(2)}) collective-permute-start(bf16[3,80,128]{2,1,0:T(8,128)(2,1)S(1)} %get-tuple-element.55), channel_id=1, source_target_pairs={{0,1},{1,2},{2,3},{3,4},{4,5},{5,6},{6,7},{7,8},{8,9},{9,10},{10,1... | collective-permute-start | bytes 184328 | tf_op jit(solution)/shard_map/ppermute | solution.py:669
  53.3 3.7 %collective-permute-start.9 = (bf16[3,80,128]{2,1,0:T(8,128)(2,1)S(1)}, bf16[3,80,128]{2,1,0:T(8,128)(2,1)S(1)}, u32[]{:S(2)}, u32[]{:S(2)}) collective-permute-start(bf16[3,80,128]{2,1,0:T(8,128)(2,1)S(1)} %get-tuple-element.57), channel_id=1, source_target_pairs={{0,15},{1,0},{2,1},{3,2},{4,3},{5,4},{6,5},{7,6},{8,7},{9,8},{10,9... | collective-permute-start | bytes 184328 | tf_op jit(solution)/shard_map/ppermute | solution.py:669
  57.0 6.6 %collective-permute-start.10 = (bf16[3,80,128]{2,1,0:T(8,128)(2,1)S(1)}, bf16[3,80,128]{2,1,0:T(8,128)(2,1)S(1)}, u32[]{:S(2)}, u32[]{:S(2)}) collective-permute-start(bf16[3,80,128]{2,1,0:T(8,128)(2,1)S(1)} %pad_maximum_fusion), channel_id=1, source_target_pairs={{0,3},{1,4},{2,5},{3,6},{4,7},{5,8},{6,9},{7,10},{8,11},{9,12},{10... | collective-permute-start | bytes 184328 | tf_op jit(solution)/shard_map/ppermute | solution.py:669
  60.3 3.9 %collective-permute-start.11 = (bf16[3,80,128]{2,1,0:T(8,128)(2,1)S(1)}, bf16[3,80,128]{2,1,0:T(8,128)(2,1)S(1)}, u32[]{:S(2)}, u32[]{:S(2)}) collective-permute-start(bf16[3,80,128]{2,1,0:T(8,128)(2,1)S(1)} %pad_maximum_fusion), channel_id=1, source_target_pairs={{0,13},{1,14},{2,15},{3,0},{4,1},{5,2},{6,3},{7,4},{8,5},{9,6},{10... | collective-permute-start | bytes 184328 | tf_op jit(solution)/shard_map/ppermute | solution.py:669

commit v5 on v4

--- a/solution.py
+++ b/solution.py
@@ -20,7 +20,6 @@
 GROUPS = 2 * TILE_COLS
 COLUMN_ORDER = [half * HALF + at for at in range(HALF) for half in range(2)]
 SLOTS = GROUPS * CAP
-CHUNK = 16
 MARK = CHANNELS
 BODY = 64
 TAILS = (MARK + 1 - BODY) * CAP
@@ -49,12 +48,11 @@
 
 
 def regrid_kernel(
-    column_rows, target_hbm, target_row_hbm, index_hbm, source_hbm, weight_hbm, *rest
+    column_rows, target_hbm, index_hbm, source_hbm, weight_hbm, *rest
 ):
     same_out, next_outs = rest[0], rest[1 : 1 + TILE_COLS]
     (
         target_ref,
-        target_row_ref,
         index_ref,
         source,
         weight,
@@ -67,33 +65,23 @@
         plan_scalars,
         plan_sem,
         in_sems,
-        weight_sems,
         out_sems,
     ) = rest[1 + TILE_COLS :]
     entries = weight.shape[0]
-    chunks = entries // CHUNK
     tile = lax.axis_index("tile")
     column, position = split(tile, column_rows)
 
-    small_copies = [
-        pltpu.make_async_copy(target_row_hbm, target_row_ref, in_sems.at[0]),
-        pltpu.make_async_copy(target_hbm, target_ref, in_sems.at[1]),
-        pltpu.make_async_copy(index_hbm, index_ref, in_sems.at[2]),
-    ]
-    source_copy = pltpu.make_async_copy(source_hbm, source, in_sems.at[3])
-    for copy in small_copies:
-        copy.start()
+    target_copy = pltpu.make_async_copy(target_hbm, target_ref, in_sems.at[0])
+    source_copy = pltpu.make_async_copy(source_hbm, source, in_sems.at[1])
+    index_copy = pltpu.make_async_copy(index_hbm, index_ref, in_sems.at[2])
+    target_copy.start()
     source_copy.start()
-
-    def chunk_copy(chunk):
-        part = pl.ds(chunk * CHUNK, CHUNK)
-        return pltpu.make_async_copy(weight_hbm.at[part], weight.at[part], weight_sems.at[chunk])
-
-    for chunk in range(chunks):
-        chunk_copy(chunk).start()
-
-    small_copies[0].wait()
-    target = target_row_ref[...]
+    index_copy.start()
+    weight_copy = pltpu.make_async_copy(weight_hbm, weight, in_sems.at[3])
+    weight_copy.start()
+
+    target_copy.wait()
+    target = target_ref[...]
     owner, row = split(target, ROWS)
     owner_column, owner_position = split(owner, column_rows)
     place = ((owner_column & (HALF - 1)) << 1) + (owner_column >= HALF).astype(jnp.int32)
@@ -113,7 +101,7 @@
     rank = jnp.sum(jnp.where(below, 1.0, 0.0), axis=0, keepdims=True)
     mentions = jnp.sum(jnp.where(equal & (down < along), 1.0, 0.0), axis=0, keepdims=True)
     slots = group * CAP + rank.astype(jnp.int32)
-    plan[...] = slots + jnp.where(mentions == 0.0, SLOTS, 0)
+    plan[...] = slots + jnp.where(mentions == 0.0, SLOTS, 0) + row * (2 * SLOTS)
     plan_copy = pltpu.make_async_copy(plan, plan_scalars, plan_sem)
     plan_copy.start()
 
@@ -130,12 +118,10 @@
         field[row] = jnp.concatenate([block, nothing], axis=0).astype(jnp.bfloat16)
     is_mark = lax.broadcasted_iota(jnp.int32, (8, BLOCK), 0) == MARK - BODY
     blank = jnp.zeros((WIDE, BLOCK), jnp.bfloat16)
-    small_copies[1].wait()
-    small_copies[2].wait()
+    index_copy.wait()
     plan_copy.wait()
 
-    for chunk in range(chunks):
-        chunk_copy(chunk).wait()
+    weight_copy.wait()
     for entry in range(0, entries, 2):
         one = jnp.concatenate([field[index_ref[entry]], blank], axis=1)
         two = jnp.concatenate([blank, field[index_ref[entry + 1]]], axis=1)
@@ -147,27 +133,29 @@
         for at in range(2):
             code = plan_scalars[0, entry + at]
             slot = code & (SLOTS - 1)
-            row = split(target_ref[entry + at], ROWS)[1]
+            fresh = (code & SLOTS) != 0
             product = products[at * WIDE : at * WIDE + PADDED]
-            total = jnp.where(code >= SLOTS, 0.0, sums[slot]) + product
+            total = jnp.where(fresh, 0.0, sums[slot]) + product
             sums[slot] = total
             group, place = split(slot, CAP)
             message[group, pl.ds(pl.multiple_of(place * BODY, BODY), BODY), :] = total[
                 :BODY
             ].astype(jnp.bfloat16)
             tails[pl.ds(pl.multiple_of(slot * 8, 8), 8), :] = jnp.where(
-                is_mark, row.astype(jnp.float32), total[BODY:]
+                is_mark, split(code, 2 * SLOTS)[0].astype(jnp.float32), total[BODY:]
             )
     copies = []
     for group in range(GROUPS):
         start = group * CAP * 8
         ends = [tails[pl.ds(start + at, CAP, stride=8), :] for at in range(MARK + 1 - BODY)]
         message[group, CAP * BODY :] = jnp.concatenate(ends, axis=0).astype(jnp.bfloat16)
-        if group < TILE_COLS:
-            out = same_out.at[pl.ds(group * MESSAGE, MESSAGE)]
+        if group == TILE_COLS - 1:
+            source_part, out = message.at[pl.ds(0, TILE_COLS)], same_out
+        elif group >= TILE_COLS:
+            source_part, out = message.at[group], next_outs[group - TILE_COLS]
         else:
-            out = next_outs[group - TILE_COLS]
-        copies.append(pltpu.make_async_copy(message.at[group], out, out_sems.at[group]))
+            continue
+        copies.append(pltpu.make_async_copy(source_part, out, out_sems.at[len(copies)]))
         copies[-1].start()
     for copy in copies:
         copy.wait()
@@ -175,16 +163,15 @@
 
 def regrid(target, source_index, field, weights, column_rows):
     piece = jax.ShapeDtypeStruct((MESSAGE, BLOCK), jnp.bfloat16)
-    same = jax.ShapeDtypeStruct((TILE_COLS * MESSAGE, BLOCK), jnp.bfloat16)
+    same = jax.ShapeDtypeStruct((TILE_COLS, MESSAGE, BLOCK), jnp.bfloat16)
     hbm = pl.BlockSpec(memory_space=pl.ANY)
     entries = weights.shape[0]
     return pl.pallas_call(
         functools.partial(regrid_kernel, column_rows),
-        in_specs=[hbm] * 5,
+        in_specs=[hbm] * 4,
         out_specs=[hbm] * (1 + TILE_COLS),
         out_shape=[same] + [piece] * TILE_COLS,
         scratch_shapes=[
-            pltpu.SMEM(target.shape, jnp.int32),
             pltpu.VMEM((1, entries), jnp.int32),
             pltpu.SMEM(source_index.shape, jnp.int32),
             pltpu.VMEM(field.shape, jnp.bfloat16),
@@ -198,12 +185,11 @@
             pltpu.SMEM((1, entries), jnp.int32),
             pltpu.SemaphoreType.DMA,
             pltpu.SemaphoreType.DMA((4,)),
-            pltpu.SemaphoreType.DMA((entries // CHUNK,)),
-            pltpu.SemaphoreType.DMA((GROUPS,)),
+            pltpu.SemaphoreType.DMA((1 + TILE_COLS,)),
         ],
         compiler_params=pltpu.CompilerParams(vmem_limit_bytes=REGRID_VMEM),
         name="regrid",
-    )(target, target.reshape(1, -1), source_index, field, weights)
+    )(target.reshape(1, -1), source_index, field, weights)
 
 
 def gather_kernel(column_rows, flip_ref, gain_ref, same, *rest):
@@ -233,7 +219,7 @@
 
     tails[:, TAILS:] = jnp.zeros((GROUPS, 8 * CAP - TAILS, BLOCK), jnp.float32)
     for group in range(TILE_COLS):
-        add(group, same.at[pl.ds(group * MESSAGE, MESSAGE)])
+        add(group, same.at[group])
 
     @pl.when(position > 0)
     def _():

time: 68.2 us -> 67.6 us (level)
  no operation moved by 1% of the time
where the time goes in v5:
time: 67.6 us; the launch traced here: 66.8 us
  waiting for transfers between devices  29.1 us (43%)
  starting transfers between devices  21.9 us (32%)
  Pallas kernels  14.1 us (21%)
  between operations  1 us (1%)
  local copies, waits for them, and re-layouts  0.72 us (1%)
    ppermute x8, waiting for transfers between devices, per_device(): nexts[across] = lax.ppermute(nexts[across], 'tile', pairs)  27.1 us
    ppermute x8, starting transfers between devices, per_device(): nexts[across] = lax.ppermute(nexts[across], 'tile', pairs)  10.3 us
    all_to_all x1, starting transfers between devices, per_device(): lax.all_to_all(same, 'tile', 0, 0, axis_index_groups=[[c * column_rows +...  6.53 us
    ppermute x4, starting transfers between devices, from_shift(): lax.ppermute(value, 'tile', [(i, (i - shift) % count) for i in range(coun...  5.05 us
    pallas_call x1, Pallas kernels, regrid(): pl.pallas_call(functools.partial(regrid_kernel, column_rows), in_specs=[h...  4.97 us
    pallas_call x1, Pallas kernels, convolutions(): pl.pallas_call(functools.partial(conv_kernel, column_rows), in_specs=[vme...  3.13 us
    pallas_call x1, Pallas kernels, channels_first(): pl.pallas_call(turn_kernel, in_specs=[vmem()], out_specs=vmem(), out_shap...  1.98 us
    pallas_call x1, Pallas kernels, gather_rows(): pl.pallas_call(functools.partial(gather_kernel, column_rows), in_specs=[s...  1.97 us
  transfers between devices with their start and end apart: 13, of which 6 were waited for; matrix products, arithmetic and copies ran while one was open for 1% of the time, Pallas kernels for 6%

profile of v5, /device:TPU:1, one launch (start us, length us, event | category | flops | bytes accessed | tf_op | source)
XLA Modules:
  0.0 66.8 jit_solution(6250660175832303841)
XLA Ops:
  0.6 5.0 %regrid.1 = (bf16[8,560,128]{2,1,0:T(8,128)(2,1)}, bf16[560,128]{1,0:T(8,128)(2,1)}, bf16[560,128]{1,0:T(8,128)(2,1)}, bf16[560,128]{1,0:T(8,128)(2,1)}, bf16[56...) custom-call(s32[1,96]{1,0:T(1,128)} %bitcast.31, ...), custom_call_target="tpu_custom_call" | custom-call | tf_op jit(solution)/shard_map/regrid/pallas_call | solution.py:169
  5.6 0.0 copy-start.9
  5.6 0.0 copy-start.8
  5.7 0.0 copy-start.1
  5.7 0.0 copy-start.2
  5.7 6.5 %all-to-all-start = ((bf16[8,560,128]{2,1,0:T(8,128)(2,1)}), bf16[8,560,128]{2,1,0:T(8,128)(2,1)S(1)}, u32[]{:S(2)}, u32[]{:S(2)}) async-start(bf16[8,560,128]{2,1,0:T(8,128)(2,1)} %get-tuple-element.36), calls=%async_computation | async-start | bytes 2293760 | tf_op jit(solution)/shard_map/all_to_all | solution.py:674
  12.2 0.0 copy-start
  12.3 1.3 %collective-permute-start = (bf16[560,128]{1,0:T(8,128)(2,1)S(1)}, bf16[560,128]{1,0:T(8,128)(2,1)S(1)}, u32[]{:S(2)}, u32[]{:S(2)}) collective-permute-start(bf16[560,128]{1,0:T(8,128)(2,1)S(1)} %copy-done.9), channel_id=1, source_target_pairs={{0,1},{2,3},{4,5},{6,7},{8,9},{10,11},{12,13},{14,15},{16,17},{18,... | collective-permute-start | bytes 430088 | tf_op jit(solution)/shard_map/ppermute | solution.py:672
  13.6 0.0 copy-done.8
  13.6 1.3 %collective-permute-start.1 = (bf16[560,128]{1,0:T(8,128)(2,1)S(1)}, bf16[560,128]{1,0:T(8,128)(2,1)S(1)}, u32[]{:S(2)}, u32[]{:S(2)}) collective-permute-start(bf16[560,128]{1,0:T(8,128)(2,1)S(1)} %copy-done.8), channel_id=1, source_target_pairs={{0,3},{2,1},{4,7},{6,5},{8,11},{10,9},{12,15},{14,13},{16,19},{18,... | collective-permute-start | bytes 430088 | tf_op jit(solution)/shard_map/ppermute | solution.py:672
  14.9 0.0 copy-done.7
  14.9 1.3 %collective-permute-start.2 = (bf16[560,128]{1,0:T(8,128)(2,1)S(1)}, bf16[560,128]{1,0:T(8,128)(2,1)S(1)}, u32[]{:S(2)}, u32[]{:S(2)}) collective-permute-start(bf16[560,128]{1,0:T(8,128)(2,1)S(1)} %copy-done.7), channel_id=1, source_target_pairs={{0,5},{2,7},{4,1},{6,3},{8,13},{10,15},{12,9},{14,11},{16,21},{18,... | collective-permute-start | bytes 430088 | tf_op jit(solution)/shard_map/ppermute | solution.py:672
  16.2 1.3 %collective-permute-start.3 = (bf16[560,128]{1,0:T(8,128)(2,1)}, bf16[560,128]{1,0:T(8,128)(2,1)S(1)}, u32[]{:S(2)}, u32[]{:S(2)}) collective-permute-start(bf16[560,128]{1,0:T(8,128)(2,1)} %get-tuple-element.40), channel_id=1, source_target_pairs={{0,9},{2,11},{4,13},{6,15},{8,1},{10,3},{12,5},{14,7},{16,25},{18,... | collective-permute-start | bytes 430088 | tf_op jit(solution)/shard_map/ppermute | solution.py:672
  17.5 0.0 copy-done.6
  17.5 1.3 %collective-permute-start.4 = (bf16[560,128]{1,0:T(8,128)(2,1)S(1)}, bf16[560,128]{1,0:T(8,128)(2,1)S(1)}, u32[]{:S(2)}, u32[]{:S(2)}) collective-permute-start(bf16[560,128]{1,0:T(8,128)(2,1)S(1)} %copy-done.6), channel_id=1, source_target_pairs={{0,11},{2,9},{4,15},{6,13},{8,3},{10,1},{12,7},{14,5},{16,27},{18,... | collective-permute-start | bytes 430088 | tf_op jit(solution)/shard_map/ppermute | solution.py:672
  18.8 0.0 collective-permute-done.rest_0_
  18.8 1.3 %collective-permute-start.5 = (bf16[560,128]{1,0:T(8,128)(2,1)S(1)}, bf16[560,128]{1,0:T(8,128)(2,1)S(1)}, u32[]{:S(2)}, u32[]{:S(2)}) collective-permute-start(bf16[560,128]{1,0:T(8,128)(2,1)S(1)} %copy-done.5), channel_id=1, source_target_pairs={{0,13},{2,15},{4,9},{6,11},{8,5},{10,7},{12,1},{14,3},{16,29},{18,... | collective-permute-start | bytes 430088 | tf_op jit(solution)/shard_map/ppermute | solution.py:672
  20.1 2.7 %collective-permute-done.1.rest_1_ = bf16[560,128]{1,0:T(8,128)(2,1)S(1)} collective-permute-done((bf16[560,128]{1,0:T(8,128)(2,1)S(1)}, bf16[560,128]{1,0:T(8,128)(2,1)S(1)}, u32[]{:S(2)}, u32[]{:S(2)}) %collective-permute-start.1) | collective-permute-done | bytes 143392 | tf_op jit(solution)/shard_map/ppermute | solution.py:672
  22.8 1.3 %collective-permute-start.6 = (bf16[560,128]{1,0:T(8,128)(2,1)S(1)}, bf16[560,128]{1,0:T(8,128)(2,1)S(1)}, u32[]{:S(2)}, u32[]{:S(2)}) collective-permute-start(bf16[560,128]{1,0:T(8,128)(2,1)S(1)} %copy-done.4), channel_id=1, source_target_pairs={{0,15},{2,13},{4,11},{6,9},{8,7},{10,5},{12,3},{14,1},{16,31},{18,... | collective-permute-start | bytes 430088 | tf_op jit(solution)/shard_map/ppermute | solution.py:672
  24.1 8.0 %collective-permute-done.2.rest_2_ = bf16[560,128]{1,0:T(8,128)(2,1)S(1)} collective-permute-done((bf16[560,128]{1,0:T(8,128)(2,1)S(1)}, bf16[560,128]{1,0:T(8,128)(2,1)S(1)}, u32[]{:S(2)}, u32[]{:S(2)}) %collective-permute-start.2) | collective-permute-done | bytes 143392 | tf_op jit(solution)/shard_map/ppermute | solution.py:672
  32.1 0.0 copy-done.3
  32.1 1.3 %collective-permute-start.7 = (bf16[560,128]{1,0:T(8,128)(2,1)S(1)}, bf16[560,128]{1,0:T(8,128)(2,1)S(1)}, u32[]{:S(2)}, u32[]{:S(2)}) collective-permute-start(bf16[560,128]{1,0:T(8,128)(2,1)S(1)} %copy-done.3), channel_id=1, source_target_pairs={{0,7},{2,5},{4,3},{6,1},{8,15},{10,13},{12,11},{14,9},{16,23},{18,... | collective-permute-start | bytes 430088 | tf_op jit(solution)/shard_map/ppermute | solution.py:672
  33.4 0.0 copy-done.1
  33.4 0.1 copy.17
  33.5 0.2 reshape.33.taps_ref.first_taps_ref
  33.7 0.0 copy-done.2
  33.8 0.1 copy.16
  33.9 0.2 reshape.35.taps_ref.second_taps_ref
  34.0 14.0 %collective-permute-done.3.rest_3_ = bf16[560,128]{1,0:T(8,128)(2,1)S(1)} collective-permute-done((bf16[560,128]{1,0:T(8,128)(2,1)}, bf16[560,128]{1,0:T(8,128)(2,1)S(1)}, u32[]{:S(2)}, u32[]{:S(2)}) %collective-permute-start.3) | collective-permute-done | bytes 143392 | tf_op jit(solution)/shard_map/ppermute | solution.py:672
  48.1 2.4 %collective-permute-done.4.rest_4_ = bf16[560,128]{1,0:T(8,128)(2,1)S(1)} collective-permute-done((bf16[560,128]{1,0:T(8,128)(2,1)S(1)}, bf16[560,128]{1,0:T(8,128)(2,1)S(1)}, u32[]{:S(2)}, u32[]{:S(2)}) %collective-permute-start.4) | collective-permute-done | bytes 143392 | tf_op jit(solution)/shard_map/ppermute | solution.py:672
  50.5 0.0 collective-permute-done.5.rest_5_
  50.5 0.0 collective-permute-done.6.rest_6_
  50.5 0.0 collective-permute-done.7.rest_7_
  50.5 0.0 all-to-all-done.same
  50.5 0.1 broadcast_in_dim.12.gain_ref
  50.6 2.0 %gather_rows.1 = (bf16[32,72,128]{2,1,0:T(8,128)(2,1)S(1)}, bf16[32,80,128]{2,1,0:T(8,128)(2,1)S(1)}, bf16[3,80,128]{2,1,0:T(8,128)(2,1)S(1)}, bf16[3,80,128]{2,1,0:T(8,128)(2,1)S(1)}, bf16[80,128]{1,0:T(8,128)(2,1)S(1)}) custom-call(s32[1,2]{1,0:T(1,128)S(1)} %copy-done, f32[72,128]{1,0:T(8,128)S(1)} %broadcast_in_dim.12.gain_ref, ...), custom_call_target="tpu_custom_call" | custom-call | tf_op jit(solution)/shard_map/gather_rows/pallas_call | solution.py:269
  52.6 0.1 collective-permute-start.8
  52.6 0.5 collective-permute-start.9
  53.1 2.0 %channels_first.1 = bf16[2208,128]{1,0:T(8,128)(2,1)} custom-call(bf16[32,72,128]{2,1,0:T(8,128)(2,1)S(1)} %get-tuple-element.63.field.gridded), custom_call_target="tpu_custom_call" | custom-call | tf_op jit(solution)/shard_map/channels_first/pallas_call | solution.py:290
  55.1 1.2 %inner_convolution.1 = (bf16[32,80,128]{2,1,0:T(8,128)(2,1)S(1)}, f32[2,80,128]{2,1,0:T(8,128)S(1)}, f32[2,80,128]{2,1,0:T(8,128)S(1)}) custom-call(bf16[240,240]{1,0:T(8,128)(2,1)S(1)} %reshape.33.taps_ref.first_taps_ref, bf16[32,80,128]{2,1,0:T(8,128)(2,1)S(1)} %get-tuple-element.59.field), custom_call_target="tpu_custom_call" | custom-call | flops 471859200 | bytes 2097152 | tf_op jit(solution)/shard_map/inner_convolution/pallas_call | solution.py:356
  56.3 0.0 collective-permute-done.8.above
  56.4 0.0 collective-permute-done.9.below
  56.4 3.3 %collective-permute-start.10 = (bf16[3,80,128]{2,1,0:T(8,128)(2,1)S(1)}, bf16[3,80,128]{2,1,0:T(8,128)(2,1)S(1)}, u32[]{:S(2)}, u32[]{:S(2)}) collective-permute-start(bf16[3,80,128]{2,1,0:T(8,128)(2,1)S(1)} %pad_maximum_fusion), channel_id=1, source_target_pairs={{0,3},{1,4},{2,5},{3,6},{4,7},{5,8},{6,9},{7,10},{8,11},{9,12},{10... | collective-permute-start | bytes 184328 | tf_op jit(solution)/shard_map/ppermute | solution.py:655
  59.7 1.2 %collective-permute-start.11 = (bf16[3,80,128]{2,1,0:T(8,128)(2,1)S(1)}, bf16[3,80,128]{2,1,0:T(8,128)(2,1)S(1)}, u32[]{:S(2)}, u32[]{:S(2)}) collective-permute-start(bf16[3,80,128]{2,1,0:T(8,128)(2,1)S(1)} %pad_maximum_fusion), channel_id=1, source_target_pairs={{0,13},{1,14},{2,15},{3,0},{4,1},{5,2},{6,3},{7,4},{8,5},{9,6},{10... | collective-permute-start | bytes 184328 | tf_op jit(solution)/shard_map/ppermute | solution.py:655
  60.9 0.8 %inner_second_convolution.1.base = f32[32,72,128]{2,1,0:T(8,128)S(1)} custom-call(bf16[240,240]{1,0:T(8,128)(2,1)S(1)} %reshape.35.taps_ref.second_taps_ref, bf16[32,80,128]{2,1,0:T(8,128)(2,1)S(1)} %get-tuple-element.66.hidden, bf16[32,72,128]{2,1,0:T(8,128)(2,1)S(1)} %get-tuple-element.63.field.gridded), custom_call_target="tpu_custom_call" | custom-call | flops 471859200 | bytes 2097152 | tf_op jit(solution)/shard_map/inner_second_convolution/pallas_call | solution.py:389
  61.7 1.4 %collective-permute-done.10.rest_0_ = bf16[3,80,128]{2,1,0:T(8,128)(2,1)S(1)} collective-permute-done((bf16[3,80,128]{2,1,0:T(8,128)(2,1)S(1)}, bf16[3,80,128]{2,1,0:T(8,128)(2,1)S(1)}, u32[]{:S(2)}, u32[]{:S(2)}) %collective-permute-start.10) | collective-permute-done | bytes 61472 | tf_op jit(solution)/shard_map/ppermute | solution.py:655
  63.0 0.6 collective-permute-done.11.rest_1_
  63.6 3.1 %convolutions.1 = bf16[69,32,128]{2,1,0:T(8,128)(2,1)} custom-call(bf16[240,240]{1,0:T(8,128)(2,1)S(1)} %reshape.33.taps_ref.first_taps_ref, bf16[240,240]{1,0:T(8,128)(2,1)S(1)} %reshape.35.taps_ref.second_taps_ref, bf16[32,80,128]{2,1,0:T(8,128)(2,1)S(1)} %get-tuple-element.59.field, f32[32,72,128]{2,1,0:T(8,128)S(1)} %inner_second_convolution.1.base, ...), custom_call_target="tpu_custom_call" | custom-call | tf_op jit(solution)/shard_map/convolutions/pallas_call | solution.py:632
  (17 shorter events, 0.1 us)
Async XLA Ops:
  5.6 6.6 %copy-start.9 = (bf16[560,128]{1,0:T(8,128)(2,1)S(1)}, bf16[560,128]{1,0:T(8,128)(2,1)}, u32[]{:S(2)}) copy-start(bf16[560,128]{1,0:T(8,128)(2,1)} %get-tuple-element.37) | copy-start | bytes 430084
  5.6 7.9 %copy-start.8 = (bf16[560,128]{1,0:T(8,128)(2,1)S(1)}, bf16[560,128]{1,0:T(8,128)(2,1)}, u32[]{:S(2)}) copy-start(bf16[560,128]{1,0:T(8,128)(2,1)} %get-tuple-element.38) | copy-start | bytes 430084
  5.6 9.2 %copy-start.7 = (bf16[560,128]{1,0:T(8,128)(2,1)S(1)}, bf16[560,128]{1,0:T(8,128)(2,1)}, u32[]{:S(2)}) copy-start(bf16[560,128]{1,0:T(8,128)(2,1)} %get-tuple-element.39) | copy-start | bytes 430084
  5.6 11.8 %copy-start.6 = (bf16[560,128]{1,0:T(8,128)(2,1)S(1)}, bf16[560,128]{1,0:T(8,128)(2,1)}, u32[]{:S(2)}) copy-start(bf16[560,128]{1,0:T(8,128)(2,1)} %get-tuple-element.41) | copy-start | bytes 430084
  5.7 13.1 %copy-start.5 = (bf16[560,128]{1,0:T(8,128)(2,1)S(1)}, bf16[560,128]{1,0:T(8,128)(2,1)}, u32[]{:S(2)}) copy-start(bf16[560,128]{1,0:T(8,128)(2,1)} %get-tuple-element.42) | copy-start | bytes 430084
  5.7 17.1 %copy-start.4 = (bf16[560,128]{1,0:T(8,128)(2,1)S(1)}, bf16[560,128]{1,0:T(8,128)(2,1)}, u32[]{:S(2)}) copy-start(bf16[560,128]{1,0:T(8,128)(2,1)} %get-tuple-element.43) | copy-start | bytes 430084
  5.7 26.4 %copy-start.3 = (bf16[560,128]{1,0:T(8,128)(2,1)S(1)}, bf16[560,128]{1,0:T(8,128)(2,1)}, u32[]{:S(2)}) copy-start(bf16[560,128]{1,0:T(8,128)(2,1)} %get-tuple-element.44) | copy-start | bytes 430084
  5.7 27.7 %copy-start.1 = (bf16[9,69,69]{2,1,0:T(8,128)(2,1)S(1)}, bf16[9,69,69]{2,1,0:T(8,128)(2,1)}, u32[]{:S(2)}) copy-start(bf16[9,69,69]{2,1,0:T(8,128)(2,1)} %param.14) | copy-start | bytes 257098
  5.7 28.0 %copy-start.2 = (bf16[9,69,69]{2,1,0:T(8,128)(2,1)S(1)}, bf16[9,69,69]{2,1,0:T(8,128)(2,1)}, u32[]{:S(2)}) copy-start(bf16[9,69,69]{2,1,0:T(8,128)(2,1)} %param.15) | copy-start | bytes 257098
  5.7 44.8 %all-to-all-start = ((bf16[8,560,128]{2,1,0:T(8,128)(2,1)}), bf16[8,560,128]{2,1,0:T(8,128)(2,1)S(1)}, u32[]{:S(2)}, u32[]{:S(2)}) async-start(bf16[8,560,128]{2,1,0:T(8,128)(2,1)} %get-tuple-element.36), calls=%async_computation | async-start | bytes 2293760 | tf_op jit(solution)/shard_map/all_to_all | solution.py:674
  12.2 21.8 %copy-start.10 = (f32[69]{0:T(128)S(1)}, f32[69]{0:T(128)}, u32[]{:S(2)}) copy-start(f32[69]{0:T(128)} %param.13) | copy-start | bytes 832
  12.2 38.3 %copy-start = (s32[1,2]{1,0:T(1,128)S(1)}, s32[1,2]{1,0:T(1,128)}, u32[]{:S(2)}) copy-start(s32[1,2]{1,0:T(1,128)} %flip_ref.1) | copy-start | bytes 28
  12.3 6.5 %collective-permute-start = (bf16[560,128]{1,0:T(8,128)(2,1)S(1)}, bf16[560,128]{1,0:T(8,128)(2,1)S(1)}, u32[]{:S(2)}, u32[]{:S(2)}) collective-permute-start(bf16[560,128]{1,0:T(8,128)(2,1)S(1)} %copy-done.9), channel_id=1, source_target_pairs={{0,1},{2,3},{4,5},{6,7},{8,9},{10,11},{12,13},{14,15},{16,17},{18,... | collective-permute-start | bytes 430088 | tf_op jit(solution)/shard_map/ppermute | solution.py:672
  13.6 9.2 %collective-permute-start.1 = (bf16[560,128]{1,0:T(8,128)(2,1)S(1)}, bf16[560,128]{1,0:T(8,128)(2,1)S(1)}, u32[]{:S(2)}, u32[]{:S(2)}) collective-permute-start(bf16[560,128]{1,0:T(8,128)(2,1)S(1)} %copy-done.8), channel_id=1, source_target_pairs={{0,3},{2,1},{4,7},{6,5},{8,11},{10,9},{12,15},{14,13},{16,19},{18,... | collective-permute-start | bytes 430088 | tf_op jit(solution)/shard_map/ppermute | solution.py:672
  14.9 17.2 %collective-permute-start.2 = (bf16[560,128]{1,0:T(8,128)(2,1)S(1)}, bf16[560,128]{1,0:T(8,128)(2,1)S(1)}, u32[]{:S(2)}, u32[]{:S(2)}) collective-permute-start(bf16[560,128]{1,0:T(8,128)(2,1)S(1)} %copy-done.7), channel_id=1, source_target_pairs={{0,5},{2,7},{4,1},{6,3},{8,13},{10,15},{12,9},{14,11},{16,21},{18,... | collective-permute-start | bytes 430088 | tf_op jit(solution)/shard_map/ppermute | solution.py:672
  16.2 31.9 %collective-permute-start.3 = (bf16[560,128]{1,0:T(8,128)(2,1)}, bf16[560,128]{1,0:T(8,128)(2,1)S(1)}, u32[]{:S(2)}, u32[]{:S(2)}) collective-permute-start(bf16[560,128]{1,0:T(8,128)(2,1)} %get-tuple-element.40), channel_id=1, source_target_pairs={{0,9},{2,11},{4,13},{6,15},{8,1},{10,3},{12,5},{14,7},{16,25},{18,... | collective-permute-start | bytes 430088 | tf_op jit(solution)/shard_map/ppermute | solution.py:672
  17.5 33.0 %collective-permute-start.4 = (bf16[560,128]{1,0:T(8,128)(2,1)S(1)}, bf16[560,128]{1,0:T(8,128)(2,1)S(1)}, u32[]{:S(2)}, u32[]{:S(2)}) collective-permute-start(bf16[560,128]{1,0:T(8,128)(2,1)S(1)} %copy-done.6), channel_id=1, source_target_pairs={{0,11},{2,9},{4,15},{6,13},{8,3},{10,1},{12,7},{14,5},{16,27},{18,... | collective-permute-start | bytes 430088 | tf_op jit(solution)/shard_map/ppermute | solution.py:672
  18.8 31.7 %collective-permute-start.5 = (bf16[560,128]{1,0:T(8,128)(2,1)S(1)}, bf16[560,128]{1,0:T(8,128)(2,1)S(1)}, u32[]{:S(2)}, u32[]{:S(2)}) collective-permute-start(bf16[560,128]{1,0:T(8,128)(2,1)S(1)} %copy-done.5), channel_id=1, source_target_pairs={{0,13},{2,15},{4,9},{6,11},{8,5},{10,7},{12,1},{14,3},{16,29},{18,... | collective-permute-start | bytes 430088 | tf_op jit(solution)/shard_map/ppermute | solution.py:672
  22.8 27.7 %collective-permute-start.6 = (bf16[560,128]{1,0:T(8,128)(2,1)S(1)}, bf16[560,128]{1,0:T(8,128)(2,1)S(1)}, u32[]{:S(2)}, u32[]{:S(2)}) collective-permute-start(bf16[560,128]{1,0:T(8,128)(2,1)S(1)} %copy-done.4), channel_id=1, source_target_pairs={{0,15},{2,13},{4,11},{6,9},{8,7},{10,5},{12,3},{14,1},{16,31},{18,... | collective-permute-start | bytes 430088 | tf_op jit(solution)/shard_map/ppermute | solution.py:672
  32.1 18.4 %collective-permute-start.7 = (bf16[560,128]{1,0:T(8,128)(2,1)S(1)}, bf16[560,128]{1,0:T(8,128)(2,1)S(1)}, u32[]{:S(2)}, u32[]{:S(2)}) collective-permute-start(bf16[560,128]{1,0:T(8,128)(2,1)S(1)} %copy-done.3), channel_id=1, source_target_pairs={{0,7},{2,5},{4,3},{6,1},{8,15},{10,13},{12,11},{14,9},{16,23},{18,... | collective-permute-start | bytes 430088 | tf_op jit(solution)/shard_map/ppermute | solution.py:672
  52.6 3.8 %collective-permute-start.8 = (bf16[3,80,128]{2,1,0:T(8,128)(2,1)S(1)}, bf16[3,80,128]{2,1,0:T(8,128)(2,1)S(1)}, u32[]{:S(2)}, u32[]{:S(2)}) collective-permute-start(bf16[3,80,128]{2,1,0:T(8,128)(2,1)S(1)} %get-tuple-element.55), channel_id=1, source_target_pairs={{0,1},{1,2},{2,3},{3,4},{4,5},{5,6},{6,7},{7,8},{8,9},{9,10},{10,1... | collective-permute-start | bytes 184328 | tf_op jit(solution)/shard_map/ppermute | solution.py:655
  52.6 3.7 %collective-permute-start.9 = (bf16[3,80,128]{2,1,0:T(8,128)(2,1)S(1)}, bf16[3,80,128]{2,1,0:T(8,128)(2,1)S(1)}, u32[]{:S(2)}, u32[]{:S(2)}) collective-permute-start(bf16[3,80,128]{2,1,0:T(8,128)(2,1)S(1)} %get-tuple-element.57), channel_id=1, source_target_pairs={{0,15},{1,0},{2,1},{3,2},{4,3},{5,4},{6,5},{7,6},{8,7},{9,8},{10,9... | collective-permute-start | bytes 184328 | tf_op jit(solution)/shard_map/ppermute | solution.py:655
  56.4 6.6 %collective-permute-start.10 = (bf16[3,80,128]{2,1,0:T(8,128)(2,1)S(1)}, bf16[3,80,128]{2,1,0:T(8,128)(2,1)S(1)}, u32[]{:S(2)}, u32[]{:S(2)}) collective-permute-start(bf16[3,80,128]{2,1,0:T(8,128)(2,1)S(1)} %pad_maximum_fusion), channel_id=1, source_target_pairs={{0,3},{1,4},{2,5},{3,6},{4,7},{5,8},{6,9},{7,10},{8,11},{9,12},{10... | collective-permute-start | bytes 184328 | tf_op jit(solution)/shard_map/ppermute | solution.py:655
  59.7 3.9 %collective-permute-start.11 = (bf16[3,80,128]{2,1,0:T(8,128)(2,1)S(1)}, bf16[3,80,128]{2,1,0:T(8,128)(2,1)S(1)}, u32[]{:S(2)}, u32[]{:S(2)}) collective-permute-start(bf16[3,80,128]{2,1,0:T(8,128)(2,1)S(1)} %pad_maximum_fusion), channel_id=1, source_target_pairs={{0,13},{1,14},{2,15},{3,0},{4,1},{5,2},{6,3},{7,4},{8,5},{9,6},{10... | collective-permute-start | bytes 184328 | tf_op jit(solution)/shard_map/ppermute | solution.py:655

commit v6 on v5

--- a/solution.py
+++ b/solution.py
@@ -24,6 +24,8 @@
 BODY = 64
 TAILS = (MARK + 1 - BODY) * CAP
 MESSAGE = CAP * BODY + TAILS
+SOURCE_PARTS = 3
+SOURCE_ROWS = CHANNELS * ROWS // SOURCE_PARTS
 EPSILON = 1e-05
 VMEM_LIMIT = 40 * 1024 * 1024
 REGRID_VMEM = 60 * 1024 * 1024
@@ -72,12 +74,17 @@
     column, position = split(tile, column_rows)
 
     target_copy = pltpu.make_async_copy(target_hbm, target_ref, in_sems.at[0])
-    source_copy = pltpu.make_async_copy(source_hbm, source, in_sems.at[1])
-    index_copy = pltpu.make_async_copy(index_hbm, index_ref, in_sems.at[2])
+    index_copy = pltpu.make_async_copy(index_hbm, index_ref, in_sems.at[1])
     target_copy.start()
-    source_copy.start()
+    source_copies = []
+    for part in range(SOURCE_PARTS):
+        rows = pl.ds(part * SOURCE_ROWS, SOURCE_ROWS)
+        source_copies.append(
+            pltpu.make_async_copy(source_hbm.at[rows], source.at[rows], in_sems.at[3 + part])
+        )
+        source_copies[-1].start()
     index_copy.start()
-    weight_copy = pltpu.make_async_copy(weight_hbm, weight, in_sems.at[3])
+    weight_copy = pltpu.make_async_copy(weight_hbm, weight, in_sems.at[2])
     weight_copy.start()
 
     target_copy.wait()
@@ -111,8 +118,10 @@
         ((PADDED - CHANNELS) * ROWS, BLOCK), jnp.float32
     )
     nothing = jnp.zeros((WIDE - PADDED, BLOCK), jnp.float32)
-    source_copy.wait()
-    wide[pl.ds(0, CHANNELS * ROWS), :] = source[...].astype(jnp.float32)
+    for part, copy in enumerate(source_copies):
+        copy.wait()
+        rows = pl.ds(part * SOURCE_ROWS, SOURCE_ROWS)
+        wide[rows, :] = source[rows, :].astype(jnp.float32)
     for row in range(ROWS):
         block = wide[pl.ds(row, PADDED, stride=ROWS), :]
         field[row] = jnp.concatenate([block, nothing], axis=0).astype(jnp.bfloat16)
@@ -149,13 +158,8 @@
         start = group * CAP * 8
         ends = [tails[pl.ds(start + at, CAP, stride=8), :] for at in range(MARK + 1 - BODY)]
         message[group, CAP * BODY :] = jnp.concatenate(ends, axis=0).astype(jnp.bfloat16)
-        if group == TILE_COLS - 1:
-            source_part, out = message.at[pl.ds(0, TILE_COLS)], same_out
-        elif group >= TILE_COLS:
-            source_part, out = message.at[group], next_outs[group - TILE_COLS]
-        else:
-            continue
-        copies.append(pltpu.make_async_copy(source_part, out, out_sems.at[len(copies)]))
+        out = same_out.at[group] if group < TILE_COLS else next_outs[group - TILE_COLS]
+        copies.append(pltpu.make_async_copy(message.at[group], out, out_sems.at[group]))
         copies[-1].start()
     for copy in copies:
         copy.wait()
@@ -184,25 +188,27 @@
             pltpu.VMEM((1, entries), jnp.int32),
             pltpu.SMEM((1, entries), jnp.int32),
             pltpu.SemaphoreType.DMA,
-            pltpu.SemaphoreType.DMA((4,)),
-            pltpu.SemaphoreType.DMA((1 + TILE_COLS,)),
+            pltpu.SemaphoreType.DMA((3 + SOURCE_PARTS,)),
+            pltpu.SemaphoreType.DMA((GROUPS,)),
         ],
         compiler_params=pltpu.CompilerParams(vmem_limit_bytes=REGRID_VMEM),
         name="regrid",
     )(target.reshape(1, -1), source_index, field, weights)
 
 
+def normalized(rounded, gain):
+    value = rounded.astype(jnp.float32)
+    real = lax.broadcasted_iota(jnp.int32, (PADDED - BODY, BLOCK), 0) < CHANNELS - BODY
+    value = jnp.concatenate([value[:BODY], jnp.where(real, value[BODY:], 0.0)], axis=0)
+    square = jnp.sum(value * value, axis=0, keepdims=True) * (1.0 / CHANNELS)
+    scaled = value * lax.rsqrt(square + EPSILON) * gain
+    nothing = jnp.zeros((WIDE - PADDED, BLOCK), jnp.float32)
+    return jnp.concatenate([scaled, nothing], axis=0).astype(jnp.bfloat16)
+
+
 def gather_kernel(column_rows, flip_ref, gain_ref, same, *rest):
     nexts = rest[:TILE_COLS]
-    (
-        gridded,
-        normed,
-        upward,
-        downward,
-        strip_out,
-        summed,
-        tails,
-    ) = rest[TILE_COLS:]
+    summed, upward, downward, strip_out, tails = rest[TILE_COLS:]
     position = lax.rem(lax.axis_index("tile"), column_rows)
     summed[...] = jnp.zeros_like(summed)
 
@@ -227,28 +233,20 @@
             add(TILE_COLS + group, nexts[group])
 
     gain = gain_ref[...]
-    real = lax.broadcasted_iota(jnp.int32, (PADDED - BODY, BLOCK), 0) < CHANNELS - BODY
-    nothing = jnp.zeros((WIDE - PADDED, BLOCK), jnp.float32)
-    lane = lanes((WIDE, BLOCK))
-    strip = jnp.zeros((WIDE, BLOCK), jnp.bfloat16)
+    for at in range(2):
+        upward[at] = normalized(summed[at].astype(jnp.bfloat16), gain)
+        downward[at] = normalized(summed[ROWS - 2 + at].astype(jnp.bfloat16), gain)
+    lane = lanes((PADDED, BLOCK))
+    strip = jnp.zeros((PADDED, BLOCK), jnp.bfloat16)
     for row in range(ROWS):
         rounded = summed[row].astype(jnp.bfloat16)
-        gridded[row] = rounded
-        value = rounded.astype(jnp.float32)
-        value = jnp.concatenate([value[:BODY], jnp.where(real, value[BODY:], 0.0)], axis=0)
-        square = jnp.sum(value * value, axis=0, keepdims=True) * (1.0 / CHANNELS)
-        scaled = value * lax.rsqrt(square + EPSILON) * gain
-        scaled = jnp.concatenate([scaled, nothing], axis=0).astype(jnp.bfloat16)
-        normed[row] = scaled
-        if row < 2:
-            upward[row] = scaled
-        if row >= ROWS - 2:
-            downward[row - ROWS + 2] = scaled
-        strip = jnp.where((lane >> 2) == row, pltpu.roll(scaled, 4 * row + 2, 1), strip)
+        strip = jnp.where((lane >> 2) == row, pltpu.roll(rounded, 4 * row + 2, 1), strip)
     to_lane = lanes((BLOCK, BLOCK))
     from_lane = 4 * (to_lane & (ROWS - 1)) + (((to_lane >> ROW_BITS) + 2) & 3)
     order = lax.broadcasted_iota(jnp.int32, (BLOCK, BLOCK), 0) == from_lane
-    strip = jnp.dot(strip, order.astype(jnp.bfloat16), preferred_element_type=jnp.float32)
+    strip = jnp.dot(
+        normalized(strip, gain), order.astype(jnp.bfloat16), preferred_element_type=jnp.float32
+    )
     channel = lax.broadcasted_iota(jnp.int32, (WIDE, BLOCK), 0)
     for side in range(2):
         strip = jnp.where(channel == CHANNELS + side, flip_ref[0, side].astype(jnp.float32), strip)
@@ -258,6 +256,29 @@
     strip_out[...] = strip
 
 
+def normalize_kernel(gain_ref, summed, gridded, normed):
+    gain = gain_ref[...]
+    for row in range(ROWS):
+        rounded = summed[row].astype(jnp.bfloat16)
+        gridded[row] = rounded
+        normed[row] = normalized(rounded, gain)
+
+
+def normalize_rows(gain, summed):
+    return pl.pallas_call(
+        normalize_kernel,
+        in_specs=[vmem()] * 2,
+        out_specs=[vmem()] * 2,
+        out_shape=[GRIDDED, FIELD],
+        compiler_params=pltpu.CompilerParams(vmem_limit_bytes=VMEM_LIMIT),
+        cost_estimate=pl.CostEstimate(
+            flops=10 * ROWS * PADDED * BLOCK, bytes_accessed=2 << 20, transcendentals=0
+        ),
+        name="normalize_rows",
+    )(gain, summed)
+
+
+SUMMED = jax.ShapeDtypeStruct((ROWS + 1, PADDED, BLOCK), jnp.float32)
 GRIDDED = jax.ShapeDtypeStruct((ROWS, PADDED, BLOCK), jnp.bfloat16)
 FIELD = jax.ShapeDtypeStruct((ROWS, WIDE, BLOCK), jnp.bfloat16)
 RIM = jax.ShapeDtypeStruct((3, WIDE, BLOCK), jnp.bfloat16)
@@ -269,12 +290,9 @@
     return pl.pallas_call(
         functools.partial(gather_kernel, column_rows),
         in_specs=[smem()] + [vmem()] * (2 + TILE_COLS),
-        out_specs=[vmem()] * 5,
-        out_shape=[GRIDDED, FIELD, RIM, RIM, STRIP],
-        scratch_shapes=[
-            pltpu.VMEM((ROWS + 1, PADDED, BLOCK), jnp.float32),
-            pltpu.VMEM((GROUPS, 8 * CAP, BLOCK), jnp.float32),
-        ],
+        out_specs=[vmem()] * 4,
+        out_shape=[SUMMED, RIM, RIM, STRIP],
+        scratch_shapes=[pltpu.VMEM((GROUPS, 8 * CAP, BLOCK), jnp.float32)],
         compiler_params=pltpu.CompilerParams(vmem_limit_bytes=VMEM_LIMIT),
         name="gather_rows",
     )(edge_flip, gain, same, *nexts)
@@ -689,18 +707,17 @@
     same, nexts, gain, first_taps, second_taps = lax.optimization_barrier(
         (same, nexts, gain, first_taps, second_taps)
     )
-    gridded, normed, upward, downward, strip = gather_rows(
-        column_rows, edge_flip, gain, same, nexts
-    )
+    summed, upward, downward, strip = gather_rows(column_rows, edge_flip, gain, same, nexts)
     rims = [from_shift(downward, -1), from_shift(upward, 1)]
     near, far, reach = strip_plan(column_rows)
     strips = [from_shift(strip, shift) for shift in near]
+    gridded, normed = normalize_rows(gain, summed)
     inner = inner_convolution(first_taps, normed)
     held = {-1: rims[0][2], 0: strip, 1: rims[1][2], **dict(zip(near, strips))}
     pack = jnp.stack([held[at] for at in range(-reach, reach + 1)])
+    pack, inner = lax.optimization_barrier((pack, inner))
+    strips += [from_shift(pack, -far), from_shift(pack, far)]
     gridded_out = channels_first(gridded)
-    pack, inner, gridded_out = lax.optimization_barrier((pack, inner, gridded_out))
-    strips += [from_shift(pack, -far), from_shift(pack, far)]
     hidden, *unfinished = inner
     base = inner_second_convolution(second_taps, hidden, gridded)
     smoothed = convolutions(

time: 67.6 us -> 67.5 us (level)
  transfers between devices with their start and end apart: 13 -> 13, of which waited for: 6 -> 5; matrix products, arithmetic and copies ran while one was open for 1% -> 1% of each run, Pallas kernels for 6% -> 6%
where the time goes in v6:
time: 67.5 us; the launch traced here: 66.8 us
  waiting for transfers between devices  28.8 us (43%)
  starting transfers between devices  21.9 us (32%)
  Pallas kernels  14.4 us (21%)
  between operations  1 us (1%)
  local copies, waits for them, and re-layouts  0.71 us (1%)
    ppermute x8, waiting for transfers between devices, per_device(): nexts[across] = lax.ppermute(nexts[across], 'tile', pairs)  27.1 us
    ppermute x8, starting transfers between devices, per_device(): nexts[across] = lax.ppermute(nexts[across], 'tile', pairs)  10.3 us
    all_to_all x1, starting transfers between devices, per_device(): lax.all_to_all(same, 'tile', 0, 0, axis_index_groups=[[c * column_rows +...  6.55 us
    pallas_call x1, Pallas kernels, regrid(): pl.pallas_call(functools.partial(regrid_kernel, column_rows), in_specs=[h...  5.14 us
    ppermute x4, starting transfers between devices, from_shift(): lax.ppermute(value, 'tile', [(i, (i - shift) % count) for i in range(coun...  5.05 us
    pallas_call x1, Pallas kernels, convolutions(): pl.pallas_call(functools.partial(conv_kernel, column_rows), in_specs=[vme...  3.14 us
    pallas_call x1, Pallas kernels, channels_first(): pl.pallas_call(turn_kernel, in_specs=[vmem()], out_specs=vmem(), out_shap...  1.98 us
    pallas_call x1, Pallas kernels, gather_rows(): pl.pallas_call(functools.partial(gather_kernel, column_rows), in_specs=[s...  1.8 us
  transfers between devices with their start and end apart: 13, of which 5 were waited for; matrix products, arithmetic and copies ran while one was open for 1% of the time, Pallas kernels for 6%

profile of v6, /device:TPU:1, one launch (start us, length us, event | category | flops | bytes accessed | tf_op | source)
XLA Modules:
  0.0 66.8 jit_solution(8452302591818744527)
XLA Ops:
  0.6 5.1 %regrid.1 = (bf16[8,560,128]{2,1,0:T(8,128)(2,1)}, bf16[560,128]{1,0:T(8,128)(2,1)}, bf16[560,128]{1,0:T(8,128)(2,1)}, bf16[560,128]{1,0:T(8,128)(2,1)}, bf16[56...) custom-call(s32[1,96]{1,0:T(1,128)} %bitcast.31, ...), custom_call_target="tpu_custom_call" | custom-call | tf_op jit(solution)/shard_map/regrid/pallas_call | solution.py:173
  5.8 0.0 copy-start.9
  5.8 0.0 copy-start.8
  5.8 0.0 copy-start.7
  5.8 0.0 copy-start.6
  5.8 0.0 copy-start.5
  5.8 0.0 copy-start.4
  5.8 0.0 copy-start.3
  5.9 0.0 copy-start.1
  5.9 0.0 copy-start.2
  5.9 6.5 %all-to-all-start = ((bf16[8,560,128]{2,1,0:T(8,128)(2,1)}), bf16[8,560,128]{2,1,0:T(8,128)(2,1)S(1)}, u32[]{:S(2)}, u32[]{:S(2)}) async-start(bf16[8,560,128]{2,1,0:T(8,128)(2,1)} %get-tuple-element.36), calls=%async_computation | async-start | bytes 2293760 | tf_op jit(solution)/shard_map/all_to_all | solution.py:692
  12.4 0.0 copy-start
  12.4 1.3 %collective-permute-start = (bf16[560,128]{1,0:T(8,128)(2,1)S(1)}, bf16[560,128]{1,0:T(8,128)(2,1)S(1)}, u32[]{:S(2)}, u32[]{:S(2)}) collective-permute-start(bf16[560,128]{1,0:T(8,128)(2,1)S(1)} %copy-done.9), channel_id=1, source_target_pairs={{0,1},{2,3},{4,5},{6,7},{8,9},{10,11},{12,13},{14,15},{16,17},{18,... | collective-permute-start | bytes 430088 | tf_op jit(solution)/shard_map/ppermute | solution.py:690
  13.8 1.3 %collective-permute-start.1 = (bf16[560,128]{1,0:T(8,128)(2,1)S(1)}, bf16[560,128]{1,0:T(8,128)(2,1)S(1)}, u32[]{:S(2)}, u32[]{:S(2)}) collective-permute-start(bf16[560,128]{1,0:T(8,128)(2,1)S(1)} %copy-done.8), channel_id=1, source_target_pairs={{0,3},{2,1},{4,7},{6,5},{8,11},{10,9},{12,15},{14,13},{16,19},{18,... | collective-permute-start | bytes 430088 | tf_op jit(solution)/shard_map/ppermute | solution.py:690
  15.1 1.3 %collective-permute-start.2 = (bf16[560,128]{1,0:T(8,128)(2,1)S(1)}, bf16[560,128]{1,0:T(8,128)(2,1)S(1)}, u32[]{:S(2)}, u32[]{:S(2)}) collective-permute-start(bf16[560,128]{1,0:T(8,128)(2,1)S(1)} %copy-done.7), channel_id=1, source_target_pairs={{0,5},{2,7},{4,1},{6,3},{8,13},{10,15},{12,9},{14,11},{16,21},{18,... | collective-permute-start | bytes 430088 | tf_op jit(solution)/shard_map/ppermute | solution.py:690
  16.4 1.3 %collective-permute-start.3 = (bf16[560,128]{1,0:T(8,128)(2,1)}, bf16[560,128]{1,0:T(8,128)(2,1)S(1)}, u32[]{:S(2)}, u32[]{:S(2)}) collective-permute-start(bf16[560,128]{1,0:T(8,128)(2,1)} %get-tuple-element.40), channel_id=1, source_target_pairs={{0,9},{2,11},{4,13},{6,15},{8,1},{10,3},{12,5},{14,7},{16,25},{18,... | collective-permute-start | bytes 430088 | tf_op jit(solution)/shard_map/ppermute | solution.py:690
  17.7 1.3 %collective-permute-start.4 = (bf16[560,128]{1,0:T(8,128)(2,1)S(1)}, bf16[560,128]{1,0:T(8,128)(2,1)S(1)}, u32[]{:S(2)}, u32[]{:S(2)}) collective-permute-start(bf16[560,128]{1,0:T(8,128)(2,1)S(1)} %copy-done.6), channel_id=1, source_target_pairs={{0,11},{2,9},{4,15},{6,13},{8,3},{10,1},{12,7},{14,5},{16,27},{18,... | collective-permute-start | bytes 430088 | tf_op jit(solution)/shard_map/ppermute | solution.py:690
  19.0 0.0 collective-permute-done.rest_0_
  19.0 1.3 %collective-permute-start.5 = (bf16[560,128]{1,0:T(8,128)(2,1)S(1)}, bf16[560,128]{1,0:T(8,128)(2,1)S(1)}, u32[]{:S(2)}, u32[]{:S(2)}) collective-permute-start(bf16[560,128]{1,0:T(8,128)(2,1)S(1)} %copy-done.5), channel_id=1, source_target_pairs={{0,13},{2,15},{4,9},{6,11},{8,5},{10,7},{12,1},{14,3},{16,29},{18,... | collective-permute-start | bytes 430088 | tf_op jit(solution)/shard_map/ppermute | solution.py:690
  20.3 2.7 %collective-permute-done.1.rest_1_ = bf16[560,128]{1,0:T(8,128)(2,1)S(1)} collective-permute-done((bf16[560,128]{1,0:T(8,128)(2,1)S(1)}, bf16[560,128]{1,0:T(8,128)(2,1)S(1)}, u32[]{:S(2)}, u32[]{:S(2)}) %collective-permute-start.1) | collective-permute-done | bytes 143392 | tf_op jit(solution)/shard_map/ppermute | solution.py:690
  23.0 1.3 %collective-permute-start.6 = (bf16[560,128]{1,0:T(8,128)(2,1)S(1)}, bf16[560,128]{1,0:T(8,128)(2,1)S(1)}, u32[]{:S(2)}, u32[]{:S(2)}) collective-permute-start(bf16[560,128]{1,0:T(8,128)(2,1)S(1)} %copy-done.4), channel_id=1, source_target_pairs={{0,15},{2,13},{4,11},{6,9},{8,7},{10,5},{12,3},{14,1},{16,31},{18,... | collective-permute-start | bytes 430088 | tf_op jit(solution)/shard_map/ppermute | solution.py:690
  24.3 8.0 %collective-permute-done.2.rest_2_ = bf16[560,128]{1,0:T(8,128)(2,1)S(1)} collective-permute-done((bf16[560,128]{1,0:T(8,128)(2,1)S(1)}, bf16[560,128]{1,0:T(8,128)(2,1)S(1)}, u32[]{:S(2)}, u32[]{:S(2)}) %collective-permute-start.2) | collective-permute-done | bytes 143392 | tf_op jit(solution)/shard_map/ppermute | solution.py:690
  32.3 1.3 %collective-permute-start.7 = (bf16[560,128]{1,0:T(8,128)(2,1)S(1)}, bf16[560,128]{1,0:T(8,128)(2,1)S(1)}, u32[]{:S(2)}, u32[]{:S(2)}) collective-permute-start(bf16[560,128]{1,0:T(8,128)(2,1)S(1)} %copy-done.3), channel_id=1, source_target_pairs={{0,7},{2,5},{4,3},{6,1},{8,15},{10,13},{12,11},{14,9},{16,23},{18,... | collective-permute-start | bytes 430088 | tf_op jit(solution)/shard_map/ppermute | solution.py:690
  33.6 0.1 copy.17
  33.7 0.2 reshape.33.taps_ref.first_taps_ref
  33.9 0.1 copy.16
  34.1 0.2 reshape.35.taps_ref.second_taps_ref
  34.2 14.0 %collective-permute-done.3.rest_3_ = bf16[560,128]{1,0:T(8,128)(2,1)S(1)} collective-permute-done((bf16[560,128]{1,0:T(8,128)(2,1)}, bf16[560,128]{1,0:T(8,128)(2,1)S(1)}, u32[]{:S(2)}, u32[]{:S(2)}) %collective-permute-start.3) | collective-permute-done | bytes 143392 | tf_op jit(solution)/shard_map/ppermute | solution.py:690
  48.2 2.4 %collective-permute-done.4.rest_4_ = bf16[560,128]{1,0:T(8,128)(2,1)S(1)} collective-permute-done((bf16[560,128]{1,0:T(8,128)(2,1)S(1)}, bf16[560,128]{1,0:T(8,128)(2,1)S(1)}, u32[]{:S(2)}, u32[]{:S(2)}) %collective-permute-start.4) | collective-permute-done | bytes 143392 | tf_op jit(solution)/shard_map/ppermute | solution.py:690
  50.7 0.0 collective-permute-done.5.rest_5_
  50.7 0.0 collective-permute-done.6.rest_6_
  50.7 0.0 collective-permute-done.7.rest_7_
  50.7 0.0 all-to-all-done.same
  50.7 0.1 broadcast_in_dim.12.gain_ref
  50.8 1.8 %gather_rows.1 = (f32[33,72,128]{2,1,0:T(8,128)S(1)}, bf16[3,80,128]{2,1,0:T(8,128)(2,1)S(1)}, bf16[3,80,128]{2,1,0:T(8,128)(2,1)S(1)}, bf16[80,128]{1,0:T(8,128)(2,1)S(1)}) custom-call(s32[1,2]{1,0:T(1,128)S(1)} %copy-done, f32[72,128]{1,0:T(8,128)S(1)} %broadcast_in_dim.12.gain_ref, bf16[8,560,128]{2,1,0:T(8,128)(2,1)S(1)} %all-to-all-done.same, ...), custom_call_target="tpu_custom_call" | custom-call | tf_op jit(solution)/shard_map/gather_rows/pallas_call | solution.py:290
  52.6 0.1 collective-permute-start.8
  52.6 0.5 collective-permute-start.9
  53.1 0.3 normalize_rows.1
  53.5 1.2 %inner_convolution.1 = (bf16[32,80,128]{2,1,0:T(8,128)(2,1)S(1)}, f32[2,80,128]{2,1,0:T(8,128)S(1)}, f32[2,80,128]{2,1,0:T(8,128)S(1)}) custom-call(bf16[240,240]{1,0:T(8,128)(2,1)S(1)} %reshape.33.taps_ref.first_taps_ref, bf16[32,80,128]{2,1,0:T(8,128)(2,1)S(1)} %get-tuple-element.59.field), custom_call_target="tpu_custom_call" | custom-call | flops 471859200 | bytes 2097152 | tf_op jit(solution)/shard_map/inner_convolution/pallas_call | solution.py:374
  54.7 0.0 collective-permute-done.8.above
  54.7 1.7 %collective-permute-done.9.below = bf16[3,80,128]{2,1,0:T(8,128)(2,1)S(1)} collective-permute-done((bf16[3,80,128]{2,1,0:T(8,128)(2,1)S(1)}, bf16[3,80,128]{2,1,0:T(8,128)(2,1)S(1)}, u32[]{:S(2)}, u32[]{:S(2)}) %collective-permute-start.9) | collective-permute-done | bytes 61472 | tf_op jit(solution)/shard_map/ppermute | solution.py:673
  56.4 1.9 %collective-permute-start.10 = (bf16[3,80,128]{2,1,0:T(8,128)(2,1)S(1)}, bf16[3,80,128]{2,1,0:T(8,128)(2,1)S(1)}, u32[]{:S(2)}, u32[]{:S(2)}) collective-permute-start(bf16[3,80,128]{2,1,0:T(8,128)(2,1)S(1)} %pad_maximum_fusion), channel_id=1, source_target_pairs={{0,3},{1,4},{2,5},{3,6},{4,7},{5,8},{6,9},{7,10},{8,11},{9,12},{10... | collective-permute-start | bytes 184328 | tf_op jit(solution)/shard_map/ppermute | solution.py:673
  58.3 2.5 %collective-permute-start.11 = (bf16[3,80,128]{2,1,0:T(8,128)(2,1)S(1)}, bf16[3,80,128]{2,1,0:T(8,128)(2,1)S(1)}, u32[]{:S(2)}, u32[]{:S(2)}) collective-permute-start(bf16[3,80,128]{2,1,0:T(8,128)(2,1)S(1)} %pad_maximum_fusion), channel_id=1, source_target_pairs={{0,13},{1,14},{2,15},{3,0},{4,1},{5,2},{6,3},{7,4},{8,5},{9,6},{10... | collective-permute-start | bytes 184328 | tf_op jit(solution)/shard_map/ppermute | solution.py:673
  60.9 2.0 %channels_first.1 = bf16[2208,128]{1,0:T(8,128)(2,1)} custom-call(bf16[32,72,128]{2,1,0:T(8,128)(2,1)S(1)} %get-tuple-element.56.field.gridded), custom_call_target="tpu_custom_call" | custom-call | tf_op jit(solution)/shard_map/channels_first/pallas_call | solution.py:308
  62.8 0.8 %inner_second_convolution.1.base = f32[32,72,128]{2,1,0:T(8,128)S(1)} custom-call(bf16[240,240]{1,0:T(8,128)(2,1)S(1)} %reshape.35.taps_ref.second_taps_ref, bf16[32,80,128]{2,1,0:T(8,128)(2,1)S(1)} %get-tuple-element.66.hidden, bf16[32,72,128]{2,1,0:T(8,128)(2,1)S(1)} %get-tuple-element.56.field.gridded), custom_call_target="tpu_custom_call" | custom-call | flops 471859200 | bytes 2097152 | tf_op jit(solution)/shard_map/inner_second_convolution/pallas_call | solution.py:407
  63.6 0.0 collective-permute-done.10.rest_0_
  63.6 0.0 collective-permute-done.11.rest_1_
  63.7 3.1 %convolutions.1 = bf16[69,32,128]{2,1,0:T(8,128)(2,1)} custom-call(bf16[240,240]{1,0:T(8,128)(2,1)S(1)} %reshape.33.taps_ref.first_taps_ref, bf16[240,240]{1,0:T(8,128)(2,1)S(1)} %reshape.35.taps_ref.second_taps_ref, bf16[32,80,128]{2,1,0:T(8,128)(2,1)S(1)} %get-tuple-element.59.field, f32[32,72,128]{2,1,0:T(8,128)S(1)} %inner_second_convolution.1.base, ...), custom_call_target="tpu_custom_call" | custom-call | tf_op jit(solution)/shard_map/convolutions/pallas_call | solution.py:650
  (18 shorter events, 0.1 us)
Async XLA Ops:
  5.8 6.7 %copy-start.9 = (bf16[560,128]{1,0:T(8,128)(2,1)S(1)}, bf16[560,128]{1,0:T(8,128)(2,1)}, u32[]{:S(2)}) copy-start(bf16[560,128]{1,0:T(8,128)(2,1)} %get-tuple-element.37) | copy-start | bytes 430084
  5.8 8.0 %copy-start.8 = (bf16[560,128]{1,0:T(8,128)(2,1)S(1)}, bf16[560,128]{1,0:T(8,128)(2,1)}, u32[]{:S(2)}) copy-start(bf16[560,128]{1,0:T(8,128)(2,1)} %get-tuple-element.38) | copy-start | bytes 430084
  5.8 9.3 %copy-start.7 = (bf16[560,128]{1,0:T(8,128)(2,1)S(1)}, bf16[560,128]{1,0:T(8,128)(2,1)}, u32[]{:S(2)}) copy-start(bf16[560,128]{1,0:T(8,128)(2,1)} %get-tuple-element.39) | copy-start | bytes 430084
  5.8 11.9 %copy-start.6 = (bf16[560,128]{1,0:T(8,128)(2,1)S(1)}, bf16[560,128]{1,0:T(8,128)(2,1)}, u32[]{:S(2)}) copy-start(bf16[560,128]{1,0:T(8,128)(2,1)} %get-tuple-element.41) | copy-start | bytes 430084
  5.8 13.2 %copy-start.5 = (bf16[560,128]{1,0:T(8,128)(2,1)S(1)}, bf16[560,128]{1,0:T(8,128)(2,1)}, u32[]{:S(2)}) copy-start(bf16[560,128]{1,0:T(8,128)(2,1)} %get-tuple-element.42) | copy-start | bytes 430084
  5.8 17.1 %copy-start.4 = (bf16[560,128]{1,0:T(8,128)(2,1)S(1)}, bf16[560,128]{1,0:T(8,128)(2,1)}, u32[]{:S(2)}) copy-start(bf16[560,128]{1,0:T(8,128)(2,1)} %get-tuple-element.43) | copy-start | bytes 430084
  5.8 26.4 %copy-start.3 = (bf16[560,128]{1,0:T(8,128)(2,1)S(1)}, bf16[560,128]{1,0:T(8,128)(2,1)}, u32[]{:S(2)}) copy-start(bf16[560,128]{1,0:T(8,128)(2,1)} %get-tuple-element.44) | copy-start | bytes 430084
  5.9 27.7 %copy-start.1 = (bf16[9,69,69]{2,1,0:T(8,128)(2,1)S(1)}, bf16[9,69,69]{2,1,0:T(8,128)(2,1)}, u32[]{:S(2)}) copy-start(bf16[9,69,69]{2,1,0:T(8,128)(2,1)} %param.14) | copy-start | bytes 257098
  5.9 28.0 %copy-start.2 = (bf16[9,69,69]{2,1,0:T(8,128)(2,1)S(1)}, bf16[9,69,69]{2,1,0:T(8,128)(2,1)}, u32[]{:S(2)}) copy-start(bf16[9,69,69]{2,1,0:T(8,128)(2,1)} %param.15) | copy-start | bytes 257098
  5.9 44.8 %all-to-all-start = ((bf16[8,560,128]{2,1,0:T(8,128)(2,1)}), bf16[8,560,128]{2,1,0:T(8,128)(2,1)S(1)}, u32[]{:S(2)}, u32[]{:S(2)}) async-start(bf16[8,560,128]{2,1,0:T(8,128)(2,1)} %get-tuple-element.36), calls=%async_computation | async-start | bytes 2293760 | tf_op jit(solution)/shard_map/all_to_all | solution.py:692
  12.4 21.8 %copy-start.10 = (f32[69]{0:T(128)S(1)}, f32[69]{0:T(128)}, u32[]{:S(2)}) copy-start(f32[69]{0:T(128)} %param.13) | copy-start | bytes 832
  12.4 38.3 %copy-start = (s32[1,2]{1,0:T(1,128)S(1)}, s32[1,2]{1,0:T(1,128)}, u32[]{:S(2)}) copy-start(s32[1,2]{1,0:T(1,128)} %flip_ref.1) | copy-start | bytes 28
  12.4 6.5 %collective-permute-start = (bf16[560,128]{1,0:T(8,128)(2,1)S(1)}, bf16[560,128]{1,0:T(8,128)(2,1)S(1)}, u32[]{:S(2)}, u32[]{:S(2)}) collective-permute-start(bf16[560,128]{1,0:T(8,128)(2,1)S(1)} %copy-done.9), channel_id=1, source_target_pairs={{0,1},{2,3},{4,5},{6,7},{8,9},{10,11},{12,13},{14,15},{16,17},{18,... | collective-permute-start | bytes 430088 | tf_op jit(solution)/shard_map/ppermute | solution.py:690
  13.8 9.2 %collective-permute-start.1 = (bf16[560,128]{1,0:T(8,128)(2,1)S(1)}, bf16[560,128]{1,0:T(8,128)(2,1)S(1)}, u32[]{:S(2)}, u32[]{:S(2)}) collective-permute-start(bf16[560,128]{1,0:T(8,128)(2,1)S(1)} %copy-done.8), channel_id=1, source_target_pairs={{0,3},{2,1},{4,7},{6,5},{8,11},{10,9},{12,15},{14,13},{16,19},{18,... | collective-permute-start | bytes 430088 | tf_op jit(solution)/shard_map/ppermute | solution.py:690
  15.1 17.2 %collective-permute-start.2 = (bf16[560,128]{1,0:T(8,128)(2,1)S(1)}, bf16[560,128]{1,0:T(8,128)(2,1)S(1)}, u32[]{:S(2)}, u32[]{:S(2)}) collective-permute-start(bf16[560,128]{1,0:T(8,128)(2,1)S(1)} %copy-done.7), channel_id=1, source_target_pairs={{0,5},{2,7},{4,1},{6,3},{8,13},{10,15},{12,9},{14,11},{16,21},{18,... | collective-permute-start | bytes 430088 | tf_op jit(solution)/shard_map/ppermute | solution.py:690
  16.4 31.9 %collective-permute-start.3 = (bf16[560,128]{1,0:T(8,128)(2,1)}, bf16[560,128]{1,0:T(8,128)(2,1)S(1)}, u32[]{:S(2)}, u32[]{:S(2)}) collective-permute-start(bf16[560,128]{1,0:T(8,128)(2,1)} %get-tuple-element.40), channel_id=1, source_target_pairs={{0,9},{2,11},{4,13},{6,15},{8,1},{10,3},{12,5},{14,7},{16,25},{18,... | collective-permute-start | bytes 430088 | tf_op jit(solution)/shard_map/ppermute | solution.py:690
  17.7 33.0 %collective-permute-start.4 = (bf16[560,128]{1,0:T(8,128)(2,1)S(1)}, bf16[560,128]{1,0:T(8,128)(2,1)S(1)}, u32[]{:S(2)}, u32[]{:S(2)}) collective-permute-start(bf16[560,128]{1,0:T(8,128)(2,1)S(1)} %copy-done.6), channel_id=1, source_target_pairs={{0,11},{2,9},{4,15},{6,13},{8,3},{10,1},{12,7},{14,5},{16,27},{18,... | collective-permute-start | bytes 430088 | tf_op jit(solution)/shard_map/ppermute | solution.py:690
  19.0 31.7 %collective-permute-start.5 = (bf16[560,128]{1,0:T(8,128)(2,1)S(1)}, bf16[560,128]{1,0:T(8,128)(2,1)S(1)}, u32[]{:S(2)}, u32[]{:S(2)}) collective-permute-start(bf16[560,128]{1,0:T(8,128)(2,1)S(1)} %copy-done.5), channel_id=1, source_target_pairs={{0,13},{2,15},{4,9},{6,11},{8,5},{10,7},{12,1},{14,3},{16,29},{18,... | collective-permute-start | bytes 430088 | tf_op jit(solution)/shard_map/ppermute | solution.py:690
  23.0 27.7 %collective-permute-start.6 = (bf16[560,128]{1,0:T(8,128)(2,1)S(1)}, bf16[560,128]{1,0:T(8,128)(2,1)S(1)}, u32[]{:S(2)}, u32[]{:S(2)}) collective-permute-start(bf16[560,128]{1,0:T(8,128)(2,1)S(1)} %copy-done.4), channel_id=1, source_target_pairs={{0,15},{2,13},{4,11},{6,9},{8,7},{10,5},{12,3},{14,1},{16,31},{18,... | collective-permute-start | bytes 430088 | tf_op jit(solution)/shard_map/ppermute | solution.py:690
  32.3 18.4 %collective-permute-start.7 = (bf16[560,128]{1,0:T(8,128)(2,1)S(1)}, bf16[560,128]{1,0:T(8,128)(2,1)S(1)}, u32[]{:S(2)}, u32[]{:S(2)}) collective-permute-start(bf16[560,128]{1,0:T(8,128)(2,1)S(1)} %copy-done.3), channel_id=1, source_target_pairs={{0,7},{2,5},{4,3},{6,1},{8,15},{10,13},{12,11},{14,9},{16,23},{18,... | collective-permute-start | bytes 430088 | tf_op jit(solution)/shard_map/ppermute | solution.py:690
  52.6 2.1 %collective-permute-start.8 = (bf16[3,80,128]{2,1,0:T(8,128)(2,1)S(1)}, bf16[3,80,128]{2,1,0:T(8,128)(2,1)S(1)}, u32[]{:S(2)}, u32[]{:S(2)}) collective-permute-start(bf16[3,80,128]{2,1,0:T(8,128)(2,1)S(1)} %get-tuple-element.60), channel_id=1, source_target_pairs={{0,1},{1,2},{2,3},{3,4},{4,5},{5,6},{6,7},{7,8},{8,9},{9,10},{10,1... | collective-permute-start | bytes 184328 | tf_op jit(solution)/shard_map/ppermute | solution.py:673
  52.6 3.7 %collective-permute-start.9 = (bf16[3,80,128]{2,1,0:T(8,128)(2,1)S(1)}, bf16[3,80,128]{2,1,0:T(8,128)(2,1)S(1)}, u32[]{:S(2)}, u32[]{:S(2)}) collective-permute-start(bf16[3,80,128]{2,1,0:T(8,128)(2,1)S(1)} %get-tuple-element.62), channel_id=1, source_target_pairs={{0,15},{1,0},{2,1},{3,2},{4,3},{5,4},{6,5},{7,6},{8,7},{9,8},{10,9... | collective-permute-start | bytes 184328 | tf_op jit(solution)/shard_map/ppermute | solution.py:673
  56.4 7.3 %collective-permute-start.10 = (bf16[3,80,128]{2,1,0:T(8,128)(2,1)S(1)}, bf16[3,80,128]{2,1,0:T(8,128)(2,1)S(1)}, u32[]{:S(2)}, u32[]{:S(2)}) collective-permute-start(bf16[3,80,128]{2,1,0:T(8,128)(2,1)S(1)} %pad_maximum_fusion), channel_id=1, source_target_pairs={{0,3},{1,4},{2,5},{3,6},{4,7},{5,8},{6,9},{7,10},{8,11},{9,12},{10... | collective-permute-start | bytes 184328 | tf_op jit(solution)/shard_map/ppermute | solution.py:673
  58.3 5.3 %collective-permute-start.11 = (bf16[3,80,128]{2,1,0:T(8,128)(2,1)S(1)}, bf16[3,80,128]{2,1,0:T(8,128)(2,1)S(1)}, u32[]{:S(2)}, u32[]{:S(2)}) collective-permute-start(bf16[3,80,128]{2,1,0:T(8,128)(2,1)S(1)} %pad_maximum_fusion), channel_id=1, source_target_pairs={{0,13},{1,14},{2,15},{3,0},{4,1},{5,2},{6,3},{7,4},{8,5},{9,6},{10... | collective-permute-start | bytes 184328 | tf_op jit(solution)/shard_map/ppermute | solution.py:673

commit v7 on v6

--- a/solution.py
+++ b/solution.py
@@ -24,8 +24,7 @@
 BODY = 64
 TAILS = (MARK + 1 - BODY) * CAP
 MESSAGE = CAP * BODY + TAILS
-SOURCE_PARTS = 3
-SOURCE_ROWS = CHANNELS * ROWS // SOURCE_PARTS
+CHUNK = 96
 EPSILON = 1e-05
 VMEM_LIMIT = 40 * 1024 * 1024
 REGRID_VMEM = 60 * 1024 * 1024
@@ -50,11 +49,12 @@
 
 
 def regrid_kernel(
-    column_rows, target_hbm, index_hbm, source_hbm, weight_hbm, *rest
+    column_rows, target_hbm, target_row_hbm, index_hbm, source_hbm, weight_hbm, *rest
 ):
     same_out, next_outs = rest[0], rest[1 : 1 + TILE_COLS]
     (
         target_ref,
+        target_row_ref,
         index_ref,
         source,
         weight,
@@ -67,28 +67,33 @@
         plan_scalars,
         plan_sem,
         in_sems,
+        weight_sems,
         out_sems,
     ) = rest[1 + TILE_COLS :]
     entries = weight.shape[0]
+    chunks = entries // CHUNK
     tile = lax.axis_index("tile")
     column, position = split(tile, column_rows)
 
-    target_copy = pltpu.make_async_copy(target_hbm, target_ref, in_sems.at[0])
-    index_copy = pltpu.make_async_copy(index_hbm, index_ref, in_sems.at[1])
-    target_copy.start()
-    source_copies = []
-    for part in range(SOURCE_PARTS):
-        rows = pl.ds(part * SOURCE_ROWS, SOURCE_ROWS)
-        source_copies.append(
-            pltpu.make_async_copy(source_hbm.at[rows], source.at[rows], in_sems.at[3 + part])
-        )
-        source_copies[-1].start()
-    index_copy.start()
-    weight_copy = pltpu.make_async_copy(weight_hbm, weight, in_sems.at[2])
-    weight_copy.start()
-
-    target_copy.wait()
-    target = target_ref[...]
+    small_copies = [
+        pltpu.make_async_copy(target_row_hbm, target_row_ref, in_sems.at[0]),
+        pltpu.make_async_copy(target_hbm, target_ref, in_sems.at[1]),
+        pltpu.make_async_copy(index_hbm, index_ref, in_sems.at[2]),
+    ]
+    source_copy = pltpu.make_async_copy(source_hbm, source, in_sems.at[3])
+    for copy in small_copies:
+        copy.start()
+    source_copy.start()
+
+    def chunk_copy(chunk):
+        part = pl.ds(chunk * CHUNK, CHUNK)
+        return pltpu.make_async_copy(weight_hbm.at[part], weight.at[part], weight_sems.at[chunk])
+
+    for chunk in range(chunks):
+        chunk_copy(chunk).start()
+
+    small_copies[0].wait()
+    target = target_row_ref[...]
     owner, row = split(target, ROWS)
     owner_column, owner_position = split(owner, column_rows)
     place = ((owner_column & (HALF - 1)) << 1) + (owner_column >= HALF).astype(jnp.int32)
@@ -108,7 +113,7 @@
     rank = jnp.sum(jnp.where(below, 1.0, 0.0), axis=0, keepdims=True)
     mentions = jnp.sum(jnp.where(equal & (down < along), 1.0, 0.0), axis=0, keepdims=True)
     slots = group * CAP + rank.astype(jnp.int32)
-    plan[...] = slots + jnp.where(mentions == 0.0, SLOTS, 0) + row * (2 * SLOTS)
+    plan[...] = slots + jnp.where(mentions == 0.0, SLOTS, 0)
     plan_copy = pltpu.make_async_copy(plan, plan_scalars, plan_sem)
     plan_copy.start()
 
@@ -118,47 +123,50 @@
         ((PADDED - CHANNELS) * ROWS, BLOCK), jnp.float32
     )
     nothing = jnp.zeros((WIDE - PADDED, BLOCK), jnp.float32)
-    for part, copy in enumerate(source_copies):
-        copy.wait()
-        rows = pl.ds(part * SOURCE_ROWS, SOURCE_ROWS)
-        wide[rows, :] = source[rows, :].astype(jnp.float32)
+    source_copy.wait()
+    wide[pl.ds(0, CHANNELS * ROWS), :] = source[...].astype(jnp.float32)
     for row in range(ROWS):
         block = wide[pl.ds(row, PADDED, stride=ROWS), :]
         field[row] = jnp.concatenate([block, nothing], axis=0).astype(jnp.bfloat16)
     is_mark = lax.broadcasted_iota(jnp.int32, (8, BLOCK), 0) == MARK - BODY
     blank = jnp.zeros((WIDE, BLOCK), jnp.bfloat16)
-    index_copy.wait()
+    small_copies[1].wait()
+    small_copies[2].wait()
     plan_copy.wait()
 
-    weight_copy.wait()
-    for entry in range(0, entries, 2):
-        one = jnp.concatenate([field[index_ref[entry]], blank], axis=1)
-        two = jnp.concatenate([blank, field[index_ref[entry + 1]]], axis=1)
-        products = jnp.dot(
-            jnp.concatenate([one, two], axis=0),
-            weight[entry : entry + 2].reshape(2 * BLOCK, BLOCK),
-            preferred_element_type=jnp.float32,
-        )
-        for at in range(2):
-            code = plan_scalars[0, entry + at]
-            slot = code & (SLOTS - 1)
-            fresh = (code & SLOTS) != 0
-            product = products[at * WIDE : at * WIDE + PADDED]
-            total = jnp.where(fresh, 0.0, sums[slot]) + product
-            sums[slot] = total
-            group, place = split(slot, CAP)
-            message[group, pl.ds(pl.multiple_of(place * BODY, BODY), BODY), :] = total[
-                :BODY
-            ].astype(jnp.bfloat16)
-            tails[pl.ds(pl.multiple_of(slot * 8, 8), 8), :] = jnp.where(
-                is_mark, split(code, 2 * SLOTS)[0].astype(jnp.float32), total[BODY:]
+    for chunk in range(chunks):
+        chunk_copy(chunk).wait()
+        for entry in range(chunk * CHUNK, (chunk + 1) * CHUNK, 2):
+            one = jnp.concatenate([field[index_ref[entry]], blank], axis=1)
+            two = jnp.concatenate([blank, field[index_ref[entry + 1]]], axis=1)
+            products = jnp.dot(
+                jnp.concatenate([one, two], axis=0),
+                weight[entry : entry + 2].reshape(2 * BLOCK, BLOCK),
+                preferred_element_type=jnp.float32,
             )
+            for at in range(2):
+                code = plan_scalars[0, entry + at]
+                slot = code & (SLOTS - 1)
+                row = split(target_ref[entry + at], ROWS)[1]
+                product = products[at * WIDE : at * WIDE + PADDED]
+                total = jnp.where(code >= SLOTS, 0.0, sums[slot]) + product
+                sums[slot] = total
+                group, place = split(slot, CAP)
+                message[group, pl.ds(pl.multiple_of(place * BODY, BODY), BODY), :] = total[
+                    :BODY
+                ].astype(jnp.bfloat16)
+                tails[pl.ds(pl.multiple_of(slot * 8, 8), 8), :] = jnp.where(
+                    is_mark, row.astype(jnp.float32), total[BODY:]
+                )
     copies = []
     for group in range(GROUPS):
         start = group * CAP * 8
         ends = [tails[pl.ds(start + at, CAP, stride=8), :] for at in range(MARK + 1 - BODY)]
         message[group, CAP * BODY :] = jnp.concatenate(ends, axis=0).astype(jnp.bfloat16)
-        out = same_out.at[group] if group < TILE_COLS else next_outs[group - TILE_COLS]
+        if group < TILE_COLS:
+            out = same_out.at[pl.ds(group * MESSAGE, MESSAGE)]
+        else:
+            out = next_outs[group - TILE_COLS]
         copies.append(pltpu.make_async_copy(message.at[group], out, out_sems.at[group]))
         copies[-1].start()
     for copy in copies:
@@ -167,15 +175,16 @@
 
 def regrid(target, source_index, field, weights, column_rows):
     piece = jax.ShapeDtypeStruct((MESSAGE, BLOCK), jnp.bfloat16)
-    same = jax.ShapeDtypeStruct((TILE_COLS, MESSAGE, BLOCK), jnp.bfloat16)
+    same = jax.ShapeDtypeStruct((TILE_COLS * MESSAGE, BLOCK), jnp.bfloat16)
     hbm = pl.BlockSpec(memory_space=pl.ANY)
     entries = weights.shape[0]
     return pl.pallas_call(
         functools.partial(regrid_kernel, column_rows),
-        in_specs=[hbm] * 4,
+        in_specs=[hbm] * 5,
         out_specs=[hbm] * (1 + TILE_COLS),
         out_shape=[same] + [piece] * TILE_COLS,
         scratch_shapes=[
+            pltpu.SMEM(target.shape, jnp.int32),
             pltpu.VMEM((1, entries), jnp.int32),
             pltpu.SMEM(source_index.shape, jnp.int32),
             pltpu.VMEM(field.shape, jnp.bfloat16),
@@ -188,12 +197,13 @@
             pltpu.VMEM((1, entries), jnp.int32),
             pltpu.SMEM((1, entries), jnp.int32),
             pltpu.SemaphoreType.DMA,
-            pltpu.SemaphoreType.DMA((3 + SOURCE_PARTS,)),
+            pltpu.SemaphoreType.DMA((4,)),
+            pltpu.SemaphoreType.DMA((entries // CHUNK,)),
             pltpu.SemaphoreType.DMA((GROUPS,)),
         ],
         compiler_params=pltpu.CompilerParams(vmem_limit_bytes=REGRID_VMEM),
         name="regrid",
-    )(target.reshape(1, -1), source_index, field, weights)
+    )(target, target.reshape(1, -1), source_index, field, weights)
 
 
 def normalized(rounded, gain):
@@ -225,7 +235,7 @@
 
     tails[:, TAILS:] = jnp.zeros((GROUPS, 8 * CAP - TAILS, BLOCK), jnp.float32)
     for group in range(TILE_COLS):
-        add(group, same.at[group])
+        add(group, same.at[pl.ds(group * MESSAGE, MESSAGE)])
 
     @pl.when(position > 0)
     def _():
@@ -418,6 +428,51 @@
     )(taps, hidden, gridded)
 
 
+def pack_kernel(above, below, own, to_west, to_east):
+    low = lanes((WIDE, BLOCK)) < BLOCK // 2
+    before, strip, after = above[2], own[...], below[2]
+
+    def other_half(plane):
+        return pltpu.roll(plane, BLOCK // 2, 1)
+
+    outer = jnp.where(low, after, before)
+    to_east[0] = jnp.where(low, other_half(strip), after)
+    to_east[1] = outer
+    to_west[0] = jnp.where(low, strip, other_half(before))
+    to_west[1] = outer
+
+
+def half_strip_packs(above, below, own):
+    pack = jax.ShapeDtypeStruct((2, WIDE, BLOCK), jnp.bfloat16)
+    return pl.pallas_call(
+        pack_kernel,
+        in_specs=[vmem()] * 3,
+        out_specs=[vmem()] * 2,
+        out_shape=[pack, pack],
+        compiler_params=pltpu.CompilerParams(vmem_limit_bytes=VMEM_LIMIT),
+        name="half_strip_packs",
+    )(above, below, own)
+
+
+def half_strips(west_pack, east_pack):
+    low = lanes((WIDE, BLOCK)) < BLOCK // 2
+
+    def other_half(plane):
+        return pltpu.roll(plane, BLOCK // 2, 1)
+
+    def both_halves(plane):
+        return jnp.where(low, plane, other_half(plane))
+
+    return {
+        -4: west_pack[1],
+        -3: both_halves(west_pack[0]),
+        -2: jnp.where(low, west_pack[1], west_pack[0]),
+        2: jnp.where(low, other_half(east_pack[0]), east_pack[1]),
+        3: both_halves(east_pack[0]),
+        4: east_pack[1],
+    }
+
+
 def strip_plan(column_rows):
     if column_rows == 2:
         return [], 3, 1
@@ -449,8 +504,11 @@
 
     strips = {-1: above[2], 0: own_strip[...], 1: below[2]}
     strips.update((shift, ref[...]) for shift, ref in zip(near, near_strips))
-    for at in range(-reach, reach + 1):
-        strips[at - far], strips[at + far] = west_pack[at + reach], east_pack[at + reach]
+    if R == 2:
+        strips.update(half_strips(west_pack, east_pack))
+    else:
+        for at in range(-reach, reach + 1):
+            strips[at - far], strips[at + far] = west_pack[at + reach], east_pack[at + reach]
 
     def place(shift):
         return lax.rem(tile + shift + count, count)
@@ -713,10 +771,13 @@
     strips = [from_shift(strip, shift) for shift in near]
     gridded, normed = normalize_rows(gain, summed)
     inner = inner_convolution(first_taps, normed)
-    held = {-1: rims[0][2], 0: strip, 1: rims[1][2], **dict(zip(near, strips))}
-    pack = jnp.stack([held[at] for at in range(-reach, reach + 1)])
-    pack, inner = lax.optimization_barrier((pack, inner))
-    strips += [from_shift(pack, -far), from_shift(pack, far)]
+    if column_rows == 2:
+        to_west, to_east = half_strip_packs(*rims, strip)
+    else:
+        held = {-1: rims[0][2], 0: strip, 1: rims[1][2], **dict(zip(near, strips))}
+        to_west = to_east = jnp.stack([held[at] for at in range(-reach, reach + 1)])
+    to_west, to_east, inner = lax.optimization_barrier((to_west, to_east, inner))
+    strips += [from_shift(to_east, -far), from_shift(to_west, far)]
     gridded_out = channels_first(gridded)
     hidden, *unfinished = inner
     base = inner_second_convolution(second_taps, hidden, gridded)

time: 67.5 us -> 67.3 us (level)
  transfers between devices with their start and end apart: 13 -> 13, of which waited for: 5 -> 6; matrix products, arithmetic and copies ran while one was open for 1% -> 1% of each run, Pallas kernels for 6% -> 6%
where the time goes in v7:
time: 67.3 us; the launch traced here: 66.6 us
  waiting for transfers between devices  28.7 us (43%)
  starting transfers between devices  21.9 us (33%)
  Pallas kernels  14.3 us (21%)
  between operations  0.98 us (1%)
  local copies, waits for them, and re-layouts  0.71 us (1%)
    ppermute x8, waiting for transfers between devices, per_device(): nexts[across] = lax.ppermute(nexts[across], 'tile', pairs)  27.1 us
    ppermute x8, starting transfers between devices, per_device(): nexts[across] = lax.ppermute(nexts[across], 'tile', pairs)  10.3 us
    all_to_all x1, starting transfers between devices, per_device(): lax.all_to_all(same, 'tile', 0, 0, axis_index_groups=[[c * column_rows +...  6.52 us
    ppermute x4, starting transfers between devices, from_shift(): lax.ppermute(value, 'tile', [(i, (i - shift) % count) for i in range(coun...  5.05 us
    pallas_call x1, Pallas kernels, regrid(): pl.pallas_call(functools.partial(regrid_kernel, column_rows), in_specs=[h...  5 us
    pallas_call x1, Pallas kernels, convolutions(): pl.pallas_call(functools.partial(conv_kernel, column_rows), in_specs=[vme...  3.2 us
    pallas_call x1, Pallas kernels, channels_first(): pl.pallas_call(turn_kernel, in_specs=[vmem()], out_specs=vmem(), out_shap...  1.99 us
    pallas_call x1, Pallas kernels, gather_rows(): pl.pallas_call(functools.partial(gather_kernel, column_rows), in_specs=[s...  1.8 us
  transfers between devices with their start and end apart: 13, of which 6 were waited for; matrix products, arithmetic and copies ran while one was open for 1% of the time, Pallas kernels for 6%

profile of v7, /device:TPU:1, one launch (start us, length us, event | category | flops | bytes accessed | tf_op | source)
XLA Modules:
  0.0 66.6 jit_solution(13976997575455271109)
XLA Ops:
  0.6 5.0 %regrid.1 = (bf16[4480,128]{1,0:T(8,128)(2,1)}, bf16[560,128]{1,0:T(8,128)(2,1)}, bf16[560,128]{1,0:T(8,128)(2,1)}, bf16[560,128]{1,0:T(8,128)(2,1)}, bf16[560,1...) custom-call(s32[96]{0:T(128)} %target_hbm.1, ...), custom_call_target="tpu_custom_call" | custom-call | tf_op jit(solution)/shard_map/regrid/pallas_call | solution.py:181
  5.6 0.0 copy-start.9
  5.6 0.0 copy-start.8
  5.7 0.0 copy-start.1
  5.7 0.0 copy-start.2
  5.7 6.5 %all-to-all-start = ((bf16[8,560,128]{2,1,0:T(8,128)(2,1)}), bf16[8,560,128]{2,1,0:T(8,128)(2,1)S(1)}, u32[]{:S(2)}, u32[]{:S(2)}) async-start(bf16[8,560,128]{2,1,0:T(8,128)(2,1)} %bitcast.25), calls=%async_computation | async-start | bytes 2293760 | tf_op jit(solution)/shard_map/all_to_all | solution.py:750
  12.3 0.0 copy-done.9
  12.3 1.3 %collective-permute-start = (bf16[560,128]{1,0:T(8,128)(2,1)S(1)}, bf16[560,128]{1,0:T(8,128)(2,1)S(1)}, u32[]{:S(2)}, u32[]{:S(2)}) collective-permute-start(bf16[560,128]{1,0:T(8,128)(2,1)S(1)} %copy-done.9), channel_id=1, source_target_pairs={{0,1},{2,3},{4,5},{6,7},{8,9},{10,11},{12,13},{14,15},{16,17},{18,... | collective-permute-start | bytes 430088 | tf_op jit(solution)/shard_map/ppermute | solution.py:748
  13.6 0.0 copy-done.8
  13.6 0.0 copy-start
  13.6 1.3 %collective-permute-start.1 = (bf16[560,128]{1,0:T(8,128)(2,1)S(1)}, bf16[560,128]{1,0:T(8,128)(2,1)S(1)}, u32[]{:S(2)}, u32[]{:S(2)}) collective-permute-start(bf16[560,128]{1,0:T(8,128)(2,1)S(1)} %copy-done.8), channel_id=1, source_target_pairs={{0,3},{2,1},{4,7},{6,5},{8,11},{10,9},{12,15},{14,13},{16,19},{18,... | collective-permute-start | bytes 430088 | tf_op jit(solution)/shard_map/ppermute | solution.py:748
  14.9 1.3 %collective-permute-start.2 = (bf16[560,128]{1,0:T(8,128)(2,1)S(1)}, bf16[560,128]{1,0:T(8,128)(2,1)S(1)}, u32[]{:S(2)}, u32[]{:S(2)}) collective-permute-start(bf16[560,128]{1,0:T(8,128)(2,1)S(1)} %copy-done.7), channel_id=1, source_target_pairs={{0,5},{2,7},{4,1},{6,3},{8,13},{10,15},{12,9},{14,11},{16,21},{18,... | collective-permute-start | bytes 430088 | tf_op jit(solution)/shard_map/ppermute | solution.py:748
  16.2 1.3 %collective-permute-start.3 = (bf16[560,128]{1,0:T(8,128)(2,1)}, bf16[560,128]{1,0:T(8,128)(2,1)S(1)}, u32[]{:S(2)}, u32[]{:S(2)}) collective-permute-start(bf16[560,128]{1,0:T(8,128)(2,1)} %get-tuple-element.43), channel_id=1, source_target_pairs={{0,9},{2,11},{4,13},{6,15},{8,1},{10,3},{12,5},{14,7},{16,25},{18,... | collective-permute-start | bytes 430088 | tf_op jit(solution)/shard_map/ppermute | solution.py:748
  17.5 1.3 %collective-permute-start.4 = (bf16[560,128]{1,0:T(8,128)(2,1)S(1)}, bf16[560,128]{1,0:T(8,128)(2,1)S(1)}, u32[]{:S(2)}, u32[]{:S(2)}) collective-permute-start(bf16[560,128]{1,0:T(8,128)(2,1)S(1)} %copy-done.6), channel_id=1, source_target_pairs={{0,11},{2,9},{4,15},{6,13},{8,3},{10,1},{12,7},{14,5},{16,27},{18,... | collective-permute-start | bytes 430088 | tf_op jit(solution)/shard_map/ppermute | solution.py:748
  18.8 0.0 collective-permute-done.rest_0_
  18.8 1.3 %collective-permute-start.5 = (bf16[560,128]{1,0:T(8,128)(2,1)S(1)}, bf16[560,128]{1,0:T(8,128)(2,1)S(1)}, u32[]{:S(2)}, u32[]{:S(2)}) collective-permute-start(bf16[560,128]{1,0:T(8,128)(2,1)S(1)} %copy-done.5), channel_id=1, source_target_pairs={{0,13},{2,15},{4,9},{6,11},{8,5},{10,7},{12,1},{14,3},{16,29},{18,... | collective-permute-start | bytes 430088 | tf_op jit(solution)/shard_map/ppermute | solution.py:748
  20.1 2.7 %collective-permute-done.1.rest_1_ = bf16[560,128]{1,0:T(8,128)(2,1)S(1)} collective-permute-done((bf16[560,128]{1,0:T(8,128)(2,1)S(1)}, bf16[560,128]{1,0:T(8,128)(2,1)S(1)}, u32[]{:S(2)}, u32[]{:S(2)}) %collective-permute-start.1) | collective-permute-done | bytes 143392 | tf_op jit(solution)/shard_map/ppermute | solution.py:748
  22.8 1.3 %collective-permute-start.6 = (bf16[560,128]{1,0:T(8,128)(2,1)S(1)}, bf16[560,128]{1,0:T(8,128)(2,1)S(1)}, u32[]{:S(2)}, u32[]{:S(2)}) collective-permute-start(bf16[560,128]{1,0:T(8,128)(2,1)S(1)} %copy-done.4), channel_id=1, source_target_pairs={{0,15},{2,13},{4,11},{6,9},{8,7},{10,5},{12,3},{14,1},{16,31},{18,... | collective-permute-start | bytes 430088 | tf_op jit(solution)/shard_map/ppermute | solution.py:748
  24.1 8.0 %collective-permute-done.2.rest_2_ = bf16[560,128]{1,0:T(8,128)(2,1)S(1)} collective-permute-done((bf16[560,128]{1,0:T(8,128)(2,1)S(1)}, bf16[560,128]{1,0:T(8,128)(2,1)S(1)}, u32[]{:S(2)}, u32[]{:S(2)}) %collective-permute-start.2) | collective-permute-done | bytes 143392 | tf_op jit(solution)/shard_map/ppermute | solution.py:748
  32.1 1.3 %collective-permute-start.7 = (bf16[560,128]{1,0:T(8,128)(2,1)S(1)}, bf16[560,128]{1,0:T(8,128)(2,1)S(1)}, u32[]{:S(2)}, u32[]{:S(2)}) collective-permute-start(bf16[560,128]{1,0:T(8,128)(2,1)S(1)} %copy-done.3), channel_id=1, source_target_pairs={{0,7},{2,5},{4,3},{6,1},{8,15},{10,13},{12,11},{14,9},{16,23},{18,... | collective-permute-start | bytes 430088 | tf_op jit(solution)/shard_map/ppermute | solution.py:748
  33.5 0.1 copy.17
  33.6 0.2 reshape.35.taps_ref.first_taps_ref
  33.7 0.0 copy-done.2
  33.8 0.1 copy.16
  33.9 0.2 reshape.37.taps_ref.second_taps_ref
  34.0 0.0 copy-done.10
  34.1 14.0 %collective-permute-done.3.rest_3_ = bf16[560,128]{1,0:T(8,128)(2,1)S(1)} collective-permute-done((bf16[560,128]{1,0:T(8,128)(2,1)}, bf16[560,128]{1,0:T(8,128)(2,1)S(1)}, u32[]{:S(2)}, u32[]{:S(2)}) %collective-permute-start.3) | collective-permute-done | bytes 143392 | tf_op jit(solution)/shard_map/ppermute | solution.py:748
  48.1 2.4 %collective-permute-done.4.rest_4_ = bf16[560,128]{1,0:T(8,128)(2,1)S(1)} collective-permute-done((bf16[560,128]{1,0:T(8,128)(2,1)S(1)}, bf16[560,128]{1,0:T(8,128)(2,1)S(1)}, u32[]{:S(2)}, u32[]{:S(2)}) %collective-permute-start.4) | collective-permute-done | bytes 143392 | tf_op jit(solution)/shard_map/ppermute | solution.py:748
  50.5 0.0 collective-permute-done.5.rest_5_
  50.5 0.0 collective-permute-done.6.rest_6_
  50.5 0.0 collective-permute-done.7.rest_7_
  50.5 0.0 all-to-all-done
  50.5 0.1 broadcast_in_dim.12.gain_ref
  50.6 1.8 %gather_rows.1 = (f32[33,72,128]{2,1,0:T(8,128)S(1)}, bf16[3,80,128]{2,1,0:T(8,128)(2,1)S(1)}, bf16[3,80,128]{2,1,0:T(8,128)(2,1)S(1)}, bf16[80,128]{1,0:T(8,128)(2,1)S(1)}) custom-call(s32[1,2]{1,0:T(1,128)S(1)} %copy-done, f32[72,128]{1,0:T(8,128)S(1)} %broadcast_in_dim.12.gain_ref, bf16[4480,128]{1,0:T(8,128)(2,1)S(1)} %bitcast.24, ...), custom_call_target="tpu_custom_call" | custom-call | tf_op jit(solution)/shard_map/gather_rows/pallas_call | solution.py:300
  52.4 0.1 collective-permute-start.8
  52.5 0.5 collective-permute-start.9
  53.0 0.3 normalize_rows.1
  53.3 2.0 %channels_first.1 = bf16[2208,128]{1,0:T(8,128)(2,1)} custom-call(bf16[32,72,128]{2,1,0:T(8,128)(2,1)S(1)} %get-tuple-element.59.field.gridded), custom_call_target="tpu_custom_call" | custom-call | tf_op jit(solution)/shard_map/channels_first/pallas_call | solution.py:318
  55.3 1.2 %inner_convolution.1 = (bf16[32,80,128]{2,1,0:T(8,128)(2,1)S(1)}, f32[2,80,128]{2,1,0:T(8,128)S(1)}, f32[2,80,128]{2,1,0:T(8,128)S(1)}) custom-call(bf16[240,240]{1,0:T(8,128)(2,1)S(1)} %reshape.35.taps_ref.first_taps_ref, bf16[32,80,128]{2,1,0:T(8,128)(2,1)S(1)} %get-tuple-element.62.field), custom_call_target="tpu_custom_call" | custom-call | flops 471859200 | bytes 2097152 | tf_op jit(solution)/shard_map/inner_convolution/pallas_call | solution.py:384
  56.5 0.0 collective-permute-done.8.above
  56.5 0.0 collective-permute-done.9.below
  56.5 0.1 half_strip_packs.1
  56.6 3.3 %collective-permute-start.10 = (bf16[2,80,128]{2,1,0:T(8,128)(2,1)S(1)}, bf16[2,80,128]{2,1,0:T(8,128)(2,1)S(1)}, u32[]{:S(2)}, u32[]{:S(2)}) collective-permute-start(bf16[2,80,128]{2,1,0:T(8,128)(2,1)S(1)} %get-tuple-element.74), channel_id=1, source_target_pairs={{0,3},{1,4},{2,5},{3,6},{4,7},{5,8},{6,9},{7,10},{8,11},{9,12},{10... | collective-permute-start | bytes 122888 | tf_op jit(solution)/shard_map/ppermute | solution.py:731
  59.9 1.2 %collective-permute-start.11 = (bf16[2,80,128]{2,1,0:T(8,128)(2,1)S(1)}, bf16[2,80,128]{2,1,0:T(8,128)(2,1)S(1)}, u32[]{:S(2)}, u32[]{:S(2)}) collective-permute-start(bf16[2,80,128]{2,1,0:T(8,128)(2,1)S(1)} %get-tuple-element.75), channel_id=1, source_target_pairs={{0,13},{1,14},{2,15},{3,0},{4,1},{5,2},{6,3},{7,4},{8,5},{9,6},{10... | collective-permute-start | bytes 122888 | tf_op jit(solution)/shard_map/ppermute | solution.py:731
  61.1 0.8 %inner_second_convolution.1.base = f32[32,72,128]{2,1,0:T(8,128)S(1)} custom-call(bf16[240,240]{1,0:T(8,128)(2,1)S(1)} %reshape.37.taps_ref.second_taps_ref, bf16[32,80,128]{2,1,0:T(8,128)(2,1)S(1)} %get-tuple-element.71.hidden, bf16[32,72,128]{2,1,0:T(8,128)(2,1)S(1)} %get-tuple-element.59.field.gridded), custom_call_target="tpu_custom_call" | custom-call | flops 471859200 | bytes 2097152 | tf_op jit(solution)/shard_map/inner_second_convolution/pallas_call | solution.py:417
  61.9 1.0 %collective-permute-done.10.rest_0_ = bf16[2,80,128]{2,1,0:T(8,128)(2,1)S(1)} collective-permute-done((bf16[2,80,128]{2,1,0:T(8,128)(2,1)S(1)}, bf16[2,80,128]{2,1,0:T(8,128)(2,1)S(1)}, u32[]{:S(2)}, u32[]{:S(2)}) %collective-permute-start.10) | collective-permute-done | bytes 40992 | tf_op jit(solution)/shard_map/ppermute | solution.py:731
  62.9 0.5 collective-permute-done.11.rest_1_
  63.4 3.2 %convolutions.1 = bf16[69,32,128]{2,1,0:T(8,128)(2,1)} custom-call(bf16[240,240]{1,0:T(8,128)(2,1)S(1)} %reshape.35.taps_ref.first_taps_ref, bf16[240,240]{1,0:T(8,128)(2,1)S(1)} %reshape.37.taps_ref.second_taps_ref, bf16[32,80,128]{2,1,0:T(8,128)(2,1)S(1)} %get-tuple-element.62.field, f32[32,72,128]{2,1,0:T(8,128)S(1)} %inner_second_convolution.1.base, ...), custom_call_target="tpu_custom_call" | custom-call | tf_op jit(solution)/shard_map/convolutions/pallas_call | solution.py:708
  (16 shorter events, 0.1 us)
Async XLA Ops:
  5.6 6.6 %copy-start.9 = (bf16[560,128]{1,0:T(8,128)(2,1)S(1)}, bf16[560,128]{1,0:T(8,128)(2,1)}, u32[]{:S(2)}) copy-start(bf16[560,128]{1,0:T(8,128)(2,1)} %get-tuple-element.40) | copy-start | bytes 430084
  5.6 7.9 %copy-start.8 = (bf16[560,128]{1,0:T(8,128)(2,1)S(1)}, bf16[560,128]{1,0:T(8,128)(2,1)}, u32[]{:S(2)}) copy-start(bf16[560,128]{1,0:T(8,128)(2,1)} %get-tuple-element.41) | copy-start | bytes 430084
  5.7 9.2 %copy-start.7 = (bf16[560,128]{1,0:T(8,128)(2,1)S(1)}, bf16[560,128]{1,0:T(8,128)(2,1)}, u32[]{:S(2)}) copy-start(bf16[560,128]{1,0:T(8,128)(2,1)} %get-tuple-element.42) | copy-start | bytes 430084
  5.7 11.8 %copy-start.6 = (bf16[560,128]{1,0:T(8,128)(2,1)S(1)}, bf16[560,128]{1,0:T(8,128)(2,1)}, u32[]{:S(2)}) copy-start(bf16[560,128]{1,0:T(8,128)(2,1)} %get-tuple-element.44) | copy-start | bytes 430084
  5.7 13.1 %copy-start.5 = (bf16[560,128]{1,0:T(8,128)(2,1)S(1)}, bf16[560,128]{1,0:T(8,128)(2,1)}, u32[]{:S(2)}) copy-start(bf16[560,128]{1,0:T(8,128)(2,1)} %get-tuple-element.45) | copy-start | bytes 430084
  5.7 17.1 %copy-start.4 = (bf16[560,128]{1,0:T(8,128)(2,1)S(1)}, bf16[560,128]{1,0:T(8,128)(2,1)}, u32[]{:S(2)}) copy-start(bf16[560,128]{1,0:T(8,128)(2,1)} %get-tuple-element.46) | copy-start | bytes 430084
  5.7 26.4 %copy-start.3 = (bf16[560,128]{1,0:T(8,128)(2,1)S(1)}, bf16[560,128]{1,0:T(8,128)(2,1)}, u32[]{:S(2)}) copy-start(bf16[560,128]{1,0:T(8,128)(2,1)} %get-tuple-element.47) | copy-start | bytes 430084
  5.7 27.7 %copy-start.1 = (bf16[9,69,69]{2,1,0:T(8,128)(2,1)S(1)}, bf16[9,69,69]{2,1,0:T(8,128)(2,1)}, u32[]{:S(2)}) copy-start(bf16[9,69,69]{2,1,0:T(8,128)(2,1)} %param.14) | copy-start | bytes 257098
  5.7 28.0 %copy-start.2 = (bf16[9,69,69]{2,1,0:T(8,128)(2,1)S(1)}, bf16[9,69,69]{2,1,0:T(8,128)(2,1)}, u32[]{:S(2)}) copy-start(bf16[9,69,69]{2,1,0:T(8,128)(2,1)} %param.15) | copy-start | bytes 257098
  5.7 44.8 %all-to-all-start = ((bf16[8,560,128]{2,1,0:T(8,128)(2,1)}), bf16[8,560,128]{2,1,0:T(8,128)(2,1)S(1)}, u32[]{:S(2)}, u32[]{:S(2)}) async-start(bf16[8,560,128]{2,1,0:T(8,128)(2,1)} %bitcast.25), calls=%async_computation | async-start | bytes 2293760 | tf_op jit(solution)/shard_map/all_to_all | solution.py:750
  12.3 21.8 %copy-start.10 = (f32[69]{0:T(128)S(1)}, f32[69]{0:T(128)}, u32[]{:S(2)}) copy-start(f32[69]{0:T(128)} %param.13) | copy-start | bytes 832
  12.3 6.5 %collective-permute-start = (bf16[560,128]{1,0:T(8,128)(2,1)S(1)}, bf16[560,128]{1,0:T(8,128)(2,1)S(1)}, u32[]{:S(2)}, u32[]{:S(2)}) collective-permute-start(bf16[560,128]{1,0:T(8,128)(2,1)S(1)} %copy-done.9), channel_id=1, source_target_pairs={{0,1},{2,3},{4,5},{6,7},{8,9},{10,11},{12,13},{14,15},{16,17},{18,... | collective-permute-start | bytes 430088 | tf_op jit(solution)/shard_map/ppermute | solution.py:748
  13.6 37.0 %copy-start = (s32[1,2]{1,0:T(1,128)S(1)}, s32[1,2]{1,0:T(1,128)}, u32[]{:S(2)}) copy-start(s32[1,2]{1,0:T(1,128)} %flip_ref.1) | copy-start | bytes 28
  13.6 9.2 %collective-permute-start.1 = (bf16[560,128]{1,0:T(8,128)(2,1)S(1)}, bf16[560,128]{1,0:T(8,128)(2,1)S(1)}, u32[]{:S(2)}, u32[]{:S(2)}) collective-permute-start(bf16[560,128]{1,0:T(8,128)(2,1)S(1)} %copy-done.8), channel_id=1, source_target_pairs={{0,3},{2,1},{4,7},{6,5},{8,11},{10,9},{12,15},{14,13},{16,19},{18,... | collective-permute-start | bytes 430088 | tf_op jit(solution)/shard_map/ppermute | solution.py:748
  14.9 17.2 %collective-permute-start.2 = (bf16[560,128]{1,0:T(8,128)(2,1)S(1)}, bf16[560,128]{1,0:T(8,128)(2,1)S(1)}, u32[]{:S(2)}, u32[]{:S(2)}) collective-permute-start(bf16[560,128]{1,0:T(8,128)(2,1)S(1)} %copy-done.7), channel_id=1, source_target_pairs={{0,5},{2,7},{4,1},{6,3},{8,13},{10,15},{12,9},{14,11},{16,21},{18,... | collective-permute-start | bytes 430088 | tf_op jit(solution)/shard_map/ppermute | solution.py:748
  16.2 31.9 %collective-permute-start.3 = (bf16[560,128]{1,0:T(8,128)(2,1)}, bf16[560,128]{1,0:T(8,128)(2,1)S(1)}, u32[]{:S(2)}, u32[]{:S(2)}) collective-permute-start(bf16[560,128]{1,0:T(8,128)(2,1)} %get-tuple-element.43), channel_id=1, source_target_pairs={{0,9},{2,11},{4,13},{6,15},{8,1},{10,3},{12,5},{14,7},{16,25},{18,... | collective-permute-start | bytes 430088 | tf_op jit(solution)/shard_map/ppermute | solution.py:748
  17.5 33.0 %collective-permute-start.4 = (bf16[560,128]{1,0:T(8,128)(2,1)S(1)}, bf16[560,128]{1,0:T(8,128)(2,1)S(1)}, u32[]{:S(2)}, u32[]{:S(2)}) collective-permute-start(bf16[560,128]{1,0:T(8,128)(2,1)S(1)} %copy-done.6), channel_id=1, source_target_pairs={{0,11},{2,9},{4,15},{6,13},{8,3},{10,1},{12,7},{14,5},{16,27},{18,... | collective-permute-start | bytes 430088 | tf_op jit(solution)/shard_map/ppermute | solution.py:748
  18.8 31.7 %collective-permute-start.5 = (bf16[560,128]{1,0:T(8,128)(2,1)S(1)}, bf16[560,128]{1,0:T(8,128)(2,1)S(1)}, u32[]{:S(2)}, u32[]{:S(2)}) collective-permute-start(bf16[560,128]{1,0:T(8,128)(2,1)S(1)} %copy-done.5), channel_id=1, source_target_pairs={{0,13},{2,15},{4,9},{6,11},{8,5},{10,7},{12,1},{14,3},{16,29},{18,... | collective-permute-start | bytes 430088 | tf_op jit(solution)/shard_map/ppermute | solution.py:748
  22.8 27.7 %collective-permute-start.6 = (bf16[560,128]{1,0:T(8,128)(2,1)S(1)}, bf16[560,128]{1,0:T(8,128)(2,1)S(1)}, u32[]{:S(2)}, u32[]{:S(2)}) collective-permute-start(bf16[560,128]{1,0:T(8,128)(2,1)S(1)} %copy-done.4), channel_id=1, source_target_pairs={{0,15},{2,13},{4,11},{6,9},{8,7},{10,5},{12,3},{14,1},{16,31},{18,... | collective-permute-start | bytes 430088 | tf_op jit(solution)/shard_map/ppermute | solution.py:748
  32.1 18.4 %collective-permute-start.7 = (bf16[560,128]{1,0:T(8,128)(2,1)S(1)}, bf16[560,128]{1,0:T(8,128)(2,1)S(1)}, u32[]{:S(2)}, u32[]{:S(2)}) collective-permute-start(bf16[560,128]{1,0:T(8,128)(2,1)S(1)} %copy-done.3), channel_id=1, source_target_pairs={{0,7},{2,5},{4,3},{6,1},{8,15},{10,13},{12,11},{14,9},{16,23},{18,... | collective-permute-start | bytes 430088 | tf_op jit(solution)/shard_map/ppermute | solution.py:748
  52.4 4.1 %collective-permute-start.8 = (bf16[3,80,128]{2,1,0:T(8,128)(2,1)S(1)}, bf16[3,80,128]{2,1,0:T(8,128)(2,1)S(1)}, u32[]{:S(2)}, u32[]{:S(2)}) collective-permute-start(bf16[3,80,128]{2,1,0:T(8,128)(2,1)S(1)} %get-tuple-element.63), channel_id=1, source_target_pairs={{0,1},{1,2},{2,3},{3,4},{4,5},{5,6},{6,7},{7,8},{8,9},{9,10},{10,1... | collective-permute-start | bytes 184328 | tf_op jit(solution)/shard_map/ppermute | solution.py:731
  52.5 4.0 %collective-permute-start.9 = (bf16[3,80,128]{2,1,0:T(8,128)(2,1)S(1)}, bf16[3,80,128]{2,1,0:T(8,128)(2,1)S(1)}, u32[]{:S(2)}, u32[]{:S(2)}) collective-permute-start(bf16[3,80,128]{2,1,0:T(8,128)(2,1)S(1)} %get-tuple-element.64), channel_id=1, source_target_pairs={{0,15},{1,0},{2,1},{3,2},{4,3},{5,4},{6,5},{7,6},{8,7},{9,8},{10,9... | collective-permute-start | bytes 184328 | tf_op jit(solution)/shard_map/ppermute | solution.py:731
  56.6 6.3 %collective-permute-start.10 = (bf16[2,80,128]{2,1,0:T(8,128)(2,1)S(1)}, bf16[2,80,128]{2,1,0:T(8,128)(2,1)S(1)}, u32[]{:S(2)}, u32[]{:S(2)}) collective-permute-start(bf16[2,80,128]{2,1,0:T(8,128)(2,1)S(1)} %get-tuple-element.74), channel_id=1, source_target_pairs={{0,3},{1,4},{2,5},{3,6},{4,7},{5,8},{6,9},{7,10},{8,11},{9,12},{10... | collective-permute-start | bytes 122888 | tf_op jit(solution)/shard_map/ppermute | solution.py:731
  59.9 3.5 %collective-permute-start.11 = (bf16[2,80,128]{2,1,0:T(8,128)(2,1)S(1)}, bf16[2,80,128]{2,1,0:T(8,128)(2,1)S(1)}, u32[]{:S(2)}, u32[]{:S(2)}) collective-permute-start(bf16[2,80,128]{2,1,0:T(8,128)(2,1)S(1)} %get-tuple-element.75), channel_id=1, source_target_pairs={{0,13},{1,14},{2,15},{3,0},{4,1},{5,2},{6,3},{7,4},{8,5},{9,6},{10... | collective-permute-start | bytes 122888 | tf_op jit(solution)/shard_map/ppermute | solution.py:731

commit v8 on v7

--- a/solution.py
+++ b/solution.py
@@ -125,9 +125,9 @@
     nothing = jnp.zeros((WIDE - PADDED, BLOCK), jnp.float32)
     source_copy.wait()
     wide[pl.ds(0, CHANNELS * ROWS), :] = source[...].astype(jnp.float32)
+    turned = jnp.transpose(wide[...].reshape(PADDED, ROWS, BLOCK), (1, 0, 2))
     for row in range(ROWS):
-        block = wide[pl.ds(row, PADDED, stride=ROWS), :]
-        field[row] = jnp.concatenate([block, nothing], axis=0).astype(jnp.bfloat16)
+        field[row] = jnp.concatenate([turned[row], nothing], axis=0).astype(jnp.bfloat16)
     is_mark = lax.broadcasted_iota(jnp.int32, (8, BLOCK), 0) == MARK - BODY
     blank = jnp.zeros((WIDE, BLOCK), jnp.bfloat16)
     small_copies[1].wait()
@@ -308,10 +308,9 @@
     )(edge_flip, gain, same, *nexts)
 
 
-def turn_kernel(field, out, turned):
-    for row in range(ROWS):
-        turned[pl.ds(row, PADDED, stride=ROWS), :] = field[row].astype(jnp.float32)
-    out[...] = turned[pl.ds(0, CHANNELS * ROWS), :].astype(jnp.bfloat16)
+def turn_kernel(field, out):
+    turned = jnp.transpose(field[...].astype(jnp.float32), (1, 0, 2))
+    out[...] = turned[:CHANNELS].reshape(CHANNELS * ROWS, BLOCK).astype(jnp.bfloat16)
 
 
 def channels_first(field):
@@ -320,7 +319,6 @@
         in_specs=[vmem()],
         out_specs=vmem(),
         out_shape=jax.ShapeDtypeStruct((CHANNELS * ROWS, BLOCK), jnp.bfloat16),
-        scratch_shapes=[pltpu.VMEM((PADDED * ROWS, BLOCK), jnp.float32)],
         compiler_params=pltpu.CompilerParams(vmem_limit_bytes=VMEM_LIMIT),
         name="channels_first",
     )(field)
@@ -494,7 +492,7 @@
 ):
     near, far, reach = strip_plan(column_rows)
     near_strips, (west_pack, east_pack) = rest[: len(near)], rest[len(near) : len(near) + 2]
-    smoothed, turned, halves, sems = rest[len(near) + 2 :]
+    smoothed, unturned, halves, sems = rest[len(near) + 2 :]
     count = lax.axis_size("tile")
     tile = lax.axis_index("tile")
     lane = lanes((WIDE, BLOCK))
@@ -694,9 +692,8 @@
             )
             if row in rim_rows:
                 value = value + rim_rows[row][:PADDED]
-            turned[half, pl.ds(row - half * HALF_ROWS, PADDED, stride=HALF_ROWS), :] = value
-        rounded = turned[half, pl.ds(0, CHANNELS * HALF_ROWS), :].astype(jnp.bfloat16)
-        halves[half] = rounded.reshape(CHANNELS, HALF_ROWS, BLOCK)
+            unturned[half, row - half * HALF_ROWS] = value
+        halves[half] = jnp.transpose(unturned[half], (1, 0, 2))[:CHANNELS].astype(jnp.bfloat16)
         rows = pl.ds(half * HALF_ROWS, HALF_ROWS)
         copies.append(pltpu.make_async_copy(halves.at[half], smoothed.at[:, rows], sems.at[half]))
         copies[-1].start()
@@ -711,7 +708,7 @@
         out_specs=pl.BlockSpec(memory_space=pl.ANY),
         out_shape=jax.ShapeDtypeStruct((CHANNELS, ROWS, BLOCK), jnp.bfloat16),
         scratch_shapes=[
-            pltpu.VMEM((2, PADDED * HALF_ROWS, BLOCK), jnp.float32),
+            pltpu.VMEM((2, HALF_ROWS, PADDED, BLOCK), jnp.float32),
             pltpu.VMEM((2, CHANNELS, HALF_ROWS, BLOCK), jnp.bfloat16),
             pltpu.SemaphoreType.DMA((2,)),
         ],

time: 67.3 us -> 67 us (level)
  Pallas kernels: 14.3 us -> 13.3 us
    pallas_call x1, Pallas kernels: 1.99 us -> 1.09 us  [channels_first(): pl.pallas_call(turn_kernel, in_specs=[vmem()], out_specs=vmem(), out_shap...]
  transfers between devices with their start and end apart: 13 -> 13, of which waited for: 6 -> 7; matrix products, arithmetic and copies ran while one was open for 1% -> 1% of each run, Pallas kernels for 6% -> 5%
where the time goes in v8:
time: 67 us; the launch traced here: 66.2 us
  waiting for transfers between devices  29.3 us (44%)
  starting transfers between devices  21.9 us (33%)
  Pallas kernels  13.3 us (20%)
  between operations  0.98 us (1%)
  local copies, waits for them, and re-layouts  0.71 us (1%)
    ppermute x8, waiting for transfers between devices, per_device(): nexts[across] = lax.ppermute(nexts[across], 'tile', pairs)  27.1 us
    ppermute x8, starting transfers between devices, per_device(): nexts[across] = lax.ppermute(nexts[across], 'tile', pairs)  10.3 us
    all_to_all x1, starting transfers between devices, per_device(): lax.all_to_all(same, 'tile', 0, 0, axis_index_groups=[[c * column_rows +...  6.53 us
    ppermute x4, starting transfers between devices, from_shift(): lax.ppermute(value, 'tile', [(i, (i - shift) % count) for i in range(coun...  5.05 us
    pallas_call x1, Pallas kernels, regrid(): pl.pallas_call(functools.partial(regrid_kernel, column_rows), in_specs=[h...  4.99 us
    pallas_call x1, Pallas kernels, convolutions(): pl.pallas_call(functools.partial(conv_kernel, column_rows), in_specs=[vme...  3.09 us
    ppermute x4, waiting for transfers between devices, from_shift(): lax.ppermute(value, 'tile', [(i, (i - shift) % count) for i in range(coun...  2.15 us
    pallas_call x1, Pallas kernels, gather_rows(): pl.pallas_call(functools.partial(gather_kernel, column_rows), in_specs=[s...  1.8 us
  transfers between devices with their start and end apart: 13, of which 7 were waited for; matrix products, arithmetic and copies ran while one was open for 1% of the time, Pallas kernels for 5%

profile of v8, /device:TPU:1, one launch (start us, length us, event | category | flops | bytes accessed | tf_op | source)
XLA Modules:
  0.0 66.2 jit_solution(8381314875552201405)
XLA Ops:
  0.6 5.0 %regrid.1 = (bf16[4480,128]{1,0:T(8,128)(2,1)}, bf16[560,128]{1,0:T(8,128)(2,1)}, bf16[560,128]{1,0:T(8,128)(2,1)}, bf16[560,128]{1,0:T(8,128)(2,1)}, bf16[560,1...) custom-call(s32[96]{0:T(128)} %target_hbm.1, ...), custom_call_target="tpu_custom_call" | custom-call | tf_op jit(solution)/shard_map/regrid/pallas_call | solution.py:181
  5.6 0.0 copy-start.9
  5.6 0.0 copy-start.8
  5.6 0.0 copy-start.7
  5.7 0.0 copy-start.6
  5.7 0.0 copy-start.5
  5.7 0.0 copy-start.4
  5.7 0.0 copy-start.1
  5.7 0.0 copy-start.2
  5.7 6.5 %all-to-all-start = ((bf16[8,560,128]{2,1,0:T(8,128)(2,1)}), bf16[8,560,128]{2,1,0:T(8,128)(2,1)S(1)}, u32[]{:S(2)}, u32[]{:S(2)}) async-start(bf16[8,560,128]{2,1,0:T(8,128)(2,1)} %bitcast.25), calls=%async_computation | async-start | bytes 2293760 | tf_op jit(solution)/shard_map/all_to_all | solution.py:747
  12.3 1.3 %collective-permute-start = (bf16[560,128]{1,0:T(8,128)(2,1)S(1)}, bf16[560,128]{1,0:T(8,128)(2,1)S(1)}, u32[]{:S(2)}, u32[]{:S(2)}) collective-permute-start(bf16[560,128]{1,0:T(8,128)(2,1)S(1)} %copy-done.9), channel_id=1, source_target_pairs={{0,1},{2,3},{4,5},{6,7},{8,9},{10,11},{12,13},{14,15},{16,17},{18,... | collective-permute-start | bytes 430088 | tf_op jit(solution)/shard_map/ppermute | solution.py:745
  13.6 0.0 copy-start
  13.6 1.3 %collective-permute-start.1 = (bf16[560,128]{1,0:T(8,128)(2,1)S(1)}, bf16[560,128]{1,0:T(8,128)(2,1)S(1)}, u32[]{:S(2)}, u32[]{:S(2)}) collective-permute-start(bf16[560,128]{1,0:T(8,128)(2,1)S(1)} %copy-done.8), channel_id=1, source_target_pairs={{0,3},{2,1},{4,7},{6,5},{8,11},{10,9},{12,15},{14,13},{16,19},{18,... | collective-permute-start | bytes 430088 | tf_op jit(solution)/shard_map/ppermute | solution.py:745
  14.9 1.3 %collective-permute-start.2 = (bf16[560,128]{1,0:T(8,128)(2,1)S(1)}, bf16[560,128]{1,0:T(8,128)(2,1)S(1)}, u32[]{:S(2)}, u32[]{:S(2)}) collective-permute-start(bf16[560,128]{1,0:T(8,128)(2,1)S(1)} %copy-done.7), channel_id=1, source_target_pairs={{0,5},{2,7},{4,1},{6,3},{8,13},{10,15},{12,9},{14,11},{16,21},{18,... | collective-permute-start | bytes 430088 | tf_op jit(solution)/shard_map/ppermute | solution.py:745
  16.2 1.3 %collective-permute-start.3 = (bf16[560,128]{1,0:T(8,128)(2,1)}, bf16[560,128]{1,0:T(8,128)(2,1)S(1)}, u32[]{:S(2)}, u32[]{:S(2)}) collective-permute-start(bf16[560,128]{1,0:T(8,128)(2,1)} %get-tuple-element.43), channel_id=1, source_target_pairs={{0,9},{2,11},{4,13},{6,15},{8,1},{10,3},{12,5},{14,7},{16,25},{18,... | collective-permute-start | bytes 430088 | tf_op jit(solution)/shard_map/ppermute | solution.py:745
  17.5 1.3 %collective-permute-start.4 = (bf16[560,128]{1,0:T(8,128)(2,1)S(1)}, bf16[560,128]{1,0:T(8,128)(2,1)S(1)}, u32[]{:S(2)}, u32[]{:S(2)}) collective-permute-start(bf16[560,128]{1,0:T(8,128)(2,1)S(1)} %copy-done.6), channel_id=1, source_target_pairs={{0,11},{2,9},{4,15},{6,13},{8,3},{10,1},{12,7},{14,5},{16,27},{18,... | collective-permute-start | bytes 430088 | tf_op jit(solution)/shard_map/ppermute | solution.py:745
  18.8 0.0 collective-permute-done.rest_0_
  18.8 1.3 %collective-permute-start.5 = (bf16[560,128]{1,0:T(8,128)(2,1)S(1)}, bf16[560,128]{1,0:T(8,128)(2,1)S(1)}, u32[]{:S(2)}, u32[]{:S(2)}) collective-permute-start(bf16[560,128]{1,0:T(8,128)(2,1)S(1)} %copy-done.5), channel_id=1, source_target_pairs={{0,13},{2,15},{4,9},{6,11},{8,5},{10,7},{12,1},{14,3},{16,29},{18,... | collective-permute-start | bytes 430088 | tf_op jit(solution)/shard_map/ppermute | solution.py:745
  20.1 2.7 %collective-permute-done.1.rest_1_ = bf16[560,128]{1,0:T(8,128)(2,1)S(1)} collective-permute-done((bf16[560,128]{1,0:T(8,128)(2,1)S(1)}, bf16[560,128]{1,0:T(8,128)(2,1)S(1)}, u32[]{:S(2)}, u32[]{:S(2)}) %collective-permute-start.1) | collective-permute-done | bytes 143392 | tf_op jit(solution)/shard_map/ppermute | solution.py:745
  22.8 1.3 %collective-permute-start.6 = (bf16[560,128]{1,0:T(8,128)(2,1)S(1)}, bf16[560,128]{1,0:T(8,128)(2,1)S(1)}, u32[]{:S(2)}, u32[]{:S(2)}) collective-permute-start(bf16[560,128]{1,0:T(8,128)(2,1)S(1)} %copy-done.4), channel_id=1, source_target_pairs={{0,15},{2,13},{4,11},{6,9},{8,7},{10,5},{12,3},{14,1},{16,31},{18,... | collective-permute-start | bytes 430088 | tf_op jit(solution)/shard_map/ppermute | solution.py:745
  24.1 8.0 %collective-permute-done.2.rest_2_ = bf16[560,128]{1,0:T(8,128)(2,1)S(1)} collective-permute-done((bf16[560,128]{1,0:T(8,128)(2,1)S(1)}, bf16[560,128]{1,0:T(8,128)(2,1)S(1)}, u32[]{:S(2)}, u32[]{:S(2)}) %collective-permute-start.2) | collective-permute-done | bytes 143392 | tf_op jit(solution)/shard_map/ppermute | solution.py:745
  32.1 1.3 %collective-permute-start.7 = (bf16[560,128]{1,0:T(8,128)(2,1)S(1)}, bf16[560,128]{1,0:T(8,128)(2,1)S(1)}, u32[]{:S(2)}, u32[]{:S(2)}) collective-permute-start(bf16[560,128]{1,0:T(8,128)(2,1)S(1)} %copy-done.3), channel_id=1, source_target_pairs={{0,7},{2,5},{4,3},{6,1},{8,15},{10,13},{12,11},{14,9},{16,23},{18,... | collective-permute-start | bytes 430088 | tf_op jit(solution)/shard_map/ppermute | solution.py:745
  33.5 0.1 copy.17
  33.6 0.2 reshape.35.taps_ref.first_taps_ref
  33.8 0.1 copy.16
  33.9 0.2 reshape.37.taps_ref.second_taps_ref
  34.1 14.0 %collective-permute-done.3.rest_3_ = bf16[560,128]{1,0:T(8,128)(2,1)S(1)} collective-permute-done((bf16[560,128]{1,0:T(8,128)(2,1)}, bf16[560,128]{1,0:T(8,128)(2,1)S(1)}, u32[]{:S(2)}, u32[]{:S(2)}) %collective-permute-start.3) | collective-permute-done | bytes 143392 | tf_op jit(solution)/shard_map/ppermute | solution.py:745
  48.1 2.4 %collective-permute-done.4.rest_4_ = bf16[560,128]{1,0:T(8,128)(2,1)S(1)} collective-permute-done((bf16[560,128]{1,0:T(8,128)(2,1)S(1)}, bf16[560,128]{1,0:T(8,128)(2,1)S(1)}, u32[]{:S(2)}, u32[]{:S(2)}) %collective-permute-start.4) | collective-permute-done | bytes 143392 | tf_op jit(solution)/shard_map/ppermute | solution.py:745
  50.5 0.0 collective-permute-done.5.rest_5_
  50.5 0.0 collective-permute-done.6.rest_6_
  50.5 0.0 collective-permute-done.7.rest_7_
  50.5 0.0 all-to-all-done
  50.5 0.1 broadcast_in_dim.12.gain_ref
  50.6 1.8 %gather_rows.1 = (f32[33,72,128]{2,1,0:T(8,128)S(1)}, bf16[3,80,128]{2,1,0:T(8,128)(2,1)S(1)}, bf16[3,80,128]{2,1,0:T(8,128)(2,1)S(1)}, bf16[80,128]{1,0:T(8,128)(2,1)S(1)}) custom-call(s32[1,2]{1,0:T(1,128)S(1)} %copy-done, f32[72,128]{1,0:T(8,128)S(1)} %broadcast_in_dim.12.gain_ref, bf16[4480,128]{1,0:T(8,128)(2,1)S(1)} %bitcast.24, ...), custom_call_target="tpu_custom_call" | custom-call | tf_op jit(solution)/shard_map/gather_rows/pallas_call | solution.py:300
  52.4 0.1 collective-permute-start.8
  52.5 0.5 collective-permute-start.9
  53.0 0.3 normalize_rows.1
  53.3 1.1 %channels_first.1 = bf16[2208,128]{1,0:T(8,128)(2,1)} custom-call(bf16[32,72,128]{2,1,0:T(8,128)(2,1)S(1)} %get-tuple-element.59.field.gridded), custom_call_target="tpu_custom_call" | custom-call | tf_op jit(solution)/shard_map/channels_first/pallas_call | solution.py:317
  54.4 1.2 %inner_convolution.1 = (bf16[32,80,128]{2,1,0:T(8,128)(2,1)S(1)}, f32[2,80,128]{2,1,0:T(8,128)S(1)}, f32[2,80,128]{2,1,0:T(8,128)S(1)}) custom-call(bf16[240,240]{1,0:T(8,128)(2,1)S(1)} %reshape.35.taps_ref.first_taps_ref, bf16[32,80,128]{2,1,0:T(8,128)(2,1)S(1)} %get-tuple-element.62.field), custom_call_target="tpu_custom_call" | custom-call | flops 471859200 | bytes 2097152 | tf_op jit(solution)/shard_map/inner_convolution/pallas_call | solution.py:382
  55.6 0.0 collective-permute-done.8.above
  55.6 0.6 collective-permute-done.9.below
  56.2 0.1 half_strip_packs.1
  56.3 2.7 %collective-permute-start.10 = (bf16[2,80,128]{2,1,0:T(8,128)(2,1)S(1)}, bf16[2,80,128]{2,1,0:T(8,128)(2,1)S(1)}, u32[]{:S(2)}, u32[]{:S(2)}) collective-permute-start(bf16[2,80,128]{2,1,0:T(8,128)(2,1)S(1)} %get-tuple-element.74), channel_id=1, source_target_pairs={{0,3},{1,4},{2,5},{3,6},{4,7},{5,8},{6,9},{7,10},{8,11},{9,12},{10... | collective-permute-start | bytes 122888 | tf_op jit(solution)/shard_map/ppermute | solution.py:728
  59.0 1.8 %collective-permute-start.11 = (bf16[2,80,128]{2,1,0:T(8,128)(2,1)S(1)}, bf16[2,80,128]{2,1,0:T(8,128)(2,1)S(1)}, u32[]{:S(2)}, u32[]{:S(2)}) collective-permute-start(bf16[2,80,128]{2,1,0:T(8,128)(2,1)S(1)} %get-tuple-element.75), channel_id=1, source_target_pairs={{0,13},{1,14},{2,15},{3,0},{4,1},{5,2},{6,3},{7,4},{8,5},{9,6},{10... | collective-permute-start | bytes 122888 | tf_op jit(solution)/shard_map/ppermute | solution.py:728
  60.8 0.8 %inner_second_convolution.1.base = f32[32,72,128]{2,1,0:T(8,128)S(1)} custom-call(bf16[240,240]{1,0:T(8,128)(2,1)S(1)} %reshape.37.taps_ref.second_taps_ref, bf16[32,80,128]{2,1,0:T(8,128)(2,1)S(1)} %get-tuple-element.71.hidden, bf16[32,72,128]{2,1,0:T(8,128)(2,1)S(1)} %get-tuple-element.59.field.gridded), custom_call_target="tpu_custom_call" | custom-call | flops 471859200 | bytes 2097152 | tf_op jit(solution)/shard_map/inner_second_convolution/pallas_call | solution.py:415
  61.5 0.9 %collective-permute-done.10.rest_0_ = bf16[2,80,128]{2,1,0:T(8,128)(2,1)S(1)} collective-permute-done((bf16[2,80,128]{2,1,0:T(8,128)(2,1)S(1)}, bf16[2,80,128]{2,1,0:T(8,128)(2,1)S(1)}, u32[]{:S(2)}, u32[]{:S(2)}) %collective-permute-start.10) | collective-permute-done | bytes 40992 | tf_op jit(solution)/shard_map/ppermute | solution.py:728
  62.5 0.6 collective-permute-done.11.rest_1_
  63.1 3.1 %convolutions.1 = bf16[69,32,128]{2,1,0:T(8,128)(2,1)} custom-call(bf16[240,240]{1,0:T(8,128)(2,1)S(1)} %reshape.35.taps_ref.first_taps_ref, bf16[240,240]{1,0:T(8,128)(2,1)S(1)} %reshape.37.taps_ref.second_taps_ref, bf16[32,80,128]{2,1,0:T(8,128)(2,1)S(1)} %get-tuple-element.62.field, f32[32,72,128]{2,1,0:T(8,128)S(1)} %inner_second_convolution.1.base, ...), custom_call_target="tpu_custom_call" | custom-call | tf_op jit(solution)/shard_map/convolutions/pallas_call | solution.py:705
  (16 shorter events, 0.1 us)
Async XLA Ops:
  5.6 6.6 %copy-start.9 = (bf16[560,128]{1,0:T(8,128)(2,1)S(1)}, bf16[560,128]{1,0:T(8,128)(2,1)}, u32[]{:S(2)}) copy-start(bf16[560,128]{1,0:T(8,128)(2,1)} %get-tuple-element.40) | copy-start | bytes 430084
  5.6 7.9 %copy-start.8 = (bf16[560,128]{1,0:T(8,128)(2,1)S(1)}, bf16[560,128]{1,0:T(8,128)(2,1)}, u32[]{:S(2)}) copy-start(bf16[560,128]{1,0:T(8,128)(2,1)} %get-tuple-element.41) | copy-start | bytes 430084
  5.6 9.2 %copy-start.7 = (bf16[560,128]{1,0:T(8,128)(2,1)S(1)}, bf16[560,128]{1,0:T(8,128)(2,1)}, u32[]{:S(2)}) copy-start(bf16[560,128]{1,0:T(8,128)(2,1)} %get-tuple-element.42) | copy-start | bytes 430084
  5.7 11.8 %copy-start.6 = (bf16[560,128]{1,0:T(8,128)(2,1)S(1)}, bf16[560,128]{1,0:T(8,128)(2,1)}, u32[]{:S(2)}) copy-start(bf16[560,128]{1,0:T(8,128)(2,1)} %get-tuple-element.44) | copy-start | bytes 430084
  5.7 13.2 %copy-start.5 = (bf16[560,128]{1,0:T(8,128)(2,1)S(1)}, bf16[560,128]{1,0:T(8,128)(2,1)}, u32[]{:S(2)}) copy-start(bf16[560,128]{1,0:T(8,128)(2,1)} %get-tuple-element.45) | copy-start | bytes 430084
  5.7 17.1 %copy-start.4 = (bf16[560,128]{1,0:T(8,128)(2,1)S(1)}, bf16[560,128]{1,0:T(8,128)(2,1)}, u32[]{:S(2)}) copy-start(bf16[560,128]{1,0:T(8,128)(2,1)} %get-tuple-element.46) | copy-start | bytes 430084
  5.7 26.4 %copy-start.3 = (bf16[560,128]{1,0:T(8,128)(2,1)S(1)}, bf16[560,128]{1,0:T(8,128)(2,1)}, u32[]{:S(2)}) copy-start(bf16[560,128]{1,0:T(8,128)(2,1)} %get-tuple-element.47) | copy-start | bytes 430084
  5.7 27.7 %copy-start.1 = (bf16[9,69,69]{2,1,0:T(8,128)(2,1)S(1)}, bf16[9,69,69]{2,1,0:T(8,128)(2,1)}, u32[]{:S(2)}) copy-start(bf16[9,69,69]{2,1,0:T(8,128)(2,1)} %param.14) | copy-start | bytes 257098
  5.7 28.0 %copy-start.2 = (bf16[9,69,69]{2,1,0:T(8,128)(2,1)S(1)}, bf16[9,69,69]{2,1,0:T(8,128)(2,1)}, u32[]{:S(2)}) copy-start(bf16[9,69,69]{2,1,0:T(8,128)(2,1)} %param.15) | copy-start | bytes 257098
  5.7 44.8 %all-to-all-start = ((bf16[8,560,128]{2,1,0:T(8,128)(2,1)}), bf16[8,560,128]{2,1,0:T(8,128)(2,1)S(1)}, u32[]{:S(2)}, u32[]{:S(2)}) async-start(bf16[8,560,128]{2,1,0:T(8,128)(2,1)} %bitcast.25), calls=%async_computation | async-start | bytes 2293760 | tf_op jit(solution)/shard_map/all_to_all | solution.py:747
  12.3 21.8 %copy-start.10 = (f32[69]{0:T(128)S(1)}, f32[69]{0:T(128)}, u32[]{:S(2)}) copy-start(f32[69]{0:T(128)} %param.13) | copy-start | bytes 832
  12.3 6.5 %collective-permute-start = (bf16[560,128]{1,0:T(8,128)(2,1)S(1)}, bf16[560,128]{1,0:T(8,128)(2,1)S(1)}, u32[]{:S(2)}, u32[]{:S(2)}) collective-permute-start(bf16[560,128]{1,0:T(8,128)(2,1)S(1)} %copy-done.9), channel_id=1, source_target_pairs={{0,1},{2,3},{4,5},{6,7},{8,9},{10,11},{12,13},{14,15},{16,17},{18,... | collective-permute-start | bytes 430088 | tf_op jit(solution)/shard_map/ppermute | solution.py:745
  13.6 37.0 %copy-start = (s32[1,2]{1,0:T(1,128)S(1)}, s32[1,2]{1,0:T(1,128)}, u32[]{:S(2)}) copy-start(s32[1,2]{1,0:T(1,128)} %flip_ref.1) | copy-start | bytes 28
  13.6 9.2 %collective-permute-start.1 = (bf16[560,128]{1,0:T(8,128)(2,1)S(1)}, bf16[560,128]{1,0:T(8,128)(2,1)S(1)}, u32[]{:S(2)}, u32[]{:S(2)}) collective-permute-start(bf16[560,128]{1,0:T(8,128)(2,1)S(1)} %copy-done.8), channel_id=1, source_target_pairs={{0,3},{2,1},{4,7},{6,5},{8,11},{10,9},{12,15},{14,13},{16,19},{18,... | collective-permute-start | bytes 430088 | tf_op jit(solution)/shard_map/ppermute | solution.py:745
  14.9 17.2 %collective-permute-start.2 = (bf16[560,128]{1,0:T(8,128)(2,1)S(1)}, bf16[560,128]{1,0:T(8,128)(2,1)S(1)}, u32[]{:S(2)}, u32[]{:S(2)}) collective-permute-start(bf16[560,128]{1,0:T(8,128)(2,1)S(1)} %copy-done.7), channel_id=1, source_target_pairs={{0,5},{2,7},{4,1},{6,3},{8,13},{10,15},{12,9},{14,11},{16,21},{18,... | collective-permute-start | bytes 430088 | tf_op jit(solution)/shard_map/ppermute | solution.py:745
  16.2 31.9 %collective-permute-start.3 = (bf16[560,128]{1,0:T(8,128)(2,1)}, bf16[560,128]{1,0:T(8,128)(2,1)S(1)}, u32[]{:S(2)}, u32[]{:S(2)}) collective-permute-start(bf16[560,128]{1,0:T(8,128)(2,1)} %get-tuple-element.43), channel_id=1, source_target_pairs={{0,9},{2,11},{4,13},{6,15},{8,1},{10,3},{12,5},{14,7},{16,25},{18,... | collective-permute-start | bytes 430088 | tf_op jit(solution)/shard_map/ppermute | solution.py:745
  17.5 33.0 %collective-permute-start.4 = (bf16[560,128]{1,0:T(8,128)(2,1)S(1)}, bf16[560,128]{1,0:T(8,128)(2,1)S(1)}, u32[]{:S(2)}, u32[]{:S(2)}) collective-permute-start(bf16[560,128]{1,0:T(8,128)(2,1)S(1)} %copy-done.6), channel_id=1, source_target_pairs={{0,11},{2,9},{4,15},{6,13},{8,3},{10,1},{12,7},{14,5},{16,27},{18,... | collective-permute-start | bytes 430088 | tf_op jit(solution)/shard_map/ppermute | solution.py:745
  18.8 31.7 %collective-permute-start.5 = (bf16[560,128]{1,0:T(8,128)(2,1)S(1)}, bf16[560,128]{1,0:T(8,128)(2,1)S(1)}, u32[]{:S(2)}, u32[]{:S(2)}) collective-permute-start(bf16[560,128]{1,0:T(8,128)(2,1)S(1)} %copy-done.5), channel_id=1, source_target_pairs={{0,13},{2,15},{4,9},{6,11},{8,5},{10,7},{12,1},{14,3},{16,29},{18,... | collective-permute-start | bytes 430088 | tf_op jit(solution)/shard_map/ppermute | solution.py:745
  22.8 27.7 %collective-permute-start.6 = (bf16[560,128]{1,0:T(8,128)(2,1)S(1)}, bf16[560,128]{1,0:T(8,128)(2,1)S(1)}, u32[]{:S(2)}, u32[]{:S(2)}) collective-permute-start(bf16[560,128]{1,0:T(8,128)(2,1)S(1)} %copy-done.4), channel_id=1, source_target_pairs={{0,15},{2,13},{4,11},{6,9},{8,7},{10,5},{12,3},{14,1},{16,31},{18,... | collective-permute-start | bytes 430088 | tf_op jit(solution)/shard_map/ppermute | solution.py:745
  32.1 18.4 %collective-permute-start.7 = (bf16[560,128]{1,0:T(8,128)(2,1)S(1)}, bf16[560,128]{1,0:T(8,128)(2,1)S(1)}, u32[]{:S(2)}, u32[]{:S(2)}) collective-permute-start(bf16[560,128]{1,0:T(8,128)(2,1)S(1)} %copy-done.3), channel_id=1, source_target_pairs={{0,7},{2,5},{4,3},{6,1},{8,15},{10,13},{12,11},{14,9},{16,23},{18,... | collective-permute-start | bytes 430088 | tf_op jit(solution)/shard_map/ppermute | solution.py:745
  52.4 3.2 %collective-permute-start.8 = (bf16[3,80,128]{2,1,0:T(8,128)(2,1)S(1)}, bf16[3,80,128]{2,1,0:T(8,128)(2,1)S(1)}, u32[]{:S(2)}, u32[]{:S(2)}) collective-permute-start(bf16[3,80,128]{2,1,0:T(8,128)(2,1)S(1)} %get-tuple-element.63), channel_id=1, source_target_pairs={{0,1},{1,2},{2,3},{3,4},{4,5},{5,6},{6,7},{7,8},{8,9},{9,10},{10,1... | collective-permute-start | bytes 184328 | tf_op jit(solution)/shard_map/ppermute | solution.py:728
  52.5 3.7 %collective-permute-start.9 = (bf16[3,80,128]{2,1,0:T(8,128)(2,1)S(1)}, bf16[3,80,128]{2,1,0:T(8,128)(2,1)S(1)}, u32[]{:S(2)}, u32[]{:S(2)}) collective-permute-start(bf16[3,80,128]{2,1,0:T(8,128)(2,1)S(1)} %get-tuple-element.64), channel_id=1, source_target_pairs={{0,15},{1,0},{2,1},{3,2},{4,3},{5,4},{6,5},{7,6},{8,7},{9,8},{10,9... | collective-permute-start | bytes 184328 | tf_op jit(solution)/shard_map/ppermute | solution.py:728
  56.3 6.2 %collective-permute-start.10 = (bf16[2,80,128]{2,1,0:T(8,128)(2,1)S(1)}, bf16[2,80,128]{2,1,0:T(8,128)(2,1)S(1)}, u32[]{:S(2)}, u32[]{:S(2)}) collective-permute-start(bf16[2,80,128]{2,1,0:T(8,128)(2,1)S(1)} %get-tuple-element.74), channel_id=1, source_target_pairs={{0,3},{1,4},{2,5},{3,6},{4,7},{5,8},{6,9},{7,10},{8,11},{9,12},{10... | collective-permute-start | bytes 122888 | tf_op jit(solution)/shard_map/ppermute | solution.py:728
  59.0 4.1 %collective-permute-start.11 = (bf16[2,80,128]{2,1,0:T(8,128)(2,1)S(1)}, bf16[2,80,128]{2,1,0:T(8,128)(2,1)S(1)}, u32[]{:S(2)}, u32[]{:S(2)}) collective-permute-start(bf16[2,80,128]{2,1,0:T(8,128)(2,1)S(1)} %get-tuple-element.75), channel_id=1, source_target_pairs={{0,13},{1,14},{2,15},{3,0},{4,1},{5,2},{6,3},{7,4},{8,5},{9,6},{10... | collective-permute-start | bytes 122888 | tf_op jit(solution)/shard_map/ppermute | solution.py:728
